TPU v7x, 512 devices: a whole 4x4x16 slice. The times are simulated.
512 devices in a mesh: pole: 4 (over x), prow: 8 (over y, core), pcol: 16 (over z).
Axes of the slice: x: 4, y: 4, z: 16, core: 2. Of those that a mesh axis runs over, the one named last changes fastest.
Arguments:
- anc_inverse: bfloat16 [32768, 8192], P(('pole', 'prow'), 'pcol'), parts along dimension 0, may hold values from -6 to 6
- factor_blocks: bfloat16 [64, 8, 256, 1024], P(('pole', 'pcol'), 'prow'), parts along dimension 0, may hold values from -0.125 to 0.125
- diag_in: float32 [64, 1024, 1024], P(('pole', 'pcol'), 'prow'), parts along dimension 0, may hold values from -6 to 6
- ancestors: int32 [16, 8], replicated, may hold values from 0 to 31, as said below
- active_count: int32 [16], replicated, may hold values from 6 to 8
Outputs:
- inverse_blocks: bfloat16 [64, 8, 256, 1024], P(('pole', 'pcol'), 'prow'), parts along dimension 0
- diagonal_inverse: float32 [64, 1024, 1024], P(('pole', 'pcol'), 'prow'), parts along dimension 0
There are 4 independent parts, one for each index of `pole`. A program takes and returns all parts, laid end to end along the dimension named above; an argument that names none is the same for every part. Nothing has to cross between parts.
Inputs may be any that keep to these rules, and one draw needn't show every extreme that they name: ancestors[K, s] % 8 == s for every slot s, so the slots of one list name distinct ancestors with distinct values modulo 16.
All inputs are finite; a program needn't handle non-finite values.
Results may differ from a plain program's by a relative error of at most 0.013.
Values may be sent and summed in bfloat16 or wider, within the bound.
No kernel may reach another device: no remote copies, remote signals or barrier semaphores. Data moves between devices by JAX's collectives and lax.ppermute only.
A program may use at most 64 MiB of HBM per device.

v0:
```python
import jax
import jax.numpy as jnp
from jax import lax
from jax.sharding import PartitionSpec as P


def outgoing(
    local_blocks, ancestors, active_count, count, sn_col, me_row, me_col, row_count, col_count
):
    targets = (
        jnp.arange(col_count, dtype=jnp.int32)[:, None] * sn_col
        + jnp.arange(count, dtype=jnp.int32)[None, :]
    )
    names = ancestors[targets]
    limits = active_count[targets]
    slots = jnp.arange(names.shape[-1], dtype=jnp.int32)
    matched = (names % col_count == me_col) & (slots < limits[..., None])
    col_name = jnp.sum(jnp.where(matched, names, 0), axis=-1)
    row_name = jnp.take_along_axis(
        names, jnp.full(names.shape[:2] + (1,), me_row, jnp.int32), axis=-1
    )[..., 0]
    found = jnp.any(matched, axis=-1) & (me_row < limits)
    picked = local_blocks[row_name // row_count, :, col_name // col_count, :]
    return picked * found[..., None, None].astype(jnp.bfloat16)


def local(anc_inverse, factor_blocks, diag_in, ancestors, active_count):
    row_count = lax.axis_size("prow")
    col_count = lax.axis_size("pcol")
    me_row = lax.axis_index("prow")
    me_col = lax.axis_index("pcol")
    sn_col = factor_blocks.shape[0]
    anc_w = factor_blocks.shape[2]
    local_blocks = anc_inverse.reshape(
        anc_inverse.shape[0] // anc_w, anc_w, anc_inverse.shape[1] // anc_w, anc_w
    )
    gathered = lax.all_gather(factor_blocks, "prow", axis=1, tiled=True)
    node_ids = me_col * sn_col + jnp.arange(sn_col, dtype=jnp.int32)
    my_names = ancestors[node_ids]
    sources = my_names % col_count
    sending = outgoing(
        local_blocks, ancestors, active_count, sn_col, sn_col, me_row, me_col, row_count, col_count
    )
    arrived = lax.all_to_all(sending, "pcol", split_axis=0, concat_axis=0, tiled=True)
    selected = arrived[sources, jnp.arange(sn_col, dtype=jnp.int32)[:, None]]
    product = -jnp.einsum("ktij,ktjw->kiw", selected, gathered, preferred_element_type=jnp.float32)
    row_live = (me_row < active_count[node_ids]).astype(jnp.float32)
    inverse_rows = (product * row_live[:, None, None]).astype(jnp.bfloat16)
    inverse_blocks = inverse_rows[:, None]
    terms = jnp.einsum(
        "kaw,kav->kwv", factor_blocks[:, 0], inverse_rows, preferred_element_type=jnp.float32
    )
    summed = lax.psum_scatter(
        terms.astype(jnp.bfloat16), "prow", scatter_dimension=1, tiled=True
    ).astype(jnp.float32)
    diagonal_inverse = diag_in - summed
    return (inverse_blocks, diagonal_inverse)


def solution(mesh):
    placed = (
        P(("pole", "prow"), "pcol"),
        P(("pole", "pcol"), "prow", None, None),
        P(("pole", "pcol"), "prow", None),
        P(),
        P(),
    )
    return jax.shard_map(
        local,
        mesh=mesh,
        in_specs=placed,
        out_specs=(P(("pole", "pcol"), "prow", None, None), P(("pole", "pcol"), "prow", None)),
        check_vma=False,
    )
```

profile of v0, /device:TPU:1, one launch (start us, length us, event | category | flops | bytes accessed | tf_op | source)
XLA Modules:
  0.0 189.6 jit_solution(2643570437025638412)
XLA Ops:
  7.2 0.8 copy.22
  8.0 0.6 gather_fusion
  8.5 0.1 copy.23
  8.6 1.3 gather_fusion.1
  10.0 0.7 gather_fusion.4
  10.7 1.3 reshape.459
  12.1 0.1 copy.24
  12.2 0.7 gather_fusion.2
  12.9 1.5 fusion.2
  14.5 15.9 %all-to-all-start = ((bf16[16,1,256,256]{3,2,1,0:T(8,128)(2,1)}), bf16[16,1,256,256]{3,2,1,0:T(8,128)(2,1)S(1)}, u32[]{:S(2)}, u32[]{:S(2)}) async-start(bf16[16,1,256,256]{3,2,1,0:T(8,128)(2,1)} %fusion.2), calls=%async_computation | async-start | bytes 4194304 | tf_op jit(solution)/shard_map/all_to_all | solution.py:44
  30.3 0.0 all-gather.2.cloned.1.call-start
  30.4 0.7 all-gather.2.cloned.1.call-update
  31.1 0.0 reduce-scatter.4.cloned.1.call-start
  31.1 0.2 dynamic-slice_reduce_fusion
  31.3 0.6 dynamic-slice.6
  32.6 89.6 %all-to-all-done = bf16[16,1,256,256]{3,2,1,0:T(8,128)(2,1)S(1)} async-done(((bf16[16,1,256,256]{3,2,1,0:T(8,128)(2,1)}), bf16[16,1,256,256]{3,2,1,0:T(8,128)(2,1)S(1)}, u32[]{:S(2)}, u32[]{:S(2)}) %all-to-all-start) | async-done | bytes 2097184 | tf_op jit(solution)/shard_map/all_to_all | solution.py:44
  122.2 0.6 gather_fusion.3
  122.8 0.0 all-gather.2.cloned.1.call-done
  122.8 0.0 copy-start.1
  122.8 3.5 %fusion.12 = bf16[256,1024]{1,0:T(8,128)(2,1)S(1)} fusion(bf16[8,256,256]{2,1,0:T(8,128)(2,1)S(1)} %gather_fusion.3, bf16[1,8,256,1024]{3,2,0,1:T(8,128)(2,1)} %all-gather.2.cloned.1.call-done, f32[]{:T(128)} %bitcast.17), kind=kOutput, calls=%fused_computation.14 | convolution fusion | flops 1074528256 | bytes 5767172 | tf_op jit(solution)/shard_map/ktij,ktjw->kiw/dot_general | solution.py:46
  126.3 0.0 copy-start.3
  126.4 0.8 copy-done.3
  127.1 0.7 convert_bitcast_fusion
  127.9 7.7 %copy.29 = bf16[1,1024,1024]{2,0,1:T(2,128)(2,1)} copy(bf16[1,1024,1024]{1,2,0:T(8,128)(2,1)S(1)} %convert_bitcast_fusion) | data formatting | bytes 4194304
  135.6 4.3 %copy.33 = bf16[1024,1,1024]{2,0,1:T(8,128)(2,1)} copy(bf16[1024,1,1024]{2,1,0:T(2,128)(2,1)} %bitcast.86) | data formatting | bytes 4194304
  139.9 0.0 reduce-scatter.4.cloned.1.call-update
  140.0 1.0 copy-done.2
  141.0 0.2 copy.27
  141.2 38.9 %reduce-scatter.4.cloned.1.call-done = bf16[128,1024]{1,0:T(8,128)(2,1)} async-done(((bf16[1024,1024]{1,0:T(8,128)(2,1)}), bf16[128,1024]{1,0:T(8,128)(2,1)}) %reduce-scatter.4.cloned.1.call-update) | async-done | bytes 262160
  180.0 1.2 reshape_bitcast_fusion
  181.3 0.4 copy.30
  181.8 1.0 copy.28
  (21 shorter events, 0.2 us)
Async XLA Ops:
  14.5 16.7 %copy-start.4 = (s32[16,8]{0,1:T(8,128)S(1)}, s32[16,8]{0,1:T(8,128)}, u32[]{:S(2)}) copy-start(s32[16,8]{0,1:T(8,128)} %param.8) | copy-start | bytes 1540
  14.5 16.9 %copy-start = (s32[16]{0:T(128)S(1)}, s32[16]{0:T(128)}, u32[]{:S(2)}) copy-start(s32[16]{0:T(128)} %param.9) | copy-start | bytes 196
  14.5 107.7 %all-to-all-start = ((bf16[16,1,256,256]{3,2,1,0:T(8,128)(2,1)}), bf16[16,1,256,256]{3,2,1,0:T(8,128)(2,1)S(1)}, u32[]{:S(2)}, u32[]{:S(2)}) async-start(bf16[16,1,256,256]{3,2,1,0:T(8,128)(2,1)} %fusion.2), calls=%async_computation | async-start | bytes 4194304 | tf_op jit(solution)/shard_map/all_to_all | solution.py:44
  30.3 92.5 %all-gather.2.cloned.1.call-start = ((), (), s32[]{:S(2)}) async-start(), calls=%async_computation.2 | async-start | bytes 4718592 | tf_op jit(solution)/shard_map/all_gather | solution.py:37
  31.1 149.0 %reduce-scatter.4.cloned.1.call-start = ((), (), s32[]{:S(2)}) async-start(), calls=%async_computation.3 | async-start | bytes 2359296
  122.8 4.3 %copy-start.1 = (bf16[1,1,256,1024]{3,2,1,0:T(8,128)(2,1)S(1)}, bf16[1,1,256,1024]{3,2,1,0:T(8,128)(2,1)}, u32[]{:S(2)}) copy-start(bf16[1,1,256,1024]{3,2,1,0:T(8,128)(2,1)} %param.6) | copy-start | bytes 1572868
  126.3 0.8 copy-start.3
  139.9 1.0 copy-start.2
Sparse Core Ops, SparseCore 0:
  33.3 41.7 all-gather.1
  140.1 39.9 reduce-scatter.3
where the time goes:
time: 191 us; the launch traced here: 190 us
  waiting for transfers between devices  129 us (68%)
  local copies, waits for them, and re-layouts  23.7 us (12%)
  starting transfers between devices  16 us (8%)
  between operations  14.9 us (8%)
  matrix products  4.24 us (2%)
    all_to_all x1, waiting for transfers between devices, local(): lax.all_to_all(sending, 'pcol', split_axis=0, concat_axis=0, tiled=True)  89.6 us
    unnamed x3, waiting for transfers between devices  39.6 us
    unnamed x18, local copies, waits for them, and re-layouts  17.5 us
    all_to_all x1, starting transfers between devices, local(): lax.all_to_all(sending, 'pcol', split_axis=0, concat_axis=0, tiled=True)  15.9 us
  transfers between devices with their start and end apart: 3, of which 2 were waited for; matrix products, arithmetic and copies ran while one was open for 1% of the time, Pallas kernels for 0%

commit v1 on v0

v1 whole, which is shorter than its diff:
```python
import functools

import jax
import jax.numpy as jnp
from jax import lax
from jax.experimental import pallas as pl
from jax.experimental.pallas import tpu as pltpu
from jax.sharding import PartitionSpec as P

W = 256
SLICE = 128
MIB = 1024 * 1024


def pick_kernel(rows, cols, anc_ref, a_ref, out_ref, sems):
    me_row = lax.axis_index("prow")
    me_col = lax.axis_index("pcol")
    slot = lax.rem(me_col, rows)
    copies = []
    for k in range(cols):
        i = anc_ref[k, me_row] // rows
        j = anc_ref[k, slot] // cols
        copy = pltpu.make_async_copy(
            a_ref.at[pl.ds(pl.multiple_of(i * W, W), W), pl.ds(pl.multiple_of(j * W, W), W)],
            out_ref.at[k],
            sems.at[k],
        )
        copy.start()
        copies.append(copy)
    for copy in copies:
        copy.wait()


def product_kernel(rows, cols, anc_ref, count_ref, a_ref, *refs):
    f_refs = refs[:rows]
    out_ref, held = refs[rows:]
    me_row = lax.axis_index("prow")
    me_col = lax.axis_index("pcol")
    count = count_ref[me_col]
    row_live = (me_row < count).astype(jnp.float32)
    for n in range(rows):
        t = slot_row(me_row, n, rows)
        live = (t < count).astype(jnp.bfloat16)
        held[n] = a_ref[lax.rem(anc_ref[me_col, t], cols)] * live
    width = out_ref.shape[-1]
    step = 256
    for at in range(0, width, step):
        total = jnp.zeros((W, step), jnp.float32)
        for n in range(rows):
            total += jnp.dot(held[n], f_refs[n][:, at : at + step], preferred_element_type=jnp.float32)
        out_ref[:, at : at + step] = (total * -row_live).astype(jnp.bfloat16)


def slot_row(me_row, n, rows):
    half = rows // 2
    base = me_row if n < half else me_row + 1 - 2 * lax.rem(me_row, 2)
    return lax.rem(base - 2 * (n % half) + rows, rows)


def turn_kernel(rows, own_ref, other_ref, out_ref):
    core = lax.rem(lax.axis_index("prow"), 2)
    for y in range(rows // 2):
        at = pl.ds(pl.multiple_of((2 * y + core) * SLICE, SLICE), SLICE)
        out_ref[pl.ds(y * SLICE, SLICE), 0:W] = own_ref[:, at].T
        out_ref[pl.ds(y * SLICE, SLICE), W : 2 * W] = other_ref[:, at].T


def term_kernel(turned_ref, own_ref, other_ref, out_ref):
    for y in range(out_ref.shape[0]):
        at = pl.ds(y * SLICE, SLICE)
        total = jnp.dot(turned_ref[at, 0:W], own_ref[...], preferred_element_type=jnp.float32)
        total += jnp.dot(turned_ref[at, W : 2 * W], other_ref[...], preferred_element_type=jnp.float32)
        out_ref[y] = total.astype(jnp.bfloat16)


def sum_kernel(diag_ref, terms_ref, out_ref):
    total = terms_ref[0].astype(jnp.float32)
    for y in range(1, terms_ref.shape[0]):
        total += terms_ref[y].astype(jnp.float32)
    out_ref[...] = diag_ref[...] - total


SMEM = pl.BlockSpec(memory_space=pltpu.SMEM)
VMEM = pl.BlockSpec(memory_space=pltpu.VMEM)
ANY = pl.BlockSpec(memory_space=pl.ANY)


def local(anc_inverse, factor_blocks, diag_in, ancestors, active_count):
    rows = lax.axis_size("prow")
    cols = lax.axis_size("pcol")
    chips = rows // 2
    width = factor_blocks.shape[-1]
    factor = factor_blocks[0, 0]

    def shift(x, h):
        return lax.ppermute(x, "prow", [(i, (i + 2 * h) % rows) for i in range(rows)])

    def swap(x):
        return lax.ppermute(x, "prow", [(i, i ^ 1) for i in range(rows)])

    sending = pl.pallas_call(
        functools.partial(pick_kernel, rows, cols),
        out_shape=jax.ShapeDtypeStruct((cols, W, W), jnp.bfloat16),
        in_specs=[SMEM, ANY],
        out_specs=ANY,
        scratch_shapes=[pltpu.SemaphoreType.DMA((cols,))],
        cost_estimate=pl.CostEstimate(flops=0, bytes_accessed=4 * MIB, transcendentals=0),
    )(ancestors, anc_inverse)
    arrived = lax.all_to_all(sending, "pcol", split_axis=0, concat_axis=0, tiled=True)

    same = [factor] + [shift(factor, h if h <= chips // 2 else h - chips) for h in range(1, chips)]
    factors = same + [swap(f) for f in same]
    turned = pl.pallas_call(
        functools.partial(turn_kernel, rows),
        out_shape=jax.ShapeDtypeStruct((chips * SLICE, 2 * W), jnp.bfloat16),
        in_specs=[VMEM, VMEM],
        out_specs=VMEM,
        compiler_params=pltpu.CompilerParams(vmem_limit_bytes=16 * MIB),
        cost_estimate=pl.CostEstimate(flops=0, bytes_accessed=2 * MIB, transcendentals=0),
    )(factors[0], factors[chips])

    product = pl.pallas_call(
        functools.partial(product_kernel, rows, cols),
        out_shape=jax.ShapeDtypeStruct((W, width), jnp.bfloat16),
        in_specs=[SMEM, SMEM] + [VMEM] * (1 + rows),
        out_specs=VMEM,
        scratch_shapes=[pltpu.VMEM((rows, W, W), jnp.bfloat16)],
        compiler_params=pltpu.CompilerParams(vmem_limit_bytes=32 * MIB),
        cost_estimate=pl.CostEstimate(flops=2 * rows * W * W * width, bytes_accessed=7 * MIB, transcendentals=0),
    )(ancestors, active_count, arrived, *factors)
    terms = pl.pallas_call(
        term_kernel,
        out_shape=jax.ShapeDtypeStruct((chips, SLICE, width), jnp.bfloat16),
        in_specs=[VMEM] * 3,
        out_specs=VMEM,
        compiler_params=pltpu.CompilerParams(vmem_limit_bytes=16 * MIB),
        cost_estimate=pl.CostEstimate(flops=4 * chips * SLICE * W * width, bytes_accessed=3 * MIB, transcendentals=0),
    )(turned, product, swap(product))
    groups = [list(range(core, rows, 2)) for core in range(2)]
    met = lax.all_to_all(terms, "prow", split_axis=0, concat_axis=0, tiled=True, axis_index_groups=groups)
    diagonal = pl.pallas_call(
        sum_kernel,
        out_shape=jax.ShapeDtypeStruct((SLICE, width), jnp.float32),
        in_specs=[VMEM, VMEM],
        out_specs=VMEM,
        compiler_params=pltpu.CompilerParams(vmem_limit_bytes=16 * MIB),
        cost_estimate=pl.CostEstimate(flops=0, bytes_accessed=2 * MIB, transcendentals=0),
    )(diag_in[0], met)
    return (product[None, None], diagonal[None])


def solution(mesh):
    placed = (
        P(("pole", "prow"), "pcol"),
        P(("pole", "pcol"), "prow", None, None),
        P(("pole", "pcol"), "prow", None),
        P(),
        P(),
    )
    return jax.shard_map(
        local,
        mesh=mesh,
        in_specs=placed,
        out_specs=(P(("pole", "pcol"), "prow", None, None), P(("pole", "pcol"), "prow", None)),
        check_vma=False,
    )
```

time: 191 us -> 215 us (1.13)
  Pallas kernels: 0 us -> 70.2 us
  waiting for transfers between devices: 129 us -> 64.4 us
  starting transfers between devices: 16 us -> 46.6 us
  blocking collectives: 0 us -> 18.2 us
  between operations: 14.9 us -> 0.8 us
  local copies, waits for them, and re-layouts: 23.7 us -> 13.4 us
  matrix products: 4.24 us -> 0 us
    pallas_call x0 -> x5, Pallas kernels: none -> 70.2 us  [the longest x1 65.6 us: local(): pl.pallas_call(functools.partial(pick_kernel, rows, cols), out_shape=jax....]
    unnamed x3 -> x0, waiting for transfers between devices: 39.6 us -> none
    all_to_all x1, waiting for transfers between devices: 89.6 us -> 54.1 us  [local(): lax.all_to_all(sending, 'pcol', split_axis=0, concat_axis=0, tiled=True)]
    ppermute x0 -> x8, starting transfers between devices: none -> 30.7 us  [the longest x5 20 us: swap(): return lax.ppermute(x, 'prow', [(i, i ^ 1) for i in range(rows)])]
    all_to_all x0 -> x1, blocking collectives: none -> 18.2 us  [local(): lax.all_to_all(terms, 'prow', split_axis=0, concat_axis=0, tiled=True, ax...]
    ppermute x0 -> x8, waiting for transfers between devices: none -> 10.4 us  [the longest x3 8.83 us: shift(): lax.ppermute(x, 'prow', [(i, (i + 2 * h) % rows) for i in range(rows)])]
    gather x9 -> x0, local copies, waits for them, and re-layouts: 4.71 us -> none  [the longest x1 1.31 us: outgoing(): limits = active_count[targets]]
    dot_general x2 -> x0, matrix products: 4.24 us -> none  [the longest x1 3.5 us: local(): jnp.einsum('ktij,ktjw->kiw', selected, gathered, preferred_element_type=j...]
  transfers between devices with their start and end apart: 3 -> 9, of which waited for: 2 -> 4; matrix products, arithmetic and copies ran while one was open for 1% -> 0% of each run, Pallas kernels for 0% -> 0%
where the time goes in v1:
time: 215 us; the launch traced here: 214 us
  Pallas kernels  70.2 us (33%)
  waiting for transfers between devices  64.4 us (30%)
  starting transfers between devices  46.6 us (22%)
  blocking collectives  18.2 us (8%)
  local copies, waits for them, and re-layouts  13.4 us (6%)
    pallas_call x1, Pallas kernels, local(): pl.pallas_call(functools.partial(pick_kernel, rows, cols), out_shape=jax....  65.6 us
    all_to_all x1, waiting for transfers between devices, local(): lax.all_to_all(sending, 'pcol', split_axis=0, concat_axis=0, tiled=True)  54.1 us
    ppermute x5, starting transfers between devices, swap(): return lax.ppermute(x, 'prow', [(i, i ^ 1) for i in range(rows)])  20 us
    all_to_all x1, blocking collectives, local(): lax.all_to_all(terms, 'prow', split_axis=0, concat_axis=0, tiled=True, ax...  18.2 us
    all_to_all x1, starting transfers between devices, local(): lax.all_to_all(sending, 'pcol', split_axis=0, concat_axis=0, tiled=True)  15.9 us
    unnamed x35, local copies, waits for them, and re-layouts  13.4 us
    ppermute x3, starting transfers between devices, shift(): lax.ppermute(x, 'prow', [(i, (i + 2 * h) % rows) for i in range(rows)])  10.7 us
    ppermute x3, waiting for transfers between devices, shift(): lax.ppermute(x, 'prow', [(i, (i + 2 * h) % rows) for i in range(rows)])  8.83 us
  transfers between devices with their start and end apart: 9, of which 4 were waited for; matrix products, arithmetic and copies ran while one was open for 0% of the time, Pallas kernels for 0%

profile of v1, /device:TPU:1, one launch (start us, length us, event | category | flops | bytes accessed | tf_op | source)
XLA Modules:
  0.0 213.6 jit_solution(10777364987634565651)
XLA Ops:
  0.6 1.4 copy.8.anc_ref
  2.0 65.6 %shard_map.68 = bf16[16,256,256]{2,1,0:T(8,128)(2,1)} custom-call(s32[16,8]{1,0:T(8,128)} %copy.8.anc_ref, bf16[1024,512]{1,0:T(8,128)(2,1)} %a_ref.1), custom_call_target="tpu_custom_call" | custom-call | bytes 4194304 | tf_op jit(solution)/shard_map/pallas_call | solution.py:101
  67.6 15.9 %all-to-all-start = ((bf16[16,256,256]{2,1,0:T(8,128)(2,1)}), bf16[16,256,256]{2,1,0:T(8,128)(2,1)S(1)}, u32[]{:S(2)}, u32[]{:S(2)}) async-start(bf16[16,256,256]{2,1,0:T(8,128)(2,1)} %shard_map.68), calls=%async_computation | async-start | bytes 4194304 | tf_op jit(solution)/shard_map/all_to_all | solution.py:109
  83.5 3.2 %collective-permute-start = (bf16[256,1024]{1,0:T(8,128)(2,1)S(1)}, bf16[256,1024]{1,0:T(8,128)(2,1)S(1)}, u32[]{:S(2)}, u32[]{:S(2)}) collective-permute-start(bf16[256,1024]{1,0:T(8,128)(2,1)S(1)} %bitcast.4), channel_id=1, source_target_pairs={{0,32},{16,48},{32,64},{48,80},{64,96},{80,112},{96,0},{112,16},{1... | collective-permute-start | bytes 1572872 | tf_op jit(solution)/shard_map/ppermute | solution.py:96
  86.7 4.5 %collective-permute-start.1 = (bf16[256,1024]{1,0:T(8,128)(2,1)S(1)}, bf16[256,1024]{1,0:T(8,128)(2,1)S(1)}, u32[]{:S(2)}, u32[]{:S(2)}) collective-permute-start(bf16[256,1024]{1,0:T(8,128)(2,1)S(1)} %bitcast.5), channel_id=1, source_target_pairs={{0,64},{16,80},{32,96},{48,112},{64,0},{80,16},{96,32},{112,48},{1... | collective-permute-start | bytes 1572872 | tf_op jit(solution)/shard_map/ppermute | solution.py:96
  91.3 3.0 %collective-permute-start.2 = (bf16[256,1024]{1,0:T(8,128)(2,1)S(1)}, bf16[256,1024]{1,0:T(8,128)(2,1)S(1)}, u32[]{:S(2)}, u32[]{:S(2)}) collective-permute-start(bf16[256,1024]{1,0:T(8,128)(2,1)S(1)} %bitcast.6), channel_id=1, source_target_pairs={{0,96},{16,112},{32,0},{48,16},{64,32},{80,48},{96,64},{112,80},{1... | collective-permute-start | bytes 1572872 | tf_op jit(solution)/shard_map/ppermute | solution.py:96
  94.3 3.7 %collective-permute-start.3 = (bf16[256,1024]{1,0:T(8,128)(2,1)S(1)}, bf16[256,1024]{1,0:T(8,128)(2,1)S(1)}, u32[]{:S(2)}, u32[]{:S(2)}) collective-permute-start(bf16[256,1024]{1,0:T(8,128)(2,1)S(1)} %bitcast.7), channel_id=1, source_target_pairs={{0,16},{16,0},{32,48},{48,32},{64,80},{80,64},{96,112},{112,96},{1... | collective-permute-start | bytes 1572872 | tf_op jit(solution)/shard_map/ppermute | solution.py:99
  98.0 1.3 collective-permute-done.refs_1_
  99.2 4.0 %collective-permute-start.4 = (bf16[256,1024]{1,0:T(8,128)(2,1)S(1)}, bf16[256,1024]{1,0:T(8,128)(2,1)S(1)}, u32[]{:S(2)}, u32[]{:S(2)}) collective-permute-start(bf16[256,1024]{1,0:T(8,128)(2,1)S(1)} %collective-permute-done.refs_1_), channel_id=1, source_target_pairs={{0,16},{16,0},{32,48},{48,32},{64,80},{80,64},{96,112},{112,96},{1... | collective-permute-start | bytes 1572872 | tf_op jit(solution)/shard_map/ppermute | solution.py:99
  103.2 0.8 copy-done.3
  104.0 7.5 %collective-permute-done.1.refs_2_ = bf16[256,1024]{1,0:T(8,128)(2,1)S(1)} collective-permute-done((bf16[256,1024]{1,0:T(8,128)(2,1)S(1)}, bf16[256,1024]{1,0:T(8,128)(2,1)S(1)}, u32[]{:S(2)}, u32[]{:S(2)}) %collective-permute-start.1) | collective-permute-done | bytes 524320 | tf_op jit(solution)/shard_map/ppermute | solution.py:96
  111.6 3.8 %collective-permute-start.5 = (bf16[256,1024]{1,0:T(8,128)(2,1)S(1)}, bf16[256,1024]{1,0:T(8,128)(2,1)S(1)}, u32[]{:S(2)}, u32[]{:S(2)}) collective-permute-start(bf16[256,1024]{1,0:T(8,128)(2,1)S(1)} %collective-permute-done.1.refs_2_), channel_id=1, source_target_pairs={{0,16},{16,0},{32,48},{48,32},{64,80},{80,64},{96,112},{112,96},{1... | collective-permute-start | bytes 1572872 | tf_op jit(solution)/shard_map/ppermute | solution.py:99
  115.4 0.8 copy-done.5
  116.1 1.9 collective-permute-start.6
  118.1 0.8 copy-done.7
  118.9 0.8 copy-done.9
  119.7 0.8 copy-done.11
  120.5 0.8 copy-done.13
  121.3 54.1 %all-to-all-done.a_ref = bf16[16,256,256]{2,1,0:T(8,128)(2,1)S(1)} async-done(((bf16[16,256,256]{2,1,0:T(8,128)(2,1)}), bf16[16,256,256]{2,1,0:T(8,128)(2,1)S(1)}, u32[]{:S(2)}, u32[]{:S(2)}) %all-to-all-start) | async-done | bytes 2097184 | tf_op jit(solution)/shard_map/all_to_all | solution.py:109
  175.4 1.0 copy-done.4
  176.4 1.0 copy-done.6
  177.4 1.0 copy-done.8
  178.5 1.0 copy-done.10
  179.5 1.0 copy-done.12
  180.6 1.0 copy-done.14
  181.6 2.7 %shard_map.69.own_ref = bf16[256,1024]{1,0:T(8,128)(2,1)} custom-call(s32[16,8]{1,0:T(8,128)S(1)} %copy-done.15, s32[16]{0:T(128)S(1)} %copy-done.16, bf16[16,256,256]{2,1,0:T(8,128)(2,1)S(1)} %all-to-all-done.a_ref, bf16[256,1024]{1,0:T(8,128)(2,1)S(1)} %bitcast.8, bf16[256,1024]{1,0:T(8,128)(2,1)S(1)} %copy-done.4, bf16[256,1024]{1,0:T(8,128)(2,1)S(1)} %copy-done.6, ...), custom_call_target="tpu_custom_call" | custom-call | flops 1073741824 | bytes 7340032 | tf_op jit(solution)/shard_map/pallas_call | solution.py:122
  184.3 6.6 %collective-permute-start.7 = (bf16[256,1024]{1,0:T(8,128)(2,1)}, bf16[256,1024]{1,0:T(8,128)(2,1)S(1)}, u32[]{:S(2)}, u32[]{:S(2)}) collective-permute-start(bf16[256,1024]{1,0:T(8,128)(2,1)} %shard_map.69.own_ref), channel_id=1, source_target_pairs={{0,16},{16,0},{32,48},{48,32},{64,80},{80,64},{96,112},{112,96},{1... | collective-permute-start | bytes 1572872 | tf_op jit(solution)/shard_map/ppermute | solution.py:99
  191.2 1.5 collective-permute-done.7.other_ref
  192.7 1.0 copy-done.1
  193.7 0.7 shard_map.71
  194.5 18.2 %all_to_all.10.terms_ref = bf16[4,128,1024]{2,1,0:T(8,128)(2,1)S(1)} all-to-all(bf16[4,128,1024]{2,1,0:T(8,128)(2,1)S(1)} %shard_map.71), channel_id=1, replica_groups={{0,32,64,96},{16,48,80,112},{1,33,65,97},{17,49,81,113},{2,34,66,98},{1..., dimensions={0} | all-to-all | bytes 2097152 | tf_op jit(solution)/shard_map/all_to_all | solution.py:140
  212.7 0.9 shard_map.72
  (27 shorter events, 0.3 us)
Async XLA Ops:
  67.6 15.9 %copy-start = (bf16[1,1,256,1024]{3,2,1,0:T(8,128)(2,1)S(1)}, bf16[1,1,256,1024]{3,2,1,0:T(8,128)(2,1)}, u32[]{:S(2)}) copy-start(bf16[1,1,256,1024]{3,2,1,0:T(8,128)(2,1)} %param.6) | copy-start | bytes 1572868
  67.6 107.8 %copy-start.15 = (s32[16,8]{1,0:T(8,128)S(1)}, s32[16,8]{1,0:T(8,128)}, u32[]{:S(2)}) copy-start(s32[16,8]{1,0:T(8,128)} %copy.8.anc_ref) | copy-start | bytes 1540
  67.6 107.8 %copy-start.16 = (s32[16]{0:T(128)S(1)}, s32[16]{0:T(128)}, u32[]{:S(2)}) copy-start(s32[16]{0:T(128)} %count_ref.1) | copy-start | bytes 196
  67.6 107.7 %all-to-all-start = ((bf16[16,256,256]{2,1,0:T(8,128)(2,1)}), bf16[16,256,256]{2,1,0:T(8,128)(2,1)S(1)}, u32[]{:S(2)}, u32[]{:S(2)}) async-start(bf16[16,256,256]{2,1,0:T(8,128)(2,1)} %shard_map.68), calls=%async_computation | async-start | bytes 4194304 | tf_op jit(solution)/shard_map/all_to_all | solution.py:109
  83.5 15.7 %collective-permute-start = (bf16[256,1024]{1,0:T(8,128)(2,1)S(1)}, bf16[256,1024]{1,0:T(8,128)(2,1)S(1)}, u32[]{:S(2)}, u32[]{:S(2)}) collective-permute-start(bf16[256,1024]{1,0:T(8,128)(2,1)S(1)} %bitcast.4), channel_id=1, source_target_pairs={{0,32},{16,48},{32,64},{48,80},{64,96},{80,112},{96,0},{112,16},{1... | collective-permute-start | bytes 1572872 | tf_op jit(solution)/shard_map/ppermute | solution.py:96
  86.7 24.8 %collective-permute-start.1 = (bf16[256,1024]{1,0:T(8,128)(2,1)S(1)}, bf16[256,1024]{1,0:T(8,128)(2,1)S(1)}, u32[]{:S(2)}, u32[]{:S(2)}) collective-permute-start(bf16[256,1024]{1,0:T(8,128)(2,1)S(1)} %bitcast.5), channel_id=1, source_target_pairs={{0,64},{16,80},{32,96},{48,112},{64,0},{80,16},{96,32},{112,48},{1... | collective-permute-start | bytes 1572872 | tf_op jit(solution)/shard_map/ppermute | solution.py:96
  91.3 24.9 %collective-permute-start.2 = (bf16[256,1024]{1,0:T(8,128)(2,1)S(1)}, bf16[256,1024]{1,0:T(8,128)(2,1)S(1)}, u32[]{:S(2)}, u32[]{:S(2)}) collective-permute-start(bf16[256,1024]{1,0:T(8,128)(2,1)S(1)} %bitcast.6), channel_id=1, source_target_pairs={{0,96},{16,112},{32,0},{48,16},{64,32},{80,48},{96,64},{112,80},{1... | collective-permute-start | bytes 1572872 | tf_op jit(solution)/shard_map/ppermute | solution.py:96
  94.3 24.6 %collective-permute-start.3 = (bf16[256,1024]{1,0:T(8,128)(2,1)S(1)}, bf16[256,1024]{1,0:T(8,128)(2,1)S(1)}, u32[]{:S(2)}, u32[]{:S(2)}) collective-permute-start(bf16[256,1024]{1,0:T(8,128)(2,1)S(1)} %bitcast.7), channel_id=1, source_target_pairs={{0,16},{16,0},{32,48},{48,32},{64,80},{80,64},{96,112},{112,96},{1... | collective-permute-start | bytes 1572872 | tf_op jit(solution)/shard_map/ppermute | solution.py:99
  99.2 19.6 %collective-permute-start.4 = (bf16[256,1024]{1,0:T(8,128)(2,1)S(1)}, bf16[256,1024]{1,0:T(8,128)(2,1)S(1)}, u32[]{:S(2)}, u32[]{:S(2)}) collective-permute-start(bf16[256,1024]{1,0:T(8,128)(2,1)S(1)} %collective-permute-done.refs_1_), channel_id=1, source_target_pairs={{0,16},{16,0},{32,48},{48,32},{64,80},{80,64},{96,112},{112,96},{1... | collective-permute-start | bytes 1572872 | tf_op jit(solution)/shard_map/ppermute | solution.py:99
  103.2 0.8 copy-start.3
  111.6 8.1 %collective-permute-start.5 = (bf16[256,1024]{1,0:T(8,128)(2,1)S(1)}, bf16[256,1024]{1,0:T(8,128)(2,1)S(1)}, u32[]{:S(2)}, u32[]{:S(2)}) collective-permute-start(bf16[256,1024]{1,0:T(8,128)(2,1)S(1)} %collective-permute-done.1.refs_2_), channel_id=1, source_target_pairs={{0,16},{16,0},{32,48},{48,32},{64,80},{80,64},{96,112},{112,96},{1... | collective-permute-start | bytes 1572872 | tf_op jit(solution)/shard_map/ppermute | solution.py:99
  115.3 0.8 copy-start.5
  116.1 4.3 %collective-permute-start.6 = (bf16[256,1024]{1,0:T(8,128)(2,1)S(1)}, bf16[256,1024]{1,0:T(8,128)(2,1)S(1)}, u32[]{:S(2)}, u32[]{:S(2)}) collective-permute-start(bf16[256,1024]{1,0:T(8,128)(2,1)S(1)} %collective-permute-done.2.refs_3_), channel_id=1, source_target_pairs={{0,16},{16,0},{32,48},{48,32},{64,80},{80,64},{96,112},{112,96},{1... | collective-permute-start | bytes 1572872 | tf_op jit(solution)/shard_map/ppermute | solution.py:99
  118.1 0.8 copy-start.7
  118.9 0.8 copy-start.9
  119.7 0.8 copy-start.11
  120.5 0.8 copy-start.13
  175.4 1.0 copy-start.4
  176.4 1.0 copy-start.6
  177.4 1.0 copy-start.8
  178.5 1.0 copy-start.10
  179.5 1.0 copy-start.12
  180.6 1.0 copy-start.14
  184.3 8.3 %collective-permute-start.7 = (bf16[256,1024]{1,0:T(8,128)(2,1)}, bf16[256,1024]{1,0:T(8,128)(2,1)S(1)}, u32[]{:S(2)}, u32[]{:S(2)}) collective-permute-start(bf16[256,1024]{1,0:T(8,128)(2,1)} %shard_map.69.own_ref), channel_id=1, source_target_pairs={{0,16},{16,0},{32,48},{48,32},{64,80},{80,64},{96,112},{112,96},{1... | collective-permute-start | bytes 1572872 | tf_op jit(solution)/shard_map/ppermute | solution.py:99
  192.7 1.0 copy-start.1
  193.7 19.0 %copy-start.2 = (f32[1,128,1024]{2,1,0:T(8,128)S(1)}, f32[1,128,1024]{2,1,0:T(8,128)}, u32[]{:S(2)}) copy-start(f32[1,128,1024]{2,1,0:T(8,128)} %param.7) | copy-start | bytes 1572868

commit v2 on v1

--- a/solution.py
+++ b/solution.py
@@ -12,28 +12,37 @@
 MIB = 1024 * 1024
 
 
-def pick_kernel(rows, cols, anc_ref, a_ref, out_ref, sems):
+def pick_kernel(rows, cols, anc_ref, a_ref, out_ref, held, in_sems, out_sems):
     me_row = lax.axis_index("prow")
     me_col = lax.axis_index("pcol")
     slot = lax.rem(me_col, rows)
-    copies = []
+    high, wide = a_ref.shape[0] // W, a_ref.shape[1] // W
+    loads = []
+    for n in range(high * wide):
+        i, j = n // wide, n % wide
+        loads.append(
+            pltpu.make_async_copy(a_ref.at[pl.ds(i * W, W), pl.ds(j * W, W)], held.at[n], in_sems.at[n])
+        )
+    for load in loads:
+        load.start()
+    picks = []
     for k in range(cols):
-        i = anc_ref[k, me_row] // rows
-        j = anc_ref[k, slot] // cols
-        copy = pltpu.make_async_copy(
-            a_ref.at[pl.ds(pl.multiple_of(i * W, W), W), pl.ds(pl.multiple_of(j * W, W), W)],
-            out_ref.at[k],
-            sems.at[k],
-        )
-        copy.start()
-        copies.append(copy)
-    for copy in copies:
-        copy.wait()
+        picks.append((anc_ref[me_row, k] // rows) * wide + anc_ref[slot, k] // cols)
+    for load in loads:
+        load.wait()
+    stores = [pltpu.make_async_copy(held.at[picks[k]], out_ref.at[k], out_sems.at[k]) for k in range(cols)]
+    for store in stores:
+        store.start()
+    for store in stores:
+        store.wait()
 
 
 def product_kernel(rows, cols, anc_ref, count_ref, a_ref, *refs):
     f_refs = refs[:rows]
-    out_ref, held = refs[rows:]
+    out_ref, own_ref, held, factors, sems, out_sem = refs[rows:]
+    loads = [pltpu.make_async_copy(f_refs[n], factors.at[n], sems.at[n]) for n in range(rows)]
+    for load in loads:
+        load.start()
     me_row = lax.axis_index("prow")
     me_col = lax.axis_index("pcol")
     count = count_ref[me_col]
@@ -41,14 +50,19 @@
     for n in range(rows):
         t = slot_row(me_row, n, rows)
         live = (t < count).astype(jnp.bfloat16)
-        held[n] = a_ref[lax.rem(anc_ref[me_col, t], cols)] * live
-    width = out_ref.shape[-1]
+        held[n] = a_ref[lax.rem(anc_ref[t, me_col], cols)] * live
+    for load in loads:
+        load.wait()
+    width = own_ref.shape[-1]
     step = 256
     for at in range(0, width, step):
         total = jnp.zeros((W, step), jnp.float32)
         for n in range(rows):
-            total += jnp.dot(held[n], f_refs[n][:, at : at + step], preferred_element_type=jnp.float32)
-        out_ref[:, at : at + step] = (total * -row_live).astype(jnp.bfloat16)
+            total += jnp.dot(held[n], factors[n, :, at : at + step], preferred_element_type=jnp.float32)
+        own_ref[:, at : at + step] = (total * -row_live).astype(jnp.bfloat16)
+    store = pltpu.make_async_copy(own_ref, out_ref, out_sem)
+    store.start()
+    store.wait()
 
 
 def slot_row(me_row, n, rows):
@@ -82,7 +96,7 @@
 
 SMEM = pl.BlockSpec(memory_space=pltpu.SMEM)
 VMEM = pl.BlockSpec(memory_space=pltpu.VMEM)
-ANY = pl.BlockSpec(memory_space=pl.ANY)
+HBM = pl.BlockSpec(memory_space=pltpu.HBM)
 
 
 def local(anc_inverse, factor_blocks, diag_in, ancestors, active_count):
@@ -91,6 +105,8 @@
     chips = rows // 2
     width = factor_blocks.shape[-1]
     factor = factor_blocks[0, 0]
+    blocks = (anc_inverse.shape[0] // W) * (anc_inverse.shape[1] // W)
+    lists = ancestors.T
 
     def shift(x, h):
         return lax.ppermute(x, "prow", [(i, (i + 2 * h) % rows) for i in range(rows)])
@@ -101,11 +117,16 @@
     sending = pl.pallas_call(
         functools.partial(pick_kernel, rows, cols),
         out_shape=jax.ShapeDtypeStruct((cols, W, W), jnp.bfloat16),
-        in_specs=[SMEM, ANY],
-        out_specs=ANY,
-        scratch_shapes=[pltpu.SemaphoreType.DMA((cols,))],
-        cost_estimate=pl.CostEstimate(flops=0, bytes_accessed=4 * MIB, transcendentals=0),
-    )(ancestors, anc_inverse)
+        in_specs=[SMEM, HBM],
+        out_specs=HBM,
+        scratch_shapes=[
+            pltpu.VMEM((blocks, W, W), jnp.bfloat16),
+            pltpu.SemaphoreType.DMA((blocks,)),
+            pltpu.SemaphoreType.DMA((cols,)),
+        ],
+        compiler_params=pltpu.CompilerParams(vmem_limit_bytes=16 * MIB),
+        cost_estimate=pl.CostEstimate(flops=0, bytes_accessed=3 * MIB, transcendentals=0),
+    )(lists, anc_inverse)
     arrived = lax.all_to_all(sending, "pcol", split_axis=0, concat_axis=0, tiled=True)
 
     same = [factor] + [shift(factor, h if h <= chips // 2 else h - chips) for h in range(1, chips)]
@@ -119,15 +140,20 @@
         cost_estimate=pl.CostEstimate(flops=0, bytes_accessed=2 * MIB, transcendentals=0),
     )(factors[0], factors[chips])
 
-    product = pl.pallas_call(
+    product, own = pl.pallas_call(
         functools.partial(product_kernel, rows, cols),
-        out_shape=jax.ShapeDtypeStruct((W, width), jnp.bfloat16),
-        in_specs=[SMEM, SMEM] + [VMEM] * (1 + rows),
-        out_specs=VMEM,
-        scratch_shapes=[pltpu.VMEM((rows, W, W), jnp.bfloat16)],
+        out_shape=(jax.ShapeDtypeStruct((W, width), jnp.bfloat16),) * 2,
+        in_specs=[SMEM, SMEM, VMEM] + [HBM] * rows,
+        out_specs=(HBM, VMEM),
+        scratch_shapes=[
+            pltpu.VMEM((rows, W, W), jnp.bfloat16),
+            pltpu.VMEM((rows, W, width), jnp.bfloat16),
+            pltpu.SemaphoreType.DMA((rows,)),
+            pltpu.SemaphoreType.DMA,
+        ],
         compiler_params=pltpu.CompilerParams(vmem_limit_bytes=32 * MIB),
         cost_estimate=pl.CostEstimate(flops=2 * rows * W * W * width, bytes_accessed=7 * MIB, transcendentals=0),
-    )(ancestors, active_count, arrived, *factors)
+    )(lists, active_count, arrived, *factors)
     terms = pl.pallas_call(
         term_kernel,
         out_shape=jax.ShapeDtypeStruct((chips, SLICE, width), jnp.bfloat16),
@@ -135,7 +161,7 @@
         out_specs=VMEM,
         compiler_params=pltpu.CompilerParams(vmem_limit_bytes=16 * MIB),
         cost_estimate=pl.CostEstimate(flops=4 * chips * SLICE * W * width, bytes_accessed=3 * MIB, transcendentals=0),
-    )(turned, product, swap(product))
+    )(turned, own, swap(own))
     groups = [list(range(core, rows, 2)) for core in range(2)]
     met = lax.all_to_all(terms, "prow", split_axis=0, concat_axis=0, tiled=True, axis_index_groups=groups)
     diagonal = pl.pallas_call(

time: 215 us -> 151 us (0.70)
  Pallas kernels: 70.2 us -> 7.42 us
    pallas_call x1, Pallas kernels: 65.6 us -> 2.42 us  [local(): pl.pallas_call(functools.partial(pick_kernel, rows, cols), out_shape=jax....]
    unnamed x35 -> x36, local copies, waits for them, and re-layouts: 13.4 us -> 13 us
where the time goes in v2:
time: 151 us; the launch traced here: 150 us
  waiting for transfers between devices  64.2 us (43%)
  starting transfers between devices  46.6 us (31%)
  blocking collectives  18.2 us (12%)
  local copies, waits for them, and re-layouts  13 us (9%)
  Pallas kernels  7.42 us (5%)
    all_to_all x1, waiting for transfers between devices, local(): lax.all_to_all(sending, 'pcol', split_axis=0, concat_axis=0, tiled=True)  54.1 us
    ppermute x5, starting transfers between devices, swap(): return lax.ppermute(x, 'prow', [(i, i ^ 1) for i in range(rows)])  20 us
    all_to_all x1, blocking collectives, local(): lax.all_to_all(terms, 'prow', split_axis=0, concat_axis=0, tiled=True, ax...  18.2 us
    all_to_all x1, starting transfers between devices, local(): lax.all_to_all(sending, 'pcol', split_axis=0, concat_axis=0, tiled=True)  15.9 us
    unnamed x36, local copies, waits for them, and re-layouts  13 us
    ppermute x3, starting transfers between devices, shift(): lax.ppermute(x, 'prow', [(i, (i + 2 * h) % rows) for i in range(rows)])  10.7 us
    ppermute x3, waiting for transfers between devices, shift(): lax.ppermute(x, 'prow', [(i, (i + 2 * h) % rows) for i in range(rows)])  8.83 us
    pallas_call x1, Pallas kernels, local(): pl.pallas_call(functools.partial(product_kernel, rows, cols), out_shape=(...  3.12 us
  transfers between devices with their start and end apart: 9, of which 4 were waited for; matrix products, arithmetic and copies ran while one was open for 0% of the time, Pallas kernels for 0%

profile of v2, /device:TPU:1, one launch (start us, length us, event | category | flops | bytes accessed | tf_op | source)
XLA Modules:
  0.0 150.2 jit_solution(5060374954825761148)
XLA Ops:
  0.6 1.2 copy-done.1
  1.9 0.7 copy-done.15
  2.5 2.4 %shard_map.68 = bf16[16,256,256]{2,1,0:T(8,128)(2,1)} custom-call(s32[8,16]{1,0:T(8,128)S(1)} %bitcast.12, bf16[1024,512]{1,0:T(8,128)(2,1)S(1)} %copy-done.1), custom_call_target="tpu_custom_call" | custom-call | bytes 3145728 | tf_op jit(solution)/shard_map/pallas_call | solution.py:117
  5.0 15.9 %all-to-all-start = ((bf16[16,256,256]{2,1,0:T(8,128)(2,1)}), bf16[16,256,256]{2,1,0:T(8,128)(2,1)S(1)}, u32[]{:S(2)}, u32[]{:S(2)}) async-start(bf16[16,256,256]{2,1,0:T(8,128)(2,1)} %shard_map.68), calls=%async_computation | async-start | bytes 4194304 | tf_op jit(solution)/shard_map/all_to_all | solution.py:130
  20.9 3.2 %collective-permute-start = (bf16[256,1024]{1,0:T(8,128)(2,1)S(1)}, bf16[256,1024]{1,0:T(8,128)(2,1)S(1)}, u32[]{:S(2)}, u32[]{:S(2)}) collective-permute-start(bf16[256,1024]{1,0:T(8,128)(2,1)S(1)} %bitcast.5), channel_id=1, source_target_pairs={{0,32},{16,48},{32,64},{48,80},{64,96},{80,112},{96,0},{112,16},{1... | collective-permute-start | bytes 1572872 | tf_op jit(solution)/shard_map/ppermute | solution.py:112
  24.1 4.5 %collective-permute-start.1 = (bf16[256,1024]{1,0:T(8,128)(2,1)S(1)}, bf16[256,1024]{1,0:T(8,128)(2,1)S(1)}, u32[]{:S(2)}, u32[]{:S(2)}) collective-permute-start(bf16[256,1024]{1,0:T(8,128)(2,1)S(1)} %bitcast.6), channel_id=1, source_target_pairs={{0,64},{16,80},{32,96},{48,112},{64,0},{80,16},{96,32},{112,48},{1... | collective-permute-start | bytes 1572872 | tf_op jit(solution)/shard_map/ppermute | solution.py:112
  28.7 3.0 %collective-permute-start.2 = (bf16[256,1024]{1,0:T(8,128)(2,1)S(1)}, bf16[256,1024]{1,0:T(8,128)(2,1)S(1)}, u32[]{:S(2)}, u32[]{:S(2)}) collective-permute-start(bf16[256,1024]{1,0:T(8,128)(2,1)S(1)} %bitcast.7), channel_id=1, source_target_pairs={{0,96},{16,112},{32,0},{48,16},{64,32},{80,48},{96,64},{112,80},{1... | collective-permute-start | bytes 1572872 | tf_op jit(solution)/shard_map/ppermute | solution.py:112
  31.6 3.7 %collective-permute-start.3 = (bf16[256,1024]{1,0:T(8,128)(2,1)S(1)}, bf16[256,1024]{1,0:T(8,128)(2,1)S(1)}, u32[]{:S(2)}, u32[]{:S(2)}) collective-permute-start(bf16[256,1024]{1,0:T(8,128)(2,1)S(1)} %bitcast.8), channel_id=1, source_target_pairs={{0,16},{16,0},{32,48},{48,32},{64,80},{80,64},{96,112},{112,96},{1... | collective-permute-start | bytes 1572872 | tf_op jit(solution)/shard_map/ppermute | solution.py:115
  35.4 1.3 collective-permute-done.refs_1_
  36.6 4.0 %collective-permute-start.4 = (bf16[256,1024]{1,0:T(8,128)(2,1)S(1)}, bf16[256,1024]{1,0:T(8,128)(2,1)S(1)}, u32[]{:S(2)}, u32[]{:S(2)}) collective-permute-start(bf16[256,1024]{1,0:T(8,128)(2,1)S(1)} %collective-permute-done.refs_1_), channel_id=1, source_target_pairs={{0,16},{16,0},{32,48},{48,32},{64,80},{80,64},{96,112},{112,96},{1... | collective-permute-start | bytes 1572872 | tf_op jit(solution)/shard_map/ppermute | solution.py:115
  40.6 0.8 copy-done.2
  41.4 7.5 %collective-permute-done.1.refs_2_ = bf16[256,1024]{1,0:T(8,128)(2,1)S(1)} collective-permute-done((bf16[256,1024]{1,0:T(8,128)(2,1)S(1)}, bf16[256,1024]{1,0:T(8,128)(2,1)S(1)}, u32[]{:S(2)}, u32[]{:S(2)}) %collective-permute-start.1) | collective-permute-done | bytes 524320 | tf_op jit(solution)/shard_map/ppermute | solution.py:112
  49.0 3.8 %collective-permute-start.5 = (bf16[256,1024]{1,0:T(8,128)(2,1)S(1)}, bf16[256,1024]{1,0:T(8,128)(2,1)S(1)}, u32[]{:S(2)}, u32[]{:S(2)}) collective-permute-start(bf16[256,1024]{1,0:T(8,128)(2,1)S(1)} %collective-permute-done.1.refs_2_), channel_id=1, source_target_pairs={{0,16},{16,0},{32,48},{48,32},{64,80},{80,64},{96,112},{112,96},{1... | collective-permute-start | bytes 1572872 | tf_op jit(solution)/shard_map/ppermute | solution.py:115
  52.8 0.8 copy-done.4
  53.5 1.9 %collective-permute-start.6 = (bf16[256,1024]{1,0:T(8,128)(2,1)S(1)}, bf16[256,1024]{1,0:T(8,128)(2,1)S(1)}, u32[]{:S(2)}, u32[]{:S(2)}) collective-permute-start(bf16[256,1024]{1,0:T(8,128)(2,1)S(1)} %collective-permute-done.2.refs_3_), channel_id=1, source_target_pairs={{0,16},{16,0},{32,48},{48,32},{64,80},{80,64},{96,112},{112,96},{1... | collective-permute-start | bytes 1572872 | tf_op jit(solution)/shard_map/ppermute | solution.py:115
  55.5 0.8 copy-done.6
  56.3 0.8 copy-done.8
  57.1 0.8 copy-done.10
  57.9 0.8 copy-done.12
  58.7 54.1 %all-to-all-done.a_ref = bf16[16,256,256]{2,1,0:T(8,128)(2,1)S(1)} async-done(((bf16[16,256,256]{2,1,0:T(8,128)(2,1)}), bf16[16,256,256]{2,1,0:T(8,128)(2,1)S(1)}, u32[]{:S(2)}, u32[]{:S(2)}) %all-to-all-start) | async-done | bytes 2097184 | tf_op jit(solution)/shard_map/all_to_all | solution.py:130
  112.8 1.0 copy-done.3
  113.8 1.0 copy-done.5
  114.8 1.0 copy-done.7
  115.9 1.0 copy-done.9
  116.9 1.0 copy-done.11
  118.0 1.0 copy-done.13
  119.0 3.1 %shard_map.69 = (bf16[256,1024]{1,0:T(8,128)(2,1)}, bf16[256,1024]{1,0:T(8,128)(2,1)S(1)}) custom-call(s32[8,16]{1,0:T(8,128)S(1)} %bitcast.13, s32[16]{0:T(128)S(1)} %copy-done.17, bf16[16,256,256]{2,1,0:T(8,128)(2,1)S(1)} %all-to-all-done.a_ref, bf16[256,1024]{1,0:T(8,128)(2,1)S(1)} %bitcast.9, bf16[256,1024]{1,0:T(8,128)(2,1)S(1)} %copy-done.3, ...), custom_call_target="tpu_custom_call" | custom-call | flops 1073741824 | bytes 7340032 | tf_op jit(solution)/shard_map/pallas_call | solution.py:143
  122.1 6.6 %collective-permute-start.7 = (bf16[256,1024]{1,0:T(8,128)(2,1)S(1)}, bf16[256,1024]{1,0:T(8,128)(2,1)S(1)}, u32[]{:S(2)}, u32[]{:S(2)}) collective-permute-start(bf16[256,1024]{1,0:T(8,128)(2,1)S(1)} %get-tuple-element.5.own_ref), channel_id=1, source_target_pairs={{0,16},{16,0},{32,48},{48,32},{64,80},{80,64},{96,112},{112,96},{1... | collective-permute-start | bytes 1572872 | tf_op jit(solution)/shard_map/ppermute | solution.py:115
  129.0 1.3 collective-permute-done.7.other_ref
  130.3 0.7 shard_map.71
  131.0 18.2 %all_to_all.10.terms_ref = bf16[4,128,1024]{2,1,0:T(8,128)(2,1)S(1)} all-to-all(bf16[4,128,1024]{2,1,0:T(8,128)(2,1)S(1)} %shard_map.71), channel_id=1, replica_groups={{0,32,64,96},{16,48,80,112},{1,33,65,97},{17,49,81,113},{2,34,66,98},{1..., dimensions={0} | all-to-all | bytes 2097152 | tf_op jit(solution)/shard_map/all_to_all | solution.py:166
  149.2 0.9 shard_map.72
  (28 shorter events, 0.3 us)
Async XLA Ops:
  0.6 1.2 copy-start.1
  1.9 0.7 copy-start.15
  5.0 15.9 %copy-start = (bf16[1,1,256,1024]{3,2,1,0:T(8,128)(2,1)S(1)}, bf16[1,1,256,1024]{3,2,1,0:T(8,128)(2,1)}, u32[]{:S(2)}) copy-start(bf16[1,1,256,1024]{3,2,1,0:T(8,128)(2,1)} %param.6) | copy-start | bytes 1572868
  5.0 107.8 %copy-start.16 = (s32[16,8]{0,1:T(8,128)S(1)}, s32[16,8]{0,1:T(8,128)}, u32[]{:S(2)}) copy-start(s32[16,8]{0,1:T(8,128)} %param.8) | copy-start | bytes 1540
  5.0 107.8 %copy-start.17 = (s32[16]{0:T(128)S(1)}, s32[16]{0:T(128)}, u32[]{:S(2)}) copy-start(s32[16]{0:T(128)} %count_ref.1) | copy-start | bytes 196
  5.0 107.7 %all-to-all-start = ((bf16[16,256,256]{2,1,0:T(8,128)(2,1)}), bf16[16,256,256]{2,1,0:T(8,128)(2,1)S(1)}, u32[]{:S(2)}, u32[]{:S(2)}) async-start(bf16[16,256,256]{2,1,0:T(8,128)(2,1)} %shard_map.68), calls=%async_computation | async-start | bytes 4194304 | tf_op jit(solution)/shard_map/all_to_all | solution.py:130
  20.9 15.7 %collective-permute-start = (bf16[256,1024]{1,0:T(8,128)(2,1)S(1)}, bf16[256,1024]{1,0:T(8,128)(2,1)S(1)}, u32[]{:S(2)}, u32[]{:S(2)}) collective-permute-start(bf16[256,1024]{1,0:T(8,128)(2,1)S(1)} %bitcast.5), channel_id=1, source_target_pairs={{0,32},{16,48},{32,64},{48,80},{64,96},{80,112},{96,0},{112,16},{1... | collective-permute-start | bytes 1572872 | tf_op jit(solution)/shard_map/ppermute | solution.py:112
  24.1 24.8 %collective-permute-start.1 = (bf16[256,1024]{1,0:T(8,128)(2,1)S(1)}, bf16[256,1024]{1,0:T(8,128)(2,1)S(1)}, u32[]{:S(2)}, u32[]{:S(2)}) collective-permute-start(bf16[256,1024]{1,0:T(8,128)(2,1)S(1)} %bitcast.6), channel_id=1, source_target_pairs={{0,64},{16,80},{32,96},{48,112},{64,0},{80,16},{96,32},{112,48},{1... | collective-permute-start | bytes 1572872 | tf_op jit(solution)/shard_map/ppermute | solution.py:112
  28.7 24.9 %collective-permute-start.2 = (bf16[256,1024]{1,0:T(8,128)(2,1)S(1)}, bf16[256,1024]{1,0:T(8,128)(2,1)S(1)}, u32[]{:S(2)}, u32[]{:S(2)}) collective-permute-start(bf16[256,1024]{1,0:T(8,128)(2,1)S(1)} %bitcast.7), channel_id=1, source_target_pairs={{0,96},{16,112},{32,0},{48,16},{64,32},{80,48},{96,64},{112,80},{1... | collective-permute-start | bytes 1572872 | tf_op jit(solution)/shard_map/ppermute | solution.py:112
  31.6 24.6 %collective-permute-start.3 = (bf16[256,1024]{1,0:T(8,128)(2,1)S(1)}, bf16[256,1024]{1,0:T(8,128)(2,1)S(1)}, u32[]{:S(2)}, u32[]{:S(2)}) collective-permute-start(bf16[256,1024]{1,0:T(8,128)(2,1)S(1)} %bitcast.8), channel_id=1, source_target_pairs={{0,16},{16,0},{32,48},{48,32},{64,80},{80,64},{96,112},{112,96},{1... | collective-permute-start | bytes 1572872 | tf_op jit(solution)/shard_map/ppermute | solution.py:115
  36.6 19.6 %collective-permute-start.4 = (bf16[256,1024]{1,0:T(8,128)(2,1)S(1)}, bf16[256,1024]{1,0:T(8,128)(2,1)S(1)}, u32[]{:S(2)}, u32[]{:S(2)}) collective-permute-start(bf16[256,1024]{1,0:T(8,128)(2,1)S(1)} %collective-permute-done.refs_1_), channel_id=1, source_target_pairs={{0,16},{16,0},{32,48},{48,32},{64,80},{80,64},{96,112},{112,96},{1... | collective-permute-start | bytes 1572872 | tf_op jit(solution)/shard_map/ppermute | solution.py:115
  40.6 0.8 copy-start.2
  49.0 8.1 %collective-permute-start.5 = (bf16[256,1024]{1,0:T(8,128)(2,1)S(1)}, bf16[256,1024]{1,0:T(8,128)(2,1)S(1)}, u32[]{:S(2)}, u32[]{:S(2)}) collective-permute-start(bf16[256,1024]{1,0:T(8,128)(2,1)S(1)} %collective-permute-done.1.refs_2_), channel_id=1, source_target_pairs={{0,16},{16,0},{32,48},{48,32},{64,80},{80,64},{96,112},{112,96},{1... | collective-permute-start | bytes 1572872 | tf_op jit(solution)/shard_map/ppermute | solution.py:115
  52.7 0.8 copy-start.4
  53.5 4.4 %collective-permute-start.6 = (bf16[256,1024]{1,0:T(8,128)(2,1)S(1)}, bf16[256,1024]{1,0:T(8,128)(2,1)S(1)}, u32[]{:S(2)}, u32[]{:S(2)}) collective-permute-start(bf16[256,1024]{1,0:T(8,128)(2,1)S(1)} %collective-permute-done.2.refs_3_), channel_id=1, source_target_pairs={{0,16},{16,0},{32,48},{48,32},{64,80},{80,64},{96,112},{112,96},{1... | collective-permute-start | bytes 1572872 | tf_op jit(solution)/shard_map/ppermute | solution.py:115
  55.5 0.8 copy-start.6
  56.3 0.8 copy-start.8
  57.1 0.8 copy-start.10
  57.9 0.8 copy-start.12
  112.8 1.0 copy-start.3
  113.8 1.0 copy-start.5
  114.8 1.0 copy-start.7
  115.9 1.0 copy-start.9
  116.9 1.0 copy-start.11
  118.0 1.0 copy-start.13
  122.1 8.2 %collective-permute-start.7 = (bf16[256,1024]{1,0:T(8,128)(2,1)S(1)}, bf16[256,1024]{1,0:T(8,128)(2,1)S(1)}, u32[]{:S(2)}, u32[]{:S(2)}) collective-permute-start(bf16[256,1024]{1,0:T(8,128)(2,1)S(1)} %get-tuple-element.5.own_ref), channel_id=1, source_target_pairs={{0,16},{16,0},{32,48},{48,32},{64,80},{80,64},{96,112},{112,96},{1... | collective-permute-start | bytes 1572872 | tf_op jit(solution)/shard_map/ppermute | solution.py:115
  129.0 20.2 %copy-start.14 = (f32[1,128,1024]{2,1,0:T(8,128)S(1)}, f32[1,128,1024]{2,1,0:T(8,128)}, u32[]{:S(2)}) copy-start(f32[1,128,1024]{2,1,0:T(8,128)} %param.7) | copy-start | bytes 1572868

commit v3 on v2

--- a/solution.py
+++ b/solution.py
@@ -13,36 +13,39 @@
 
 
 def pick_kernel(rows, cols, anc_ref, a_ref, out_ref, held, in_sems, out_sems):
-    me_row = lax.axis_index("prow")
-    me_col = lax.axis_index("pcol")
-    slot = lax.rem(me_col, rows)
     high, wide = a_ref.shape[0] // W, a_ref.shape[1] // W
     loads = []
     for n in range(high * wide):
         i, j = n // wide, n % wide
-        loads.append(
-            pltpu.make_async_copy(a_ref.at[pl.ds(i * W, W), pl.ds(j * W, W)], held.at[n], in_sems.at[n])
-        )
-    for load in loads:
+        load = pltpu.make_async_copy(a_ref.at[pl.ds(i * W, W), pl.ds(j * W, W)], held.at[n], in_sems.at[n])
         load.start()
-    picks = []
+        loads.append(load)
+    me_row = lax.axis_index("prow")
+    me_col = lax.axis_index("pcol")
+    slot = lax.rem(me_col, rows)
+    stores = []
     for k in range(cols):
-        picks.append((anc_ref[me_row, k] // rows) * wide + anc_ref[slot, k] // cols)
+        name = anc_ref[slot, k]
+        pick = (anc_ref[me_row, k] // rows) * wide + name // cols
+        store = pltpu.make_async_copy(held.at[pick], out_ref.at[k], out_sems.at[k])
+        stores.append((lax.rem(name, cols) == me_col, store))
     for load in loads:
         load.wait()
-    stores = [pltpu.make_async_copy(held.at[picks[k]], out_ref.at[k], out_sems.at[k]) for k in range(cols)]
-    for store in stores:
-        store.start()
-    for store in stores:
-        store.wait()
-
-
-def product_kernel(rows, cols, anc_ref, count_ref, a_ref, *refs):
-    f_refs = refs[:rows]
-    out_ref, own_ref, held, factors, sems, out_sem = refs[rows:]
-    loads = [pltpu.make_async_copy(f_refs[n], factors.at[n], sems.at[n]) for n in range(rows)]
-    for load in loads:
+    for owed, store in stores:
+        pl.when(owed)(store.start)
+    for owed, store in stores:
+        pl.when(owed)(store.wait)
+
+
+def product_kernel(rows, cols, anc_ref, count_ref, a_ref, f_ref, out_ref, own_ref, held, factors, total, sems, out_sems):
+    half = rows // 2
+    width = own_ref.shape[-1]
+    step = 256
+    loads = []
+    for n in range(rows):
+        load = pltpu.make_async_copy(f_ref.at[n], factors.at[n], sems.at[n])
         load.start()
+        loads.append(load)
     me_row = lax.axis_index("prow")
     me_col = lax.axis_index("pcol")
     count = count_ref[me_col]
@@ -51,18 +54,25 @@
         t = slot_row(me_row, n, rows)
         live = (t < count).astype(jnp.bfloat16)
         held[n] = a_ref[lax.rem(anc_ref[t, me_col], cols)] * live
-    for load in loads:
-        load.wait()
-    width = own_ref.shape[-1]
-    step = 256
-    for at in range(0, width, step):
-        total = jnp.zeros((W, step), jnp.float32)
-        for n in range(rows):
-            total += jnp.dot(held[n], factors[n, :, at : at + step], preferred_element_type=jnp.float32)
-        own_ref[:, at : at + step] = (total * -row_live).astype(jnp.bfloat16)
-    store = pltpu.make_async_copy(own_ref, out_ref, out_sem)
-    store.start()
-    store.wait()
+    stores = []
+    for n in range(0, rows, 2):
+        loads[n].wait()
+        loads[n + 1].wait()
+        for q in range(width // step):
+            at = pl.ds(q * step, step)
+            part = jnp.dot(held[n], factors[n, :, at], preferred_element_type=jnp.float32)
+            part += jnp.dot(held[n + 1], factors[n + 1, :, at], preferred_element_type=jnp.float32)
+            if n > 0:
+                part += total[:, at]
+            if n < rows - 2:
+                total[:, at] = part
+            else:
+                own_ref[:, at] = (part * -row_live).astype(jnp.bfloat16)
+                store = pltpu.make_async_copy(own_ref.at[:, at], out_ref.at[:, at], out_sems.at[q])
+                store.start()
+                stores.append(store)
+    for store in stores:
+        store.wait()
 
 
 def slot_row(me_row, n, rows):
@@ -71,12 +81,18 @@
     return lax.rem(base - 2 * (n % half) + rows, rows)
 
 
-def turn_kernel(rows, own_ref, other_ref, out_ref):
+def turn_kernel(rows, f_ref, out_ref, held, sems):
+    half = rows // 2
+    loads = [pltpu.make_async_copy(f_ref.at[n * half], held.at[n], sems.at[n]) for n in range(2)]
+    for load in loads:
+        load.start()
+    for load in loads:
+        load.wait()
     core = lax.rem(lax.axis_index("prow"), 2)
-    for y in range(rows // 2):
+    for y in range(half):
         at = pl.ds(pl.multiple_of((2 * y + core) * SLICE, SLICE), SLICE)
-        out_ref[pl.ds(y * SLICE, SLICE), 0:W] = own_ref[:, at].T
-        out_ref[pl.ds(y * SLICE, SLICE), W : 2 * W] = other_ref[:, at].T
+        for n in range(2):
+            out_ref[pl.ds(y * SLICE, SLICE), n * W : (n + 1) * W] = held[n, :, at].T
 
 
 def term_kernel(turned_ref, own_ref, other_ref, out_ref):
@@ -105,7 +121,6 @@
     chips = rows // 2
     width = factor_blocks.shape[-1]
     factor = factor_blocks[0, 0]
-    blocks = (anc_inverse.shape[0] // W) * (anc_inverse.shape[1] // W)
     lists = ancestors.T
 
     def shift(x, h):
@@ -114,6 +129,7 @@
     def swap(x):
         return lax.ppermute(x, "prow", [(i, i ^ 1) for i in range(rows)])
 
+    blocks = (anc_inverse.shape[0] // W) * (anc_inverse.shape[1] // W)
     sending = pl.pallas_call(
         functools.partial(pick_kernel, rows, cols),
         out_shape=jax.ShapeDtypeStruct((cols, W, W), jnp.bfloat16),
@@ -124,36 +140,39 @@
             pltpu.SemaphoreType.DMA((blocks,)),
             pltpu.SemaphoreType.DMA((cols,)),
         ],
-        compiler_params=pltpu.CompilerParams(vmem_limit_bytes=16 * MIB),
+        compiler_params=pltpu.CompilerParams(vmem_limit_bytes=60 * MIB),
         cost_estimate=pl.CostEstimate(flops=0, bytes_accessed=3 * MIB, transcendentals=0),
     )(lists, anc_inverse)
     arrived = lax.all_to_all(sending, "pcol", split_axis=0, concat_axis=0, tiled=True)
 
-    same = [factor] + [shift(factor, h if h <= chips // 2 else h - chips) for h in range(1, chips)]
-    factors = same + [swap(f) for f in same]
+    same = jnp.stack([factor] + [shift(factor, h if h <= chips // 2 else h - chips) for h in range(1, chips)])
+    factors = jnp.concatenate([same, swap(same)])
     turned = pl.pallas_call(
         functools.partial(turn_kernel, rows),
         out_shape=jax.ShapeDtypeStruct((chips * SLICE, 2 * W), jnp.bfloat16),
-        in_specs=[VMEM, VMEM],
+        in_specs=[HBM],
         out_specs=VMEM,
-        compiler_params=pltpu.CompilerParams(vmem_limit_bytes=16 * MIB),
+        scratch_shapes=[pltpu.VMEM((2, W, width), jnp.bfloat16), pltpu.SemaphoreType.DMA((2,))],
+        compiler_params=pltpu.CompilerParams(vmem_limit_bytes=50 * MIB),
         cost_estimate=pl.CostEstimate(flops=0, bytes_accessed=2 * MIB, transcendentals=0),
-    )(factors[0], factors[chips])
+    )(factors)
+    arrived, turned = lax.optimization_barrier((arrived, turned))
 
     product, own = pl.pallas_call(
         functools.partial(product_kernel, rows, cols),
         out_shape=(jax.ShapeDtypeStruct((W, width), jnp.bfloat16),) * 2,
-        in_specs=[SMEM, SMEM, VMEM] + [HBM] * rows,
+        in_specs=[SMEM, SMEM, VMEM, HBM],
         out_specs=(HBM, VMEM),
         scratch_shapes=[
             pltpu.VMEM((rows, W, W), jnp.bfloat16),
             pltpu.VMEM((rows, W, width), jnp.bfloat16),
+            pltpu.VMEM((W, width), jnp.float32),
             pltpu.SemaphoreType.DMA((rows,)),
-            pltpu.SemaphoreType.DMA,
+            pltpu.SemaphoreType.DMA((width // 256,)),
         ],
-        compiler_params=pltpu.CompilerParams(vmem_limit_bytes=32 * MIB),
+        compiler_params=pltpu.CompilerParams(vmem_limit_bytes=50 * MIB),
         cost_estimate=pl.CostEstimate(flops=2 * rows * W * W * width, bytes_accessed=7 * MIB, transcendentals=0),
-    )(lists, active_count, arrived, *factors)
+    )(lists, active_count, arrived, factors)
     terms = pl.pallas_call(
         term_kernel,
         out_shape=jax.ShapeDtypeStruct((chips, SLICE, width), jnp.bfloat16),

time: 151 us -> 144 us (0.954)
  waiting for transfers between devices: 64.2 us -> 75.1 us
  local copies, waits for them, and re-layouts: 13 us -> 2.28 us
  starting transfers between devices: 46.6 us -> 36.5 us
  Pallas kernels: 7.42 us -> 10.4 us
    unnamed x36 -> x14, local copies, waits for them, and re-layouts: 13 us -> 2.11 us
    ppermute x3, waiting for transfers between devices: 8.83 us -> 19 us  [shift(): lax.ppermute(x, 'prow', [(i, (i + 2 * h) % rows) for i in range(rows)])]
    ppermute x5 -> x2, starting transfers between devices: 20 us -> 10.1 us  [swap(): return lax.ppermute(x, 'prow', [(i, i ^ 1) for i in range(rows)])]
    ppermute x5 -> x2, waiting for transfers between devices: 1.3 us -> 5.08 us  [swap(): return lax.ppermute(x, 'prow', [(i, i ^ 1) for i in range(rows)])]
    all_to_all x1, waiting for transfers between devices: 54.1 us -> 51 us  [local(): lax.all_to_all(sending, 'pcol', split_axis=0, concat_axis=0, tiled=True)]
  transfers between devices with their start and end apart: 9 -> 6, of which waited for: 4 -> 6; matrix products, arithmetic and copies ran while one was open for 0% -> 0% of each run, Pallas kernels for 0% -> 1%
where the time goes in v3:
time: 144 us
  waiting for transfers between devices  75.1 us (52%)
  starting transfers between devices  36.5 us (25%)
  blocking collectives  18.2 us (13%)
  Pallas kernels  10.4 us (7%)
  local copies, waits for them, and re-layouts  2.28 us (2%)
    all_to_all x1, waiting for transfers between devices, local(): lax.all_to_all(sending, 'pcol', split_axis=0, concat_axis=0, tiled=True)  51 us
    ppermute x3, waiting for transfers between devices, shift(): lax.ppermute(x, 'prow', [(i, (i + 2 * h) % rows) for i in range(rows)])  19 us
    all_to_all x1, blocking collectives, local(): lax.all_to_all(terms, 'prow', split_axis=0, concat_axis=0, tiled=True, ax...  18.2 us
    all_to_all x1, starting transfers between devices, local(): lax.all_to_all(sending, 'pcol', split_axis=0, concat_axis=0, tiled=True)  15.7 us
    ppermute x3, starting transfers between devices, shift(): lax.ppermute(x, 'prow', [(i, (i + 2 * h) % rows) for i in range(rows)])  10.7 us
    ppermute x2, starting transfers between devices, swap(): return lax.ppermute(x, 'prow', [(i, i ^ 1) for i in range(rows)])  10.1 us
    ppermute x2, waiting for transfers between devices, swap(): return lax.ppermute(x, 'prow', [(i, i ^ 1) for i in range(rows)])  5.08 us
    pallas_call x1, Pallas kernels, local(): pl.pallas_call(functools.partial(product_kernel, rows, cols), out_shape=(...  4.03 us
  transfers between devices with their start and end apart: 6, of which 6 were waited for; matrix products, arithmetic and copies ran while one was open for 0% of the time, Pallas kernels for 1%

profile of v3, /device:TPU:1, one launch (start us, length us, event | category | flops | bytes accessed | tf_op | source)
XLA Modules:
  0.0 143.7 jit_solution(13860847720265422098)
XLA Ops:
  0.6 0.0 copy-start.4
  0.6 3.4 %shard_map.68 = bf16[16,256,256]{2,1,0:T(8,128)(2,1)} custom-call(s32[8,16]{1,0:T(8,128)} %bitcast.14, bf16[1024,512]{1,0:T(8,128)(2,1)} %a_ref.1), custom_call_target="tpu_custom_call" | custom-call | bytes 3145728 | tf_op jit(solution)/shard_map/pallas_call | solution.py:133
  4.0 15.7 %all-to-all-start = ((bf16[16,256,256]{2,1,0:T(8,128)(2,1)}), bf16[16,256,256]{2,1,0:T(8,128)(2,1)S(1)}, u32[]{:S(2)}, u32[]{:S(2)}) async-start(bf16[16,256,256]{2,1,0:T(8,128)(2,1)} %shard_map.68), calls=%async_computation | async-start | bytes 4194304 | tf_op jit(solution)/shard_map/all_to_all | solution.py:146
  19.7 0.0 copy-done.4
  19.8 3.2 %collective-permute-start = (bf16[256,1024]{1,0:T(8,128)(2,1)S(1)}, bf16[256,1024]{1,0:T(8,128)(2,1)S(1)}, u32[]{:S(2)}, u32[]{:S(2)}) collective-permute-start(bf16[256,1024]{1,0:T(8,128)(2,1)S(1)} %bitcast.16), channel_id=1, source_target_pairs={{0,32},{16,48},{32,64},{48,80},{64,96},{80,112},{96,0},{112,16},{1... | collective-permute-start | bytes 1572872 | tf_op jit(solution)/shard_map/ppermute | solution.py:127
  23.0 4.5 %collective-permute-start.1 = (bf16[256,1024]{1,0:T(8,128)(2,1)S(1)}, bf16[256,1024]{1,0:T(8,128)(2,1)S(1)}, u32[]{:S(2)}, u32[]{:S(2)}) collective-permute-start(bf16[256,1024]{1,0:T(8,128)(2,1)S(1)} %bitcast.17), channel_id=1, source_target_pairs={{0,64},{16,80},{32,96},{48,112},{64,0},{80,16},{96,32},{112,48},{1... | collective-permute-start | bytes 1572872 | tf_op jit(solution)/shard_map/ppermute | solution.py:127
  27.5 3.0 %collective-permute-start.2 = (bf16[256,1024]{1,0:T(8,128)(2,1)S(1)}, bf16[256,1024]{1,0:T(8,128)(2,1)S(1)}, u32[]{:S(2)}, u32[]{:S(2)}) collective-permute-start(bf16[256,1024]{1,0:T(8,128)(2,1)S(1)} %bitcast.18), channel_id=1, source_target_pairs={{0,96},{16,112},{32,0},{48,16},{64,32},{80,48},{96,64},{112,80},{1... | collective-permute-start | bytes 1572872 | tf_op jit(solution)/shard_map/ppermute | solution.py:127
  30.5 5.0 %collective-permute-done = bf16[256,1024]{1,0:T(8,128)(2,1)S(1)} collective-permute-done((bf16[256,1024]{1,0:T(8,128)(2,1)S(1)}, bf16[256,1024]{1,0:T(8,128)(2,1)S(1)}, u32[]{:S(2)}, u32[]{:S(2)}) %collective-permute-start) | collective-permute-done | bytes 524320 | tf_op jit(solution)/shard_map/ppermute | solution.py:127
  35.5 12.3 %collective-permute-done.1 = bf16[256,1024]{1,0:T(8,128)(2,1)S(1)} collective-permute-done((bf16[256,1024]{1,0:T(8,128)(2,1)S(1)}, bf16[256,1024]{1,0:T(8,128)(2,1)S(1)}, u32[]{:S(2)}, u32[]{:S(2)}) %collective-permute-start.1) | collective-permute-done | bytes 524320 | tf_op jit(solution)/shard_map/ppermute | solution.py:127
  47.8 1.7 %collective-permute-done.2 = bf16[256,1024]{1,0:T(8,128)(2,1)S(1)} collective-permute-done((bf16[256,1024]{1,0:T(8,128)(2,1)S(1)}, bf16[256,1024]{1,0:T(8,128)(2,1)S(1)}, u32[]{:S(2)}, u32[]{:S(2)}) %collective-permute-start.2) | collective-permute-done | bytes 524320 | tf_op jit(solution)/shard_map/ppermute | solution.py:127
  49.5 0.3 pad_maximum_fusion
  49.7 3.5 %collective-permute-start.3 = (bf16[4,256,1024]{2,1,0:T(8,128)(2,1)S(1)}, bf16[4,256,1024]{2,1,0:T(8,128)(2,1)S(1)}, u32[]{:S(2)}, u32[]{:S(2)}) collective-permute-start(bf16[4,256,1024]{2,1,0:T(8,128)(2,1)S(1)} %pad_maximum_fusion), channel_id=1, source_target_pairs={{0,16},{16,0},{32,48},{48,32},{64,80},{80,64},{96,112},{112,96},{1... | collective-permute-start | bytes 6291464 | tf_op jit(solution)/shard_map/ppermute | solution.py:130
  53.4 0.0 copy-start.1
  53.4 0.0 copy-start.2
  53.4 3.6 %collective-permute-done.3 = bf16[4,256,1024]{2,1,0:T(8,128)(2,1)S(1)} collective-permute-done((bf16[4,256,1024]{2,1,0:T(8,128)(2,1)S(1)}, bf16[4,256,1024]{2,1,0:T(8,128)(2,1)S(1)}, u32[]{:S(2)}, u32[]{:S(2)}) %collective-permute-start.3) | collective-permute-done | bytes 2097184 | tf_op jit(solution)/shard_map/ppermute | solution.py:130
  57.0 0.2 constant_dynamic-update-slice_fusion.f_ref
  57.2 0.0 copy-start.3
  57.2 1.9 %copy-done.3 = bf16[8,256,1024]{2,1,0:T(8,128)(2,1)} copy-done((bf16[8,256,1024]{2,1,0:T(8,128)(2,1)}, bf16[8,256,1024]{2,1,0:T(8,128)(2,1)S(1)}, u32[]{:S(2)}) %copy-start.3) | copy-done | bytes 4194328
  59.1 1.4 shard_map.69.turned_ref
  60.5 0.0 copy-start
  60.5 51.0 %all-to-all-done.a_ref = bf16[16,256,256]{2,1,0:T(8,128)(2,1)S(1)} async-done(((bf16[16,256,256]{2,1,0:T(8,128)(2,1)}), bf16[16,256,256]{2,1,0:T(8,128)(2,1)S(1)}, u32[]{:S(2)}, u32[]{:S(2)}) %all-to-all-start) | async-done | bytes 2097184 | tf_op jit(solution)/shard_map/all_to_all | solution.py:146
  111.6 0.0 copy-done.1
  111.6 0.0 copy-done.2
  111.6 4.0 %shard_map.70 = (bf16[256,1024]{1,0:T(8,128)(2,1)}, bf16[256,1024]{1,0:T(8,128)(2,1)S(1)}) custom-call(s32[8,16]{1,0:T(8,128)S(1)} %bitcast.15, s32[16]{0:T(128)S(1)} %copy-done.2, bf16[16,256,256]{2,1,0:T(8,128)(2,1)S(1)} %all-to-all-done.a_ref, bf16[8,256,1024]{2,1,0:T(8,128)(2,1)} %copy-done.3), custom_call_target="tpu_custom_call" | custom-call | flops 1073741824 | bytes 7340032 | tf_op jit(solution)/shard_map/pallas_call | solution.py:161
  115.6 6.6 %collective-permute-start.4 = (bf16[256,1024]{1,0:T(8,128)(2,1)S(1)}, bf16[256,1024]{1,0:T(8,128)(2,1)S(1)}, u32[]{:S(2)}, u32[]{:S(2)}) collective-permute-start(bf16[256,1024]{1,0:T(8,128)(2,1)S(1)} %get-tuple-element.9.own_ref), channel_id=1, source_target_pairs={{0,16},{16,0},{32,48},{48,32},{64,80},{80,64},{96,112},{112,96},{1... | collective-permute-start | bytes 1572872 | tf_op jit(solution)/shard_map/ppermute | solution.py:130
  122.3 1.5 %collective-permute-done.4.other_ref = bf16[256,1024]{1,0:T(8,128)(2,1)S(1)} collective-permute-done((bf16[256,1024]{1,0:T(8,128)(2,1)S(1)}, bf16[256,1024]{1,0:T(8,128)(2,1)S(1)}, u32[]{:S(2)}, u32[]{:S(2)}) %collective-permute-start.4) | collective-permute-done | bytes 524320 | tf_op jit(solution)/shard_map/ppermute | solution.py:130
  123.8 0.7 shard_map.71
  124.5 18.2 %all_to_all.10.terms_ref = bf16[4,128,1024]{2,1,0:T(8,128)(2,1)S(1)} all-to-all(bf16[4,128,1024]{2,1,0:T(8,128)(2,1)S(1)} %shard_map.71), channel_id=1, replica_groups={{0,32,64,96},{16,48,80,112},{1,33,65,97},{17,49,81,113},{2,34,66,98},{1..., dimensions={0} | all-to-all | bytes 2097152 | tf_op jit(solution)/shard_map/all_to_all | solution.py:185
  142.7 0.0 copy-done
  142.7 0.9 shard_map.72
  (4 shorter events, 0.1 us)
Async XLA Ops:
  0.6 19.1 %copy-start.4 = (bf16[1,1,256,1024]{3,2,1,0:T(8,128)(2,1)S(1)}, bf16[1,1,256,1024]{3,2,1,0:T(8,128)(2,1)}, u32[]{:S(2)}) copy-start(bf16[1,1,256,1024]{3,2,1,0:T(8,128)(2,1)} %param.6) | copy-start | bytes 1572868
  4.0 107.6 %all-to-all-start = ((bf16[16,256,256]{2,1,0:T(8,128)(2,1)}), bf16[16,256,256]{2,1,0:T(8,128)(2,1)S(1)}, u32[]{:S(2)}, u32[]{:S(2)}) async-start(bf16[16,256,256]{2,1,0:T(8,128)(2,1)} %shard_map.68), calls=%async_computation | async-start | bytes 4194304 | tf_op jit(solution)/shard_map/all_to_all | solution.py:146
  19.8 15.7 %collective-permute-start = (bf16[256,1024]{1,0:T(8,128)(2,1)S(1)}, bf16[256,1024]{1,0:T(8,128)(2,1)S(1)}, u32[]{:S(2)}, u32[]{:S(2)}) collective-permute-start(bf16[256,1024]{1,0:T(8,128)(2,1)S(1)} %bitcast.16), channel_id=1, source_target_pairs={{0,32},{16,48},{32,64},{48,80},{64,96},{80,112},{96,0},{112,16},{1... | collective-permute-start | bytes 1572872 | tf_op jit(solution)/shard_map/ppermute | solution.py:127
  23.0 24.8 %collective-permute-start.1 = (bf16[256,1024]{1,0:T(8,128)(2,1)S(1)}, bf16[256,1024]{1,0:T(8,128)(2,1)S(1)}, u32[]{:S(2)}, u32[]{:S(2)}) collective-permute-start(bf16[256,1024]{1,0:T(8,128)(2,1)S(1)} %bitcast.17), channel_id=1, source_target_pairs={{0,64},{16,80},{32,96},{48,112},{64,0},{80,16},{96,32},{112,48},{1... | collective-permute-start | bytes 1572872 | tf_op jit(solution)/shard_map/ppermute | solution.py:127
  27.5 22.0 %collective-permute-start.2 = (bf16[256,1024]{1,0:T(8,128)(2,1)S(1)}, bf16[256,1024]{1,0:T(8,128)(2,1)S(1)}, u32[]{:S(2)}, u32[]{:S(2)}) collective-permute-start(bf16[256,1024]{1,0:T(8,128)(2,1)S(1)} %bitcast.18), channel_id=1, source_target_pairs={{0,96},{16,112},{32,0},{48,16},{64,32},{80,48},{96,64},{112,80},{1... | collective-permute-start | bytes 1572872 | tf_op jit(solution)/shard_map/ppermute | solution.py:127
  49.7 7.2 %collective-permute-start.3 = (bf16[4,256,1024]{2,1,0:T(8,128)(2,1)S(1)}, bf16[4,256,1024]{2,1,0:T(8,128)(2,1)S(1)}, u32[]{:S(2)}, u32[]{:S(2)}) collective-permute-start(bf16[4,256,1024]{2,1,0:T(8,128)(2,1)S(1)} %pad_maximum_fusion), channel_id=1, source_target_pairs={{0,16},{16,0},{32,48},{48,32},{64,80},{80,64},{96,112},{112,96},{1... | collective-permute-start | bytes 6291464 | tf_op jit(solution)/shard_map/ppermute | solution.py:130
  53.4 58.2 %copy-start.1 = (s32[16,8]{0,1:T(8,128)S(1)}, s32[16,8]{0,1:T(8,128)}, u32[]{:S(2)}) copy-start(s32[16,8]{0,1:T(8,128)} %param.8) | copy-start | bytes 1540
  53.4 58.2 %copy-start.2 = (s32[16]{0:T(128)S(1)}, s32[16]{0:T(128)}, u32[]{:S(2)}) copy-start(s32[16]{0:T(128)} %count_ref.1) | copy-start | bytes 196
  57.2 2.0 %copy-start.3 = (bf16[8,256,1024]{2,1,0:T(8,128)(2,1)}, bf16[8,256,1024]{2,1,0:T(8,128)(2,1)S(1)}, u32[]{:S(2)}) copy-start(bf16[8,256,1024]{2,1,0:T(8,128)(2,1)S(1)} %constant_dynamic-update-slice_fusion.f_ref) | copy-start | bytes 12582916
  60.5 82.2 %copy-start = (f32[1,128,1024]{2,1,0:T(8,128)S(1)}, f32[1,128,1024]{2,1,0:T(8,128)}, u32[]{:S(2)}) copy-start(f32[1,128,1024]{2,1,0:T(8,128)} %param.7) | copy-start | bytes 1572868
  115.6 8.2 %collective-permute-start.4 = (bf16[256,1024]{1,0:T(8,128)(2,1)S(1)}, bf16[256,1024]{1,0:T(8,128)(2,1)S(1)}, u32[]{:S(2)}, u32[]{:S(2)}) collective-permute-start(bf16[256,1024]{1,0:T(8,128)(2,1)S(1)} %get-tuple-element.9.own_ref), channel_id=1, source_target_pairs={{0,16},{16,0},{32,48},{48,32},{64,80},{80,64},{96,112},{112,96},{1... | collective-permute-start | bytes 1572872 | tf_op jit(solution)/shard_map/ppermute | solution.py:130

commit v4 on v3

--- a/solution.py
+++ b/solution.py
@@ -12,29 +12,42 @@
 MIB = 1024 * 1024
 
 
-def pick_kernel(rows, cols, anc_ref, a_ref, out_ref, held, in_sems, out_sems):
+def pick_kernel(rows, cols, anc_ref, a_ref, out_ref, names, held, names_sem, in_sems, out_sems):
     high, wide = a_ref.shape[0] // W, a_ref.shape[1] // W
+    part = W // 2
+    fetch = pltpu.make_async_copy(anc_ref, names, names_sem)
+    fetch.start()
     loads = []
-    for n in range(high * wide):
-        i, j = n // wide, n % wide
-        load = pltpu.make_async_copy(a_ref.at[pl.ds(i * W, W), pl.ds(j * W, W)], held.at[n], in_sems.at[n])
-        load.start()
-        loads.append(load)
+    for p in range(2):
+        for n in range(high * wide):
+            i, j = n // wide, n % wide
+            load = pltpu.make_async_copy(
+                a_ref.at[pl.ds(i * W + p * part, part), pl.ds(j * W, W)],
+                held.at[n, pl.ds(p * part, part)],
+                in_sems.at[p, n],
+            )
+            load.start()
+            loads.append(load)
     me_row = lax.axis_index("prow")
     me_col = lax.axis_index("pcol")
     slot = lax.rem(me_col, rows)
+    fetch.wait()
+    owed, picks = [], []
+    for k in range(cols):
+        name = names[slot, k]
+        picks.append((names[me_row, k] // rows) * wide + name // cols)
+        owed.append(lax.rem(name, cols) == me_col)
     stores = []
-    for k in range(cols):
-        name = anc_ref[slot, k]
-        pick = (anc_ref[me_row, k] // rows) * wide + name // cols
-        store = pltpu.make_async_copy(held.at[pick], out_ref.at[k], out_sems.at[k])
-        stores.append((lax.rem(name, cols) == me_col, store))
-    for load in loads:
-        load.wait()
-    for owed, store in stores:
-        pl.when(owed)(store.start)
-    for owed, store in stores:
-        pl.when(owed)(store.wait)
+    for p in range(2):
+        for load in loads[p * high * wide : (p + 1) * high * wide]:
+            load.wait()
+        at = pl.ds(p * part, part)
+        for k in range(cols):
+            store = pltpu.make_async_copy(held.at[picks[k], at], out_ref.at[k, at], out_sems.at[p, k])
+            pl.when(owed[k])(store.start)
+            stores.append((owed[k], store))
+    for needed, store in stores:
+        pl.when(needed)(store.wait)
 
 
 def product_kernel(rows, cols, anc_ref, count_ref, a_ref, f_ref, out_ref, own_ref, held, factors, total, sems, out_sems):
@@ -56,8 +69,8 @@
         held[n] = a_ref[lax.rem(anc_ref[t, me_col], cols)] * live
     stores = []
     for n in range(0, rows, 2):
-        loads[n].wait()
-        loads[n + 1].wait()
+        for load in loads[n : n + 2]:
+            load.wait()
         for q in range(width // step):
             at = pl.ds(q * step, step)
             part = jnp.dot(held[n], factors[n, :, at], preferred_element_type=jnp.float32)
@@ -88,26 +101,27 @@
         load.start()
     for load in loads:
         load.wait()
-    core = lax.rem(lax.axis_index("prow"), 2)
-    for y in range(half):
-        at = pl.ds(pl.multiple_of((2 * y + core) * SLICE, SLICE), SLICE)
+    me = lax.axis_index("prow")
+    y, core = me // 2, lax.rem(me, 2)
+    for p, h in enumerate((2, 1, 3, 0)):
+        at = pl.ds(pl.multiple_of((2 * lax.rem(y + h, half) + core) * SLICE, SLICE), SLICE)
         for n in range(2):
-            out_ref[pl.ds(y * SLICE, SLICE), n * W : (n + 1) * W] = held[n, :, at].T
-
-
-def term_kernel(turned_ref, own_ref, other_ref, out_ref):
-    for y in range(out_ref.shape[0]):
-        at = pl.ds(y * SLICE, SLICE)
+            out_ref[pl.ds(p * SLICE, SLICE), n * W : (n + 1) * W] = held[n, :, at].T
+
+
+def term_kernel(base, turned_ref, own_ref, other_ref, *out_refs):
+    for n, ref in enumerate(out_refs):
+        at = pl.ds((base + n) * SLICE, SLICE)
         total = jnp.dot(turned_ref[at, 0:W], own_ref[...], preferred_element_type=jnp.float32)
         total += jnp.dot(turned_ref[at, W : 2 * W], other_ref[...], preferred_element_type=jnp.float32)
-        out_ref[y] = total.astype(jnp.bfloat16)
-
-
-def sum_kernel(diag_ref, terms_ref, out_ref):
-    total = terms_ref[0].astype(jnp.float32)
-    for y in range(1, terms_ref.shape[0]):
-        total += terms_ref[y].astype(jnp.float32)
-    out_ref[...] = diag_ref[...] - total
+        ref[...] = total.astype(ref.dtype)
+
+
+def sum_kernel(diag_ref, kept_ref, *refs):
+    total = kept_ref[...]
+    for ref in refs[:-1]:
+        total += ref[...].astype(jnp.float32)
+    refs[-1][...] = diag_ref[...] - total
 
 
 SMEM = pl.BlockSpec(memory_space=pltpu.SMEM)
@@ -133,12 +147,14 @@
     sending = pl.pallas_call(
         functools.partial(pick_kernel, rows, cols),
         out_shape=jax.ShapeDtypeStruct((cols, W, W), jnp.bfloat16),
-        in_specs=[SMEM, HBM],
+        in_specs=[HBM, HBM],
         out_specs=HBM,
         scratch_shapes=[
+            pltpu.SMEM((rows, cols), jnp.int32),
             pltpu.VMEM((blocks, W, W), jnp.bfloat16),
-            pltpu.SemaphoreType.DMA((blocks,)),
-            pltpu.SemaphoreType.DMA((cols,)),
+            pltpu.SemaphoreType.DMA,
+            pltpu.SemaphoreType.DMA((2, blocks)),
+            pltpu.SemaphoreType.DMA((2, cols)),
         ],
         compiler_params=pltpu.CompilerParams(vmem_limit_bytes=60 * MIB),
         cost_estimate=pl.CostEstimate(flops=0, bytes_accessed=3 * MIB, transcendentals=0),
@@ -173,24 +189,30 @@
         compiler_params=pltpu.CompilerParams(vmem_limit_bytes=50 * MIB),
         cost_estimate=pl.CostEstimate(flops=2 * rows * W * W * width, bytes_accessed=7 * MIB, transcendentals=0),
     )(lists, active_count, arrived, factors)
-    terms = pl.pallas_call(
-        term_kernel,
-        out_shape=jax.ShapeDtypeStruct((chips, SLICE, width), jnp.bfloat16),
-        in_specs=[VMEM] * 3,
-        out_specs=VMEM,
-        compiler_params=pltpu.CompilerParams(vmem_limit_bytes=16 * MIB),
-        cost_estimate=pl.CostEstimate(flops=4 * chips * SLICE * W * width, bytes_accessed=3 * MIB, transcendentals=0),
-    )(turned, own, swap(own))
-    groups = [list(range(core, rows, 2)) for core in range(2)]
-    met = lax.all_to_all(terms, "prow", split_axis=0, concat_axis=0, tiled=True, axis_index_groups=groups)
+    other = swap(own)
+
+    def terms(base, dtypes):
+        return pl.pallas_call(
+            functools.partial(term_kernel, base),
+            out_shape=[jax.ShapeDtypeStruct((SLICE, width), dtype) for dtype in dtypes],
+            in_specs=[VMEM] * 3,
+            out_specs=[VMEM] * len(dtypes),
+            compiler_params=pltpu.CompilerParams(vmem_limit_bytes=16 * MIB),
+            cost_estimate=pl.CostEstimate(flops=4 * len(dtypes) * SLICE * W * width, bytes_accessed=2 * MIB, transcendentals=0),
+        )(turned, own, other)
+
+    (far,) = terms(0, [jnp.bfloat16])
+    met = [shift(far, 2)]
+    near, back, kept = terms(1, [jnp.bfloat16, jnp.bfloat16, jnp.float32])
+    met += [shift(near, 1), shift(back, -1)]
     diagonal = pl.pallas_call(
         sum_kernel,
         out_shape=jax.ShapeDtypeStruct((SLICE, width), jnp.float32),
-        in_specs=[VMEM, VMEM],
+        in_specs=[VMEM] * (chips + 1),
         out_specs=VMEM,
         compiler_params=pltpu.CompilerParams(vmem_limit_bytes=16 * MIB),
         cost_estimate=pl.CostEstimate(flops=0, bytes_accessed=2 * MIB, transcendentals=0),
-    )(diag_in[0], met)
+    )(diag_in[0], kept, *met)
     return (product[None, None], diagonal[None])
 
 

time: 144 us -> 142 us (0.986)
  blocking collectives: 18.2 us -> 0 us
  starting transfers between devices: 36.5 us -> 47.7 us
  waiting for transfers between devices: 75.1 us -> 80.1 us
    all_to_all x1 -> x0, blocking collectives: 18.2 us -> none  [local(): lax.all_to_all(terms, 'prow', split_axis=0, concat_axis=0, tiled=True, ax...]
    ppermute x3 -> x6, starting transfers between devices: 10.7 us -> 22 us  [shift(): lax.ppermute(x, 'prow', [(i, (i + 2 * h) % rows) for i in range(rows)])]
    ppermute x3 -> x6, waiting for transfers between devices: 19 us -> 24 us  [shift(): lax.ppermute(x, 'prow', [(i, (i + 2 * h) % rows) for i in range(rows)])]
  transfers between devices with their start and end apart: 6 -> 9, of which waited for: 6 -> 7; matrix products, arithmetic and copies ran while one was open for 0% -> 0% of each run, Pallas kernels for 1% -> 1%
where the time goes in v4:
time: 142 us; the launch traced here: 141 us
  waiting for transfers between devices  80.1 us (56%)
  starting transfers between devices  47.7 us (34%)
  Pallas kernels  9.89 us (7%)
  local copies, waits for them, and re-layouts  2.3 us (2%)
    all_to_all x1, waiting for transfers between devices, local(): lax.all_to_all(sending, 'pcol', split_axis=0, concat_axis=0, tiled=True)  51 us
    ppermute x6, waiting for transfers between devices, shift(): lax.ppermute(x, 'prow', [(i, (i + 2 * h) % rows) for i in range(rows)])  24 us
    ppermute x6, starting transfers between devices, shift(): lax.ppermute(x, 'prow', [(i, (i + 2 * h) % rows) for i in range(rows)])  22 us
    all_to_all x1, starting transfers between devices, local(): lax.all_to_all(sending, 'pcol', split_axis=0, concat_axis=0, tiled=True)  15.6 us
    ppermute x2, starting transfers between devices, swap(): return lax.ppermute(x, 'prow', [(i, i ^ 1) for i in range(rows)])  10.1 us
    ppermute x2, waiting for transfers between devices, swap(): return lax.ppermute(x, 'prow', [(i, i ^ 1) for i in range(rows)])  5.08 us
    pallas_call x1, Pallas kernels, local(): pl.pallas_call(functools.partial(product_kernel, rows, cols), out_shape=(...  4.03 us
  transfers between devices with their start and end apart: 9, of which 7 were waited for; matrix products, arithmetic and copies ran while one was open for 0% of the time, Pallas kernels for 1%

profile of v4, /device:TPU:1, one launch (start us, length us, event | category | flops | bytes accessed | tf_op | source)
XLA Modules:
  0.0 141.1 jit_solution(11447418142423192813)
XLA Ops:
  0.6 0.0 copy-start.4
  0.6 2.6 %shard_map.68 = bf16[16,256,256]{2,1,0:T(8,128)(2,1)} custom-call(s32[8,16]{1,0:T(8,128)} %bitcast.14, bf16[1024,512]{1,0:T(8,128)(2,1)} %a_ref.1), custom_call_target="tpu_custom_call" | custom-call | bytes 3145728 | tf_op jit(solution)/shard_map/pallas_call | solution.py:147
  3.3 15.6 %all-to-all-start = ((bf16[16,256,256]{2,1,0:T(8,128)(2,1)}), bf16[16,256,256]{2,1,0:T(8,128)(2,1)S(1)}, u32[]{:S(2)}, u32[]{:S(2)}) async-start(bf16[16,256,256]{2,1,0:T(8,128)(2,1)} %shard_map.68), calls=%async_computation | async-start | bytes 4194304 | tf_op jit(solution)/shard_map/all_to_all | solution.py:162
  18.9 3.2 %collective-permute-start = (bf16[256,1024]{1,0:T(8,128)(2,1)S(1)}, bf16[256,1024]{1,0:T(8,128)(2,1)S(1)}, u32[]{:S(2)}, u32[]{:S(2)}) collective-permute-start(bf16[256,1024]{1,0:T(8,128)(2,1)S(1)} %bitcast.16), channel_id=1, source_target_pairs={{0,32},{16,48},{32,64},{48,80},{64,96},{80,112},{96,0},{112,16},{1... | collective-permute-start | bytes 1572872 | tf_op jit(solution)/shard_map/ppermute | solution.py:141
  22.1 4.5 %collective-permute-start.1 = (bf16[256,1024]{1,0:T(8,128)(2,1)S(1)}, bf16[256,1024]{1,0:T(8,128)(2,1)S(1)}, u32[]{:S(2)}, u32[]{:S(2)}) collective-permute-start(bf16[256,1024]{1,0:T(8,128)(2,1)S(1)} %bitcast.17), channel_id=1, source_target_pairs={{0,64},{16,80},{32,96},{48,112},{64,0},{80,16},{96,32},{112,48},{1... | collective-permute-start | bytes 1572872 | tf_op jit(solution)/shard_map/ppermute | solution.py:141
  26.7 3.0 %collective-permute-start.2 = (bf16[256,1024]{1,0:T(8,128)(2,1)S(1)}, bf16[256,1024]{1,0:T(8,128)(2,1)S(1)}, u32[]{:S(2)}, u32[]{:S(2)}) collective-permute-start(bf16[256,1024]{1,0:T(8,128)(2,1)S(1)} %bitcast.18), channel_id=1, source_target_pairs={{0,96},{16,112},{32,0},{48,16},{64,32},{80,48},{96,64},{112,80},{1... | collective-permute-start | bytes 1572872 | tf_op jit(solution)/shard_map/ppermute | solution.py:141
  29.7 5.0 %collective-permute-done = bf16[256,1024]{1,0:T(8,128)(2,1)S(1)} collective-permute-done((bf16[256,1024]{1,0:T(8,128)(2,1)S(1)}, bf16[256,1024]{1,0:T(8,128)(2,1)S(1)}, u32[]{:S(2)}, u32[]{:S(2)}) %collective-permute-start) | collective-permute-done | bytes 524320 | tf_op jit(solution)/shard_map/ppermute | solution.py:141
  34.7 12.3 %collective-permute-done.1 = bf16[256,1024]{1,0:T(8,128)(2,1)S(1)} collective-permute-done((bf16[256,1024]{1,0:T(8,128)(2,1)S(1)}, bf16[256,1024]{1,0:T(8,128)(2,1)S(1)}, u32[]{:S(2)}, u32[]{:S(2)}) %collective-permute-start.1) | collective-permute-done | bytes 524320 | tf_op jit(solution)/shard_map/ppermute | solution.py:141
  47.0 1.7 %collective-permute-done.2 = bf16[256,1024]{1,0:T(8,128)(2,1)S(1)} collective-permute-done((bf16[256,1024]{1,0:T(8,128)(2,1)S(1)}, bf16[256,1024]{1,0:T(8,128)(2,1)S(1)}, u32[]{:S(2)}, u32[]{:S(2)}) %collective-permute-start.2) | collective-permute-done | bytes 524320 | tf_op jit(solution)/shard_map/ppermute | solution.py:141
  48.7 0.3 pad_maximum_fusion
  48.9 3.5 %collective-permute-start.3 = (bf16[4,256,1024]{2,1,0:T(8,128)(2,1)S(1)}, bf16[4,256,1024]{2,1,0:T(8,128)(2,1)S(1)}, u32[]{:S(2)}, u32[]{:S(2)}) collective-permute-start(bf16[4,256,1024]{2,1,0:T(8,128)(2,1)S(1)} %pad_maximum_fusion), channel_id=1, source_target_pairs={{0,16},{16,0},{32,48},{48,32},{64,80},{80,64},{96,112},{112,96},{1... | collective-permute-start | bytes 6291464 | tf_op jit(solution)/shard_map/ppermute | solution.py:144
  52.6 0.0 copy-start.1
  52.6 0.0 copy-start.2
  52.6 3.6 %collective-permute-done.3 = bf16[4,256,1024]{2,1,0:T(8,128)(2,1)S(1)} collective-permute-done((bf16[4,256,1024]{2,1,0:T(8,128)(2,1)S(1)}, bf16[4,256,1024]{2,1,0:T(8,128)(2,1)S(1)}, u32[]{:S(2)}, u32[]{:S(2)}) %collective-permute-start.3) | collective-permute-done | bytes 2097184 | tf_op jit(solution)/shard_map/ppermute | solution.py:144
  56.2 0.2 constant_dynamic-update-slice_fusion.f_ref
  56.3 2.0 %copy-done.3 = bf16[8,256,1024]{2,1,0:T(8,128)(2,1)} copy-done((bf16[8,256,1024]{2,1,0:T(8,128)(2,1)}, bf16[8,256,1024]{2,1,0:T(8,128)(2,1)S(1)}, u32[]{:S(2)}) %copy-start.3) | copy-done | bytes 4194328
  58.3 1.4 shard_map.69.turned_ref
  59.7 0.0 copy-start
  59.7 51.0 %all-to-all-done.a_ref = bf16[16,256,256]{2,1,0:T(8,128)(2,1)S(1)} async-done(((bf16[16,256,256]{2,1,0:T(8,128)(2,1)}), bf16[16,256,256]{2,1,0:T(8,128)(2,1)S(1)}, u32[]{:S(2)}, u32[]{:S(2)}) %all-to-all-start) | async-done | bytes 2097184 | tf_op jit(solution)/shard_map/all_to_all | solution.py:162
  110.8 0.0 copy-done.1
  110.8 4.0 %shard_map.70 = (bf16[256,1024]{1,0:T(8,128)(2,1)}, bf16[256,1024]{1,0:T(8,128)(2,1)S(1)}) custom-call(s32[8,16]{1,0:T(8,128)S(1)} %bitcast.15, s32[16]{0:T(128)S(1)} %copy-done.2, bf16[16,256,256]{2,1,0:T(8,128)(2,1)S(1)} %all-to-all-done.a_ref, bf16[8,256,1024]{2,1,0:T(8,128)(2,1)} %copy-done.3), custom_call_target="tpu_custom_call" | custom-call | flops 1073741824 | bytes 7340032 | tf_op jit(solution)/shard_map/pallas_call | solution.py:177
  114.8 6.6 %collective-permute-start.4 = (bf16[256,1024]{1,0:T(8,128)(2,1)S(1)}, bf16[256,1024]{1,0:T(8,128)(2,1)S(1)}, u32[]{:S(2)}, u32[]{:S(2)}) collective-permute-start(bf16[256,1024]{1,0:T(8,128)(2,1)S(1)} %get-tuple-element.12.own_ref), channel_id=1, source_target_pairs={{0,16},{16,0},{32,48},{48,32},{64,80},{80,64},{96,112},{112,96},{1... | collective-permute-start | bytes 1572872 | tf_op jit(solution)/shard_map/ppermute | solution.py:144
  121.4 1.5 %collective-permute-done.4.other_ref = bf16[256,1024]{1,0:T(8,128)(2,1)S(1)} collective-permute-done((bf16[256,1024]{1,0:T(8,128)(2,1)S(1)}, bf16[256,1024]{1,0:T(8,128)(2,1)S(1)}, u32[]{:S(2)}, u32[]{:S(2)}) %collective-permute-start.4) | collective-permute-done | bytes 524320 | tf_op jit(solution)/shard_map/ppermute | solution.py:144
  123.0 0.3 shard_map.72
  123.3 4.8 %collective-permute-start.5 = (bf16[128,1024]{1,0:T(8,128)(2,1)S(1)}, bf16[128,1024]{1,0:T(8,128)(2,1)S(1)}, u32[]{:S(2)}, u32[]{:S(2)}) collective-permute-start(bf16[128,1024]{1,0:T(8,128)(2,1)S(1)} %shard_map.72), channel_id=1, source_target_pairs={{0,64},{16,80},{32,96},{48,112},{64,0},{80,16},{96,32},{112,48},{1... | collective-permute-start | bytes 786440 | tf_op jit(solution)/shard_map/ppermute | solution.py:141
  128.1 0.6 shard_map.71
  128.7 2.3 %collective-permute-start.6 = (bf16[128,1024]{1,0:T(8,128)(2,1)S(1)}, bf16[128,1024]{1,0:T(8,128)(2,1)S(1)}, u32[]{:S(2)}, u32[]{:S(2)}) collective-permute-start(bf16[128,1024]{1,0:T(8,128)(2,1)S(1)} %get-tuple-element.14), channel_id=1, source_target_pairs={{0,32},{16,48},{32,64},{48,80},{64,96},{80,112},{96,0},{112,16},{1... | collective-permute-start | bytes 786440 | tf_op jit(solution)/shard_map/ppermute | solution.py:141
  131.0 4.2 %collective-permute-start.7 = (bf16[128,1024]{1,0:T(8,128)(2,1)S(1)}, bf16[128,1024]{1,0:T(8,128)(2,1)S(1)}, u32[]{:S(2)}, u32[]{:S(2)}) collective-permute-start(bf16[128,1024]{1,0:T(8,128)(2,1)S(1)} %get-tuple-element.15), channel_id=1, source_target_pairs={{0,96},{16,112},{32,0},{48,16},{64,32},{80,48},{96,64},{112,80},{1... | collective-permute-start | bytes 786440 | tf_op jit(solution)/shard_map/ppermute | solution.py:141
  135.2 0.0 collective-permute-done.5.refs_0_
  135.2 5.0 %collective-permute-done.6.refs_1_ = bf16[128,1024]{1,0:T(8,128)(2,1)S(1)} collective-permute-done((bf16[128,1024]{1,0:T(8,128)(2,1)S(1)}, bf16[128,1024]{1,0:T(8,128)(2,1)S(1)}, u32[]{:S(2)}, u32[]{:S(2)}) %collective-permute-start.6) | collective-permute-done | bytes 262176 | tf_op jit(solution)/shard_map/ppermute | solution.py:141
  140.2 0.0 collective-permute-done.7.refs_2_
  140.2 0.9 shard_map.73
  (8 shorter events, 0.2 us)
Async XLA Ops:
  0.6 18.3 %copy-start.4 = (bf16[1,1,256,1024]{3,2,1,0:T(8,128)(2,1)S(1)}, bf16[1,1,256,1024]{3,2,1,0:T(8,128)(2,1)}, u32[]{:S(2)}) copy-start(bf16[1,1,256,1024]{3,2,1,0:T(8,128)(2,1)} %param.6) | copy-start | bytes 1572868
  3.3 107.5 %all-to-all-start = ((bf16[16,256,256]{2,1,0:T(8,128)(2,1)}), bf16[16,256,256]{2,1,0:T(8,128)(2,1)S(1)}, u32[]{:S(2)}, u32[]{:S(2)}) async-start(bf16[16,256,256]{2,1,0:T(8,128)(2,1)} %shard_map.68), calls=%async_computation | async-start | bytes 4194304 | tf_op jit(solution)/shard_map/all_to_all | solution.py:162
  18.9 15.7 %collective-permute-start = (bf16[256,1024]{1,0:T(8,128)(2,1)S(1)}, bf16[256,1024]{1,0:T(8,128)(2,1)S(1)}, u32[]{:S(2)}, u32[]{:S(2)}) collective-permute-start(bf16[256,1024]{1,0:T(8,128)(2,1)S(1)} %bitcast.16), channel_id=1, source_target_pairs={{0,32},{16,48},{32,64},{48,80},{64,96},{80,112},{96,0},{112,16},{1... | collective-permute-start | bytes 1572872 | tf_op jit(solution)/shard_map/ppermute | solution.py:141
  22.1 24.8 %collective-permute-start.1 = (bf16[256,1024]{1,0:T(8,128)(2,1)S(1)}, bf16[256,1024]{1,0:T(8,128)(2,1)S(1)}, u32[]{:S(2)}, u32[]{:S(2)}) collective-permute-start(bf16[256,1024]{1,0:T(8,128)(2,1)S(1)} %bitcast.17), channel_id=1, source_target_pairs={{0,64},{16,80},{32,96},{48,112},{64,0},{80,16},{96,32},{112,48},{1... | collective-permute-start | bytes 1572872 | tf_op jit(solution)/shard_map/ppermute | solution.py:141
  26.7 22.0 %collective-permute-start.2 = (bf16[256,1024]{1,0:T(8,128)(2,1)S(1)}, bf16[256,1024]{1,0:T(8,128)(2,1)S(1)}, u32[]{:S(2)}, u32[]{:S(2)}) collective-permute-start(bf16[256,1024]{1,0:T(8,128)(2,1)S(1)} %bitcast.18), channel_id=1, source_target_pairs={{0,96},{16,112},{32,0},{48,16},{64,32},{80,48},{96,64},{112,80},{1... | collective-permute-start | bytes 1572872 | tf_op jit(solution)/shard_map/ppermute | solution.py:141
  48.9 7.2 %collective-permute-start.3 = (bf16[4,256,1024]{2,1,0:T(8,128)(2,1)S(1)}, bf16[4,256,1024]{2,1,0:T(8,128)(2,1)S(1)}, u32[]{:S(2)}, u32[]{:S(2)}) collective-permute-start(bf16[4,256,1024]{2,1,0:T(8,128)(2,1)S(1)} %pad_maximum_fusion), channel_id=1, source_target_pairs={{0,16},{16,0},{32,48},{48,32},{64,80},{80,64},{96,112},{112,96},{1... | collective-permute-start | bytes 6291464 | tf_op jit(solution)/shard_map/ppermute | solution.py:144
  52.6 58.2 %copy-start.1 = (s32[16,8]{0,1:T(8,128)S(1)}, s32[16,8]{0,1:T(8,128)}, u32[]{:S(2)}) copy-start(s32[16,8]{0,1:T(8,128)} %param.8) | copy-start | bytes 1540
  52.6 58.2 %copy-start.2 = (s32[16]{0:T(128)S(1)}, s32[16]{0:T(128)}, u32[]{:S(2)}) copy-start(s32[16]{0:T(128)} %count_ref.1) | copy-start | bytes 196
  56.3 2.0 %copy-start.3 = (bf16[8,256,1024]{2,1,0:T(8,128)(2,1)}, bf16[8,256,1024]{2,1,0:T(8,128)(2,1)S(1)}, u32[]{:S(2)}) copy-start(bf16[8,256,1024]{2,1,0:T(8,128)(2,1)S(1)} %constant_dynamic-update-slice_fusion.f_ref) | copy-start | bytes 12582916
  59.7 80.5 %copy-start = (f32[1,128,1024]{2,1,0:T(8,128)S(1)}, f32[1,128,1024]{2,1,0:T(8,128)}, u32[]{:S(2)}) copy-start(f32[1,128,1024]{2,1,0:T(8,128)} %param.7) | copy-start | bytes 1572868
  114.8 8.2 %collective-permute-start.4 = (bf16[256,1024]{1,0:T(8,128)(2,1)S(1)}, bf16[256,1024]{1,0:T(8,128)(2,1)S(1)}, u32[]{:S(2)}, u32[]{:S(2)}) collective-permute-start(bf16[256,1024]{1,0:T(8,128)(2,1)S(1)} %get-tuple-element.12.own_ref), channel_id=1, source_target_pairs={{0,16},{16,0},{32,48},{48,32},{64,80},{80,64},{96,112},{112,96},{1... | collective-permute-start | bytes 1572872 | tf_op jit(solution)/shard_map/ppermute | solution.py:144
  123.3 11.9 %collective-permute-start.5 = (bf16[128,1024]{1,0:T(8,128)(2,1)S(1)}, bf16[128,1024]{1,0:T(8,128)(2,1)S(1)}, u32[]{:S(2)}, u32[]{:S(2)}) collective-permute-start(bf16[128,1024]{1,0:T(8,128)(2,1)S(1)} %shard_map.72), channel_id=1, source_target_pairs={{0,64},{16,80},{32,96},{48,112},{64,0},{80,16},{96,32},{112,48},{1... | collective-permute-start | bytes 786440 | tf_op jit(solution)/shard_map/ppermute | solution.py:141
  128.7 11.5 %collective-permute-start.6 = (bf16[128,1024]{1,0:T(8,128)(2,1)S(1)}, bf16[128,1024]{1,0:T(8,128)(2,1)S(1)}, u32[]{:S(2)}, u32[]{:S(2)}) collective-permute-start(bf16[128,1024]{1,0:T(8,128)(2,1)S(1)} %get-tuple-element.14), channel_id=1, source_target_pairs={{0,32},{16,48},{32,64},{48,80},{64,96},{80,112},{96,0},{112,16},{1... | collective-permute-start | bytes 786440 | tf_op jit(solution)/shard_map/ppermute | solution.py:141
  131.0 9.2 %collective-permute-start.7 = (bf16[128,1024]{1,0:T(8,128)(2,1)S(1)}, bf16[128,1024]{1,0:T(8,128)(2,1)S(1)}, u32[]{:S(2)}, u32[]{:S(2)}) collective-permute-start(bf16[128,1024]{1,0:T(8,128)(2,1)S(1)} %get-tuple-element.15), channel_id=1, source_target_pairs={{0,96},{16,112},{32,0},{48,16},{64,32},{80,48},{96,64},{112,80},{1... | collective-permute-start | bytes 786440 | tf_op jit(solution)/shard_map/ppermute | solution.py:141

commit v5 on v4

--- a/solution.py
+++ b/solution.py
@@ -50,7 +50,7 @@
         pl.when(needed)(store.wait)
 
 
-def product_kernel(rows, cols, anc_ref, count_ref, a_ref, f_ref, out_ref, own_ref, held, factors, total, sems, out_sems):
+def product_kernel(rows, cols, anc_ref, count_ref, a_ref, f_ref, own_ref, held, factors, total, sems):
     half = rows // 2
     width = own_ref.shape[-1]
     step = 256
@@ -67,7 +67,6 @@
         t = slot_row(me_row, n, rows)
         live = (t < count).astype(jnp.bfloat16)
         held[n] = a_ref[lax.rem(anc_ref[t, me_col], cols)] * live
-    stores = []
     for n in range(0, rows, 2):
         for load in loads[n : n + 2]:
             load.wait()
@@ -81,11 +80,6 @@
                 total[:, at] = part
             else:
                 own_ref[:, at] = (part * -row_live).astype(jnp.bfloat16)
-                store = pltpu.make_async_copy(own_ref.at[:, at], out_ref.at[:, at], out_sems.at[q])
-                store.start()
-                stores.append(store)
-    for store in stores:
-        store.wait()
 
 
 def slot_row(me_row, n, rows):
@@ -115,6 +109,12 @@
         total = jnp.dot(turned_ref[at, 0:W], own_ref[...], preferred_element_type=jnp.float32)
         total += jnp.dot(turned_ref[at, W : 2 * W], other_ref[...], preferred_element_type=jnp.float32)
         ref[...] = total.astype(ref.dtype)
+
+
+def store_kernel(own_ref, out_ref, sem):
+    store = pltpu.make_async_copy(own_ref, out_ref, sem)
+    store.start()
+    store.wait()
 
 
 def sum_kernel(diag_ref, kept_ref, *refs):
@@ -174,17 +174,16 @@
     )(factors)
     arrived, turned = lax.optimization_barrier((arrived, turned))
 
-    product, own = pl.pallas_call(
+    own = pl.pallas_call(
         functools.partial(product_kernel, rows, cols),
-        out_shape=(jax.ShapeDtypeStruct((W, width), jnp.bfloat16),) * 2,
+        out_shape=jax.ShapeDtypeStruct((W, width), jnp.bfloat16),
         in_specs=[SMEM, SMEM, VMEM, HBM],
-        out_specs=(HBM, VMEM),
+        out_specs=VMEM,
         scratch_shapes=[
             pltpu.VMEM((rows, W, W), jnp.bfloat16),
             pltpu.VMEM((rows, W, width), jnp.bfloat16),
             pltpu.VMEM((W, width), jnp.float32),
             pltpu.SemaphoreType.DMA((rows,)),
-            pltpu.SemaphoreType.DMA((width // 256,)),
         ],
         compiler_params=pltpu.CompilerParams(vmem_limit_bytes=50 * MIB),
         cost_estimate=pl.CostEstimate(flops=2 * rows * W * W * width, bytes_accessed=7 * MIB, transcendentals=0),
@@ -205,6 +204,15 @@
     met = [shift(far, 2)]
     near, back, kept = terms(1, [jnp.bfloat16, jnp.bfloat16, jnp.float32])
     met += [shift(near, 1), shift(back, -1)]
+    product = pl.pallas_call(
+        store_kernel,
+        out_shape=jax.ShapeDtypeStruct((W, width), jnp.bfloat16),
+        in_specs=[VMEM],
+        out_specs=HBM,
+        scratch_shapes=[pltpu.SemaphoreType.DMA],
+        compiler_params=pltpu.CompilerParams(vmem_limit_bytes=16 * MIB),
+        cost_estimate=pl.CostEstimate(flops=0, bytes_accessed=MIB, transcendentals=0),
+    )(own)
     diagonal = pl.pallas_call(
         sum_kernel,
         out_shape=jax.ShapeDtypeStruct((SLICE, width), jnp.float32),

time: 142 us -> 142 us (level)
    pallas_call x1 -> x2, Pallas kernels: 4.03 us -> 4.1 us  [the longest x1 3.3 us: local(): pl.pallas_call(functools.partial(product_kernel, rows, cols), out_shape=j...]
  transfers between devices with their start and end apart: 9 -> 9, of which waited for: 7 -> 7; matrix products, arithmetic and copies ran while one was open for 0% -> 0% of each run, Pallas kernels for 1% -> 2%
where the time goes in v5:
time: 142 us; the launch traced here: 140 us
  waiting for transfers between devices  79.3 us (56%)
  starting transfers between devices  48 us (34%)
  Pallas kernels  9.82 us (7%)
  local copies, waits for them, and re-layouts  2.29 us (2%)
    all_to_all x1, waiting for transfers between devices, local(): lax.all_to_all(sending, 'pcol', split_axis=0, concat_axis=0, tiled=True)  51 us
    ppermute x6, waiting for transfers between devices, shift(): lax.ppermute(x, 'prow', [(i, (i + 2 * h) % rows) for i in range(rows)])  23.2 us
    ppermute x6, starting transfers between devices, shift(): lax.ppermute(x, 'prow', [(i, (i + 2 * h) % rows) for i in range(rows)])  22 us
    all_to_all x1, starting transfers between devices, local(): lax.all_to_all(sending, 'pcol', split_axis=0, concat_axis=0, tiled=True)  15.8 us
    ppermute x2, starting transfers between devices, swap(): return lax.ppermute(x, 'prow', [(i, i ^ 1) for i in range(rows)])  10.1 us
    ppermute x2, waiting for transfers between devices, swap(): return lax.ppermute(x, 'prow', [(i, i ^ 1) for i in range(rows)])  5.08 us
    pallas_call x1, Pallas kernels, local(): pl.pallas_call(functools.partial(product_kernel, rows, cols), out_shape=j...  3.3 us
  transfers between devices with their start and end apart: 9, of which 7 were waited for; matrix products, arithmetic and copies ran while one was open for 0% of the time, Pallas kernels for 2%

profile of v5, /device:TPU:1, one launch (start us, length us, event | category | flops | bytes accessed | tf_op | source)
XLA Modules:
  0.0 140.5 jit_solution(6220471563361273881)
XLA Ops:
  0.6 0.0 copy-start.4
  0.6 2.5 %shard_map.68 = bf16[16,256,256]{2,1,0:T(8,128)(2,1)} custom-call(s32[8,16]{1,0:T(8,128)} %bitcast.14, bf16[1024,512]{1,0:T(8,128)(2,1)} %a_ref.1), custom_call_target="tpu_custom_call" | custom-call | bytes 3145728 | tf_op jit(solution)/shard_map/pallas_call | solution.py:147
  3.2 15.8 %all-to-all-start = ((bf16[16,256,256]{2,1,0:T(8,128)(2,1)}), bf16[16,256,256]{2,1,0:T(8,128)(2,1)S(1)}, u32[]{:S(2)}, u32[]{:S(2)}) async-start(bf16[16,256,256]{2,1,0:T(8,128)(2,1)} %shard_map.68), calls=%async_computation | async-start | bytes 4194304 | tf_op jit(solution)/shard_map/all_to_all | solution.py:162
  19.0 3.2 %collective-permute-start = (bf16[256,1024]{1,0:T(8,128)(2,1)S(1)}, bf16[256,1024]{1,0:T(8,128)(2,1)S(1)}, u32[]{:S(2)}, u32[]{:S(2)}) collective-permute-start(bf16[256,1024]{1,0:T(8,128)(2,1)S(1)} %bitcast.16), channel_id=1, source_target_pairs={{0,32},{16,48},{32,64},{48,80},{64,96},{80,112},{96,0},{112,16},{1... | collective-permute-start | bytes 1572872 | tf_op jit(solution)/shard_map/ppermute | solution.py:141
  22.2 4.5 %collective-permute-start.1 = (bf16[256,1024]{1,0:T(8,128)(2,1)S(1)}, bf16[256,1024]{1,0:T(8,128)(2,1)S(1)}, u32[]{:S(2)}, u32[]{:S(2)}) collective-permute-start(bf16[256,1024]{1,0:T(8,128)(2,1)S(1)} %bitcast.17), channel_id=1, source_target_pairs={{0,64},{16,80},{32,96},{48,112},{64,0},{80,16},{96,32},{112,48},{1... | collective-permute-start | bytes 1572872 | tf_op jit(solution)/shard_map/ppermute | solution.py:141
  26.8 3.0 %collective-permute-start.2 = (bf16[256,1024]{1,0:T(8,128)(2,1)S(1)}, bf16[256,1024]{1,0:T(8,128)(2,1)S(1)}, u32[]{:S(2)}, u32[]{:S(2)}) collective-permute-start(bf16[256,1024]{1,0:T(8,128)(2,1)S(1)} %bitcast.18), channel_id=1, source_target_pairs={{0,96},{16,112},{32,0},{48,16},{64,32},{80,48},{96,64},{112,80},{1... | collective-permute-start | bytes 1572872 | tf_op jit(solution)/shard_map/ppermute | solution.py:141
  29.7 5.0 %collective-permute-done = bf16[256,1024]{1,0:T(8,128)(2,1)S(1)} collective-permute-done((bf16[256,1024]{1,0:T(8,128)(2,1)S(1)}, bf16[256,1024]{1,0:T(8,128)(2,1)S(1)}, u32[]{:S(2)}, u32[]{:S(2)}) %collective-permute-start) | collective-permute-done | bytes 524320 | tf_op jit(solution)/shard_map/ppermute | solution.py:141
  34.7 12.3 %collective-permute-done.1 = bf16[256,1024]{1,0:T(8,128)(2,1)S(1)} collective-permute-done((bf16[256,1024]{1,0:T(8,128)(2,1)S(1)}, bf16[256,1024]{1,0:T(8,128)(2,1)S(1)}, u32[]{:S(2)}, u32[]{:S(2)}) %collective-permute-start.1) | collective-permute-done | bytes 524320 | tf_op jit(solution)/shard_map/ppermute | solution.py:141
  47.1 1.7 %collective-permute-done.2 = bf16[256,1024]{1,0:T(8,128)(2,1)S(1)} collective-permute-done((bf16[256,1024]{1,0:T(8,128)(2,1)S(1)}, bf16[256,1024]{1,0:T(8,128)(2,1)S(1)}, u32[]{:S(2)}, u32[]{:S(2)}) %collective-permute-start.2) | collective-permute-done | bytes 524320 | tf_op jit(solution)/shard_map/ppermute | solution.py:141
  48.7 0.3 pad_maximum_fusion
  49.0 3.5 %collective-permute-start.3 = (bf16[4,256,1024]{2,1,0:T(8,128)(2,1)S(1)}, bf16[4,256,1024]{2,1,0:T(8,128)(2,1)S(1)}, u32[]{:S(2)}, u32[]{:S(2)}) collective-permute-start(bf16[4,256,1024]{2,1,0:T(8,128)(2,1)S(1)} %pad_maximum_fusion), channel_id=1, source_target_pairs={{0,16},{16,0},{32,48},{48,32},{64,80},{80,64},{96,112},{112,96},{1... | collective-permute-start | bytes 6291464 | tf_op jit(solution)/shard_map/ppermute | solution.py:144
  52.6 0.0 copy-start.1
  52.7 0.0 copy-start.2
  52.7 3.6 %collective-permute-done.3 = bf16[4,256,1024]{2,1,0:T(8,128)(2,1)S(1)} collective-permute-done((bf16[4,256,1024]{2,1,0:T(8,128)(2,1)S(1)}, bf16[4,256,1024]{2,1,0:T(8,128)(2,1)S(1)}, u32[]{:S(2)}, u32[]{:S(2)}) %collective-permute-start.3) | collective-permute-done | bytes 2097184 | tf_op jit(solution)/shard_map/ppermute | solution.py:144
  56.2 0.2 constant_dynamic-update-slice_fusion.f_ref
  56.4 1.9 %copy-done.3 = bf16[8,256,1024]{2,1,0:T(8,128)(2,1)} copy-done((bf16[8,256,1024]{2,1,0:T(8,128)(2,1)}, bf16[8,256,1024]{2,1,0:T(8,128)(2,1)S(1)}, u32[]{:S(2)}) %copy-start.3) | copy-done | bytes 4194328
  58.4 1.4 %shard_map.69.turned_ref = bf16[512,512]{1,0:T(8,128)(2,1)S(1)} custom-call(bf16[8,256,1024]{2,1,0:T(8,128)(2,1)} %copy-done.3), custom_call_target="tpu_custom_call" | custom-call | bytes 2097152 | tf_op jit(solution)/shard_map/pallas_call | solution.py:166
  59.8 0.0 copy-start
  59.8 51.0 %all-to-all-done.a_ref = bf16[16,256,256]{2,1,0:T(8,128)(2,1)S(1)} async-done(((bf16[16,256,256]{2,1,0:T(8,128)(2,1)}), bf16[16,256,256]{2,1,0:T(8,128)(2,1)S(1)}, u32[]{:S(2)}, u32[]{:S(2)}) %all-to-all-start) | async-done | bytes 2097184 | tf_op jit(solution)/shard_map/all_to_all | solution.py:162
  110.8 3.3 %shard_map.70.own_ref = bf16[256,1024]{1,0:T(8,128)(2,1)S(1)} custom-call(s32[8,16]{1,0:T(8,128)S(1)} %bitcast.15, s32[16]{0:T(128)S(1)} %copy-done.2, bf16[16,256,256]{2,1,0:T(8,128)(2,1)S(1)} %all-to-all-done.a_ref, bf16[8,256,1024]{2,1,0:T(8,128)(2,1)} %copy-done.3), custom_call_target="tpu_custom_call" | custom-call | flops 1073741824 | bytes 7340032 | tf_op jit(solution)/shard_map/pallas_call | solution.py:177
  114.1 6.6 %collective-permute-start.4 = (bf16[256,1024]{1,0:T(8,128)(2,1)S(1)}, bf16[256,1024]{1,0:T(8,128)(2,1)S(1)}, u32[]{:S(2)}, u32[]{:S(2)}) collective-permute-start(bf16[256,1024]{1,0:T(8,128)(2,1)S(1)} %shard_map.70.own_ref), channel_id=1, source_target_pairs={{0,16},{16,0},{32,48},{48,32},{64,80},{80,64},{96,112},{112,96},{1... | collective-permute-start | bytes 1572872 | tf_op jit(solution)/shard_map/ppermute | solution.py:144
  120.8 1.5 %collective-permute-done.4.other_ref = bf16[256,1024]{1,0:T(8,128)(2,1)S(1)} collective-permute-done((bf16[256,1024]{1,0:T(8,128)(2,1)S(1)}, bf16[256,1024]{1,0:T(8,128)(2,1)S(1)}, u32[]{:S(2)}, u32[]{:S(2)}) %collective-permute-start.4) | collective-permute-done | bytes 524320 | tf_op jit(solution)/shard_map/ppermute | solution.py:144
  122.3 0.3 shard_map.73
  122.6 4.8 %collective-permute-start.5 = (bf16[128,1024]{1,0:T(8,128)(2,1)S(1)}, bf16[128,1024]{1,0:T(8,128)(2,1)S(1)}, u32[]{:S(2)}, u32[]{:S(2)}) collective-permute-start(bf16[128,1024]{1,0:T(8,128)(2,1)S(1)} %shard_map.73), channel_id=1, source_target_pairs={{0,64},{16,80},{32,96},{48,112},{64,0},{80,16},{96,32},{112,48},{1... | collective-permute-start | bytes 786440 | tf_op jit(solution)/shard_map/ppermute | solution.py:141
  127.4 0.6 shard_map.72
  128.0 2.3 %collective-permute-start.6 = (bf16[128,1024]{1,0:T(8,128)(2,1)S(1)}, bf16[128,1024]{1,0:T(8,128)(2,1)S(1)}, u32[]{:S(2)}, u32[]{:S(2)}) collective-permute-start(bf16[128,1024]{1,0:T(8,128)(2,1)S(1)} %get-tuple-element.10), channel_id=1, source_target_pairs={{0,32},{16,48},{32,64},{48,80},{64,96},{80,112},{96,0},{112,16},{1... | collective-permute-start | bytes 786440 | tf_op jit(solution)/shard_map/ppermute | solution.py:141
  130.3 4.2 %collective-permute-start.7 = (bf16[128,1024]{1,0:T(8,128)(2,1)S(1)}, bf16[128,1024]{1,0:T(8,128)(2,1)S(1)}, u32[]{:S(2)}, u32[]{:S(2)}) collective-permute-start(bf16[128,1024]{1,0:T(8,128)(2,1)S(1)} %get-tuple-element.11), channel_id=1, source_target_pairs={{0,96},{16,112},{32,0},{48,16},{64,32},{80,48},{96,64},{112,80},{1... | collective-permute-start | bytes 786440 | tf_op jit(solution)/shard_map/ppermute | solution.py:141
  134.5 0.8 shard_map.71
  135.4 0.0 collective-permute-done.5.refs_0_
  135.4 4.2 %collective-permute-done.6.refs_1_ = bf16[128,1024]{1,0:T(8,128)(2,1)S(1)} collective-permute-done((bf16[128,1024]{1,0:T(8,128)(2,1)S(1)}, bf16[128,1024]{1,0:T(8,128)(2,1)S(1)}, u32[]{:S(2)}, u32[]{:S(2)}) %collective-permute-start.6) | collective-permute-done | bytes 262176 | tf_op jit(solution)/shard_map/ppermute | solution.py:141
  139.5 0.0 collective-permute-done.7.refs_2_
  139.5 0.9 shard_map.74
  (9 shorter events, 0.2 us)
Async XLA Ops:
  0.6 18.4 %copy-start.4 = (bf16[1,1,256,1024]{3,2,1,0:T(8,128)(2,1)S(1)}, bf16[1,1,256,1024]{3,2,1,0:T(8,128)(2,1)}, u32[]{:S(2)}) copy-start(bf16[1,1,256,1024]{3,2,1,0:T(8,128)(2,1)} %param.6) | copy-start | bytes 1572868
  3.2 107.7 %all-to-all-start = ((bf16[16,256,256]{2,1,0:T(8,128)(2,1)}), bf16[16,256,256]{2,1,0:T(8,128)(2,1)S(1)}, u32[]{:S(2)}, u32[]{:S(2)}) async-start(bf16[16,256,256]{2,1,0:T(8,128)(2,1)} %shard_map.68), calls=%async_computation | async-start | bytes 4194304 | tf_op jit(solution)/shard_map/all_to_all | solution.py:162
  19.0 15.7 %collective-permute-start = (bf16[256,1024]{1,0:T(8,128)(2,1)S(1)}, bf16[256,1024]{1,0:T(8,128)(2,1)S(1)}, u32[]{:S(2)}, u32[]{:S(2)}) collective-permute-start(bf16[256,1024]{1,0:T(8,128)(2,1)S(1)} %bitcast.16), channel_id=1, source_target_pairs={{0,32},{16,48},{32,64},{48,80},{64,96},{80,112},{96,0},{112,16},{1... | collective-permute-start | bytes 1572872 | tf_op jit(solution)/shard_map/ppermute | solution.py:141
  22.2 24.8 %collective-permute-start.1 = (bf16[256,1024]{1,0:T(8,128)(2,1)S(1)}, bf16[256,1024]{1,0:T(8,128)(2,1)S(1)}, u32[]{:S(2)}, u32[]{:S(2)}) collective-permute-start(bf16[256,1024]{1,0:T(8,128)(2,1)S(1)} %bitcast.17), channel_id=1, source_target_pairs={{0,64},{16,80},{32,96},{48,112},{64,0},{80,16},{96,32},{112,48},{1... | collective-permute-start | bytes 1572872 | tf_op jit(solution)/shard_map/ppermute | solution.py:141
  26.8 22.0 %collective-permute-start.2 = (bf16[256,1024]{1,0:T(8,128)(2,1)S(1)}, bf16[256,1024]{1,0:T(8,128)(2,1)S(1)}, u32[]{:S(2)}, u32[]{:S(2)}) collective-permute-start(bf16[256,1024]{1,0:T(8,128)(2,1)S(1)} %bitcast.18), channel_id=1, source_target_pairs={{0,96},{16,112},{32,0},{48,16},{64,32},{80,48},{96,64},{112,80},{1... | collective-permute-start | bytes 1572872 | tf_op jit(solution)/shard_map/ppermute | solution.py:141
  49.0 7.2 %collective-permute-start.3 = (bf16[4,256,1024]{2,1,0:T(8,128)(2,1)S(1)}, bf16[4,256,1024]{2,1,0:T(8,128)(2,1)S(1)}, u32[]{:S(2)}, u32[]{:S(2)}) collective-permute-start(bf16[4,256,1024]{2,1,0:T(8,128)(2,1)S(1)} %pad_maximum_fusion), channel_id=1, source_target_pairs={{0,16},{16,0},{32,48},{48,32},{64,80},{80,64},{96,112},{112,96},{1... | collective-permute-start | bytes 6291464 | tf_op jit(solution)/shard_map/ppermute | solution.py:144
  52.6 58.2 %copy-start.1 = (s32[16,8]{0,1:T(8,128)S(1)}, s32[16,8]{0,1:T(8,128)}, u32[]{:S(2)}) copy-start(s32[16,8]{0,1:T(8,128)} %param.8) | copy-start | bytes 1540
  52.7 58.2 %copy-start.2 = (s32[16]{0:T(128)S(1)}, s32[16]{0:T(128)}, u32[]{:S(2)}) copy-start(s32[16]{0:T(128)} %count_ref.1) | copy-start | bytes 196
  56.4 2.0 %copy-start.3 = (bf16[8,256,1024]{2,1,0:T(8,128)(2,1)}, bf16[8,256,1024]{2,1,0:T(8,128)(2,1)S(1)}, u32[]{:S(2)}) copy-start(bf16[8,256,1024]{2,1,0:T(8,128)(2,1)S(1)} %constant_dynamic-update-slice_fusion.f_ref) | copy-start | bytes 12582916
  59.8 79.8 %copy-start = (f32[1,128,1024]{2,1,0:T(8,128)S(1)}, f32[1,128,1024]{2,1,0:T(8,128)}, u32[]{:S(2)}) copy-start(f32[1,128,1024]{2,1,0:T(8,128)} %param.7) | copy-start | bytes 1572868
  114.1 8.2 %collective-permute-start.4 = (bf16[256,1024]{1,0:T(8,128)(2,1)S(1)}, bf16[256,1024]{1,0:T(8,128)(2,1)S(1)}, u32[]{:S(2)}, u32[]{:S(2)}) collective-permute-start(bf16[256,1024]{1,0:T(8,128)(2,1)S(1)} %shard_map.70.own_ref), channel_id=1, source_target_pairs={{0,16},{16,0},{32,48},{48,32},{64,80},{80,64},{96,112},{112,96},{1... | collective-permute-start | bytes 1572872 | tf_op jit(solution)/shard_map/ppermute | solution.py:144
  122.6 12.7 %collective-permute-start.5 = (bf16[128,1024]{1,0:T(8,128)(2,1)S(1)}, bf16[128,1024]{1,0:T(8,128)(2,1)S(1)}, u32[]{:S(2)}, u32[]{:S(2)}) collective-permute-start(bf16[128,1024]{1,0:T(8,128)(2,1)S(1)} %shard_map.73), channel_id=1, source_target_pairs={{0,64},{16,80},{32,96},{48,112},{64,0},{80,16},{96,32},{112,48},{1... | collective-permute-start | bytes 786440 | tf_op jit(solution)/shard_map/ppermute | solution.py:141
  128.0 11.5 %collective-permute-start.6 = (bf16[128,1024]{1,0:T(8,128)(2,1)S(1)}, bf16[128,1024]{1,0:T(8,128)(2,1)S(1)}, u32[]{:S(2)}, u32[]{:S(2)}) collective-permute-start(bf16[128,1024]{1,0:T(8,128)(2,1)S(1)} %get-tuple-element.10), channel_id=1, source_target_pairs={{0,32},{16,48},{32,64},{48,80},{64,96},{80,112},{96,0},{112,16},{1... | collective-permute-start | bytes 786440 | tf_op jit(solution)/shard_map/ppermute | solution.py:141
  130.3 9.2 %collective-permute-start.7 = (bf16[128,1024]{1,0:T(8,128)(2,1)S(1)}, bf16[128,1024]{1,0:T(8,128)(2,1)S(1)}, u32[]{:S(2)}, u32[]{:S(2)}) collective-permute-start(bf16[128,1024]{1,0:T(8,128)(2,1)S(1)} %get-tuple-element.11), channel_id=1, source_target_pairs={{0,96},{16,112},{32,0},{48,16},{64,32},{80,48},{96,64},{112,80},{1... | collective-permute-start | bytes 786440 | tf_op jit(solution)/shard_map/ppermute | solution.py:141

commit v6 on v5

--- a/solution.py
+++ b/solution.py
@@ -97,7 +97,7 @@
         load.wait()
     me = lax.axis_index("prow")
     y, core = me // 2, lax.rem(me, 2)
-    for p, h in enumerate((2, 1, 3, 0)):
+    for p, h in enumerate((2, 1 + 2 * core, 3 - 2 * core, 0)):
         at = pl.ds(pl.multiple_of((2 * lax.rem(y + h, half) + core) * SLICE, SLICE), SLICE)
         for n in range(2):
             out_ref[pl.ds(p * SLICE, SLICE), n * W : (n + 1) * W] = held[n, :, at].T
@@ -200,10 +200,16 @@
             cost_estimate=pl.CostEstimate(flops=4 * len(dtypes) * SLICE * W * width, bytes_accessed=2 * MIB, transcendentals=0),
         )(turned, own, other)
 
+    def beside(x, way):
+        pairs = []
+        for i in range(rows):
+            pairs.append((i, (i + way * (2 - 4 * (i % 2))) % rows))
+        return lax.ppermute(x, "prow", pairs)
+
     (far,) = terms(0, [jnp.bfloat16])
     met = [shift(far, 2)]
     near, back, kept = terms(1, [jnp.bfloat16, jnp.bfloat16, jnp.float32])
-    met += [shift(near, 1), shift(back, -1)]
+    met += [beside(near, 1), beside(back, -1)]
     product = pl.pallas_call(
         store_kernel,
         out_shape=jax.ShapeDtypeStruct((W, width), jnp.bfloat16),

time: 142 us -> 142 us (level)
  waiting for transfers between devices: 79.3 us -> 81.3 us
    ppermute x6 -> x4, starting transfers between devices: 22 us -> 15.5 us  [shift(): lax.ppermute(x, 'prow', [(i, (i + 2 * h) % rows) for i in range(rows)])]
    ppermute x0 -> x2, waiting for transfers between devices: none -> 6.14 us  [beside(): return lax.ppermute(x, 'prow', pairs)]
    ppermute x0 -> x2, starting transfers between devices: none -> 5.28 us  [beside(): return lax.ppermute(x, 'prow', pairs)]
    ppermute x6 -> x4, waiting for transfers between devices: 23.2 us -> 19 us  [shift(): lax.ppermute(x, 'prow', [(i, (i + 2 * h) % rows) for i in range(rows)])]
  transfers between devices with their start and end apart: 9 -> 9, of which waited for: 7 -> 8; matrix products, arithmetic and copies ran while one was open for 0% -> 0% of each run, Pallas kernels for 2% -> 2%
where the time goes in v6:
time: 142 us; the launch traced here: 141 us
  waiting for transfers between devices  81.3 us (57%)
  starting transfers between devices  46.7 us (33%)
  Pallas kernels  9.84 us (7%)
  local copies, waits for them, and re-layouts  2.29 us (2%)
    all_to_all x1, waiting for transfers between devices, local(): lax.all_to_all(sending, 'pcol', split_axis=0, concat_axis=0, tiled=True)  51 us
    ppermute x4, waiting for transfers between devices, shift(): lax.ppermute(x, 'prow', [(i, (i + 2 * h) % rows) for i in range(rows)])  19 us
    all_to_all x1, starting transfers between devices, local(): lax.all_to_all(sending, 'pcol', split_axis=0, concat_axis=0, tiled=True)  15.8 us
    ppermute x4, starting transfers between devices, shift(): lax.ppermute(x, 'prow', [(i, (i + 2 * h) % rows) for i in range(rows)])  15.5 us
    ppermute x2, starting transfers between devices, swap(): return lax.ppermute(x, 'prow', [(i, i ^ 1) for i in range(rows)])  10.1 us
    ppermute x2, waiting for transfers between devices, beside(): return lax.ppermute(x, 'prow', pairs)  6.14 us
    ppermute x2, starting transfers between devices, beside(): return lax.ppermute(x, 'prow', pairs)  5.28 us
    ppermute x2, waiting for transfers between devices, swap(): return lax.ppermute(x, 'prow', [(i, i ^ 1) for i in range(rows)])  5.08 us
  transfers between devices with their start and end apart: 9, of which 8 were waited for; matrix products, arithmetic and copies ran while one was open for 0% of the time, Pallas kernels for 2%

profile of v6, /device:TPU:1, one launch (start us, length us, event | category | flops | bytes accessed | tf_op | source)
XLA Modules:
  0.0 141.2 jit_solution(18201952622574813327)
XLA Ops:
  0.6 0.0 copy-start.4
  0.6 2.5 %shard_map.68 = bf16[16,256,256]{2,1,0:T(8,128)(2,1)} custom-call(s32[8,16]{1,0:T(8,128)} %bitcast.14, bf16[1024,512]{1,0:T(8,128)(2,1)} %a_ref.1), custom_call_target="tpu_custom_call" | custom-call | bytes 3145728 | tf_op jit(solution)/shard_map/pallas_call | solution.py:147
  3.2 15.8 %all-to-all-start = ((bf16[16,256,256]{2,1,0:T(8,128)(2,1)}), bf16[16,256,256]{2,1,0:T(8,128)(2,1)S(1)}, u32[]{:S(2)}, u32[]{:S(2)}) async-start(bf16[16,256,256]{2,1,0:T(8,128)(2,1)} %shard_map.68), calls=%async_computation | async-start | bytes 4194304 | tf_op jit(solution)/shard_map/all_to_all | solution.py:162
  19.0 3.2 %collective-permute-start = (bf16[256,1024]{1,0:T(8,128)(2,1)S(1)}, bf16[256,1024]{1,0:T(8,128)(2,1)S(1)}, u32[]{:S(2)}, u32[]{:S(2)}) collective-permute-start(bf16[256,1024]{1,0:T(8,128)(2,1)S(1)} %bitcast.16), channel_id=1, source_target_pairs={{0,32},{16,48},{32,64},{48,80},{64,96},{80,112},{96,0},{112,16},{1... | collective-permute-start | bytes 1572872 | tf_op jit(solution)/shard_map/ppermute | solution.py:141
  22.2 4.5 %collective-permute-start.1 = (bf16[256,1024]{1,0:T(8,128)(2,1)S(1)}, bf16[256,1024]{1,0:T(8,128)(2,1)S(1)}, u32[]{:S(2)}, u32[]{:S(2)}) collective-permute-start(bf16[256,1024]{1,0:T(8,128)(2,1)S(1)} %bitcast.17), channel_id=1, source_target_pairs={{0,64},{16,80},{32,96},{48,112},{64,0},{80,16},{96,32},{112,48},{1... | collective-permute-start | bytes 1572872 | tf_op jit(solution)/shard_map/ppermute | solution.py:141
  26.7 3.0 %collective-permute-start.2 = (bf16[256,1024]{1,0:T(8,128)(2,1)S(1)}, bf16[256,1024]{1,0:T(8,128)(2,1)S(1)}, u32[]{:S(2)}, u32[]{:S(2)}) collective-permute-start(bf16[256,1024]{1,0:T(8,128)(2,1)S(1)} %bitcast.18), channel_id=1, source_target_pairs={{0,96},{16,112},{32,0},{48,16},{64,32},{80,48},{96,64},{112,80},{1... | collective-permute-start | bytes 1572872 | tf_op jit(solution)/shard_map/ppermute | solution.py:141
  29.7 5.0 %collective-permute-done = bf16[256,1024]{1,0:T(8,128)(2,1)S(1)} collective-permute-done((bf16[256,1024]{1,0:T(8,128)(2,1)S(1)}, bf16[256,1024]{1,0:T(8,128)(2,1)S(1)}, u32[]{:S(2)}, u32[]{:S(2)}) %collective-permute-start) | collective-permute-done | bytes 524320 | tf_op jit(solution)/shard_map/ppermute | solution.py:141
  34.7 12.3 %collective-permute-done.1 = bf16[256,1024]{1,0:T(8,128)(2,1)S(1)} collective-permute-done((bf16[256,1024]{1,0:T(8,128)(2,1)S(1)}, bf16[256,1024]{1,0:T(8,128)(2,1)S(1)}, u32[]{:S(2)}, u32[]{:S(2)}) %collective-permute-start.1) | collective-permute-done | bytes 524320 | tf_op jit(solution)/shard_map/ppermute | solution.py:141
  47.0 1.7 %collective-permute-done.2 = bf16[256,1024]{1,0:T(8,128)(2,1)S(1)} collective-permute-done((bf16[256,1024]{1,0:T(8,128)(2,1)S(1)}, bf16[256,1024]{1,0:T(8,128)(2,1)S(1)}, u32[]{:S(2)}, u32[]{:S(2)}) %collective-permute-start.2) | collective-permute-done | bytes 524320 | tf_op jit(solution)/shard_map/ppermute | solution.py:141
  48.7 0.3 pad_maximum_fusion
  49.0 3.5 %collective-permute-start.3 = (bf16[4,256,1024]{2,1,0:T(8,128)(2,1)S(1)}, bf16[4,256,1024]{2,1,0:T(8,128)(2,1)S(1)}, u32[]{:S(2)}, u32[]{:S(2)}) collective-permute-start(bf16[4,256,1024]{2,1,0:T(8,128)(2,1)S(1)} %pad_maximum_fusion), channel_id=1, source_target_pairs={{0,16},{16,0},{32,48},{48,32},{64,80},{80,64},{96,112},{112,96},{1... | collective-permute-start | bytes 6291464 | tf_op jit(solution)/shard_map/ppermute | solution.py:144
  52.6 0.0 copy-start.1
  52.6 0.0 copy-start.2
  52.7 3.6 %collective-permute-done.3 = bf16[4,256,1024]{2,1,0:T(8,128)(2,1)S(1)} collective-permute-done((bf16[4,256,1024]{2,1,0:T(8,128)(2,1)S(1)}, bf16[4,256,1024]{2,1,0:T(8,128)(2,1)S(1)}, u32[]{:S(2)}, u32[]{:S(2)}) %collective-permute-start.3) | collective-permute-done | bytes 2097184 | tf_op jit(solution)/shard_map/ppermute | solution.py:144
  56.2 0.2 constant_dynamic-update-slice_fusion.f_ref
  56.4 1.9 %copy-done.3 = bf16[8,256,1024]{2,1,0:T(8,128)(2,1)} copy-done((bf16[8,256,1024]{2,1,0:T(8,128)(2,1)}, bf16[8,256,1024]{2,1,0:T(8,128)(2,1)S(1)}, u32[]{:S(2)}) %copy-start.3) | copy-done | bytes 4194328
  58.4 1.4 shard_map.69.turned_ref
  59.8 0.0 copy-start
  59.8 51.0 %all-to-all-done.a_ref = bf16[16,256,256]{2,1,0:T(8,128)(2,1)S(1)} async-done(((bf16[16,256,256]{2,1,0:T(8,128)(2,1)}), bf16[16,256,256]{2,1,0:T(8,128)(2,1)S(1)}, u32[]{:S(2)}, u32[]{:S(2)}) %all-to-all-start) | async-done | bytes 2097184 | tf_op jit(solution)/shard_map/all_to_all | solution.py:162
  110.8 3.3 %shard_map.70.own_ref = bf16[256,1024]{1,0:T(8,128)(2,1)S(1)} custom-call(s32[8,16]{1,0:T(8,128)S(1)} %bitcast.15, s32[16]{0:T(128)S(1)} %copy-done.2, bf16[16,256,256]{2,1,0:T(8,128)(2,1)S(1)} %all-to-all-done.a_ref, bf16[8,256,1024]{2,1,0:T(8,128)(2,1)} %copy-done.3), custom_call_target="tpu_custom_call" | custom-call | flops 1073741824 | bytes 7340032 | tf_op jit(solution)/shard_map/pallas_call | solution.py:177
  114.1 6.6 %collective-permute-start.4 = (bf16[256,1024]{1,0:T(8,128)(2,1)S(1)}, bf16[256,1024]{1,0:T(8,128)(2,1)S(1)}, u32[]{:S(2)}, u32[]{:S(2)}) collective-permute-start(bf16[256,1024]{1,0:T(8,128)(2,1)S(1)} %shard_map.70.own_ref), channel_id=1, source_target_pairs={{0,16},{16,0},{32,48},{48,32},{64,80},{80,64},{96,112},{112,96},{1... | collective-permute-start | bytes 1572872 | tf_op jit(solution)/shard_map/ppermute | solution.py:144
  120.8 1.5 %collective-permute-done.4.other_ref = bf16[256,1024]{1,0:T(8,128)(2,1)S(1)} collective-permute-done((bf16[256,1024]{1,0:T(8,128)(2,1)S(1)}, bf16[256,1024]{1,0:T(8,128)(2,1)S(1)}, u32[]{:S(2)}, u32[]{:S(2)}) %collective-permute-start.4) | collective-permute-done | bytes 524320 | tf_op jit(solution)/shard_map/ppermute | solution.py:144
  122.3 0.3 shard_map.73
  122.6 4.8 %collective-permute-start.5 = (bf16[128,1024]{1,0:T(8,128)(2,1)S(1)}, bf16[128,1024]{1,0:T(8,128)(2,1)S(1)}, u32[]{:S(2)}, u32[]{:S(2)}) collective-permute-start(bf16[128,1024]{1,0:T(8,128)(2,1)S(1)} %shard_map.73), channel_id=1, source_target_pairs={{0,64},{16,80},{32,96},{48,112},{64,0},{80,16},{96,32},{112,48},{1... | collective-permute-start | bytes 786440 | tf_op jit(solution)/shard_map/ppermute | solution.py:141
  127.4 0.6 shard_map.72
  128.0 2.7 %collective-permute-start.6 = (bf16[128,1024]{1,0:T(8,128)(2,1)S(1)}, bf16[128,1024]{1,0:T(8,128)(2,1)S(1)}, u32[]{:S(2)}, u32[]{:S(2)}) collective-permute-start(bf16[128,1024]{1,0:T(8,128)(2,1)S(1)} %get-tuple-element.10), channel_id=1, source_target_pairs={{0,32},{16,112},{32,64},{48,16},{64,96},{80,48},{96,0},{112,80},{1... | collective-permute-start | bytes 786440 | tf_op jit(solution)/shard_map/ppermute | solution.py:207
  130.7 2.6 %collective-permute-start.7 = (bf16[128,1024]{1,0:T(8,128)(2,1)S(1)}, bf16[128,1024]{1,0:T(8,128)(2,1)S(1)}, u32[]{:S(2)}, u32[]{:S(2)}) collective-permute-start(bf16[128,1024]{1,0:T(8,128)(2,1)S(1)} %get-tuple-element.11), channel_id=1, source_target_pairs={{0,96},{16,48},{32,0},{48,80},{64,32},{80,112},{96,64},{112,16},{1... | collective-permute-start | bytes 786440 | tf_op jit(solution)/shard_map/ppermute | solution.py:207
  133.3 0.8 shard_map.71
  134.1 0.0 collective-permute-done.5.refs_0_
  134.1 4.4 %collective-permute-done.6.refs_1_ = bf16[128,1024]{1,0:T(8,128)(2,1)S(1)} collective-permute-done((bf16[128,1024]{1,0:T(8,128)(2,1)S(1)}, bf16[128,1024]{1,0:T(8,128)(2,1)S(1)}, u32[]{:S(2)}, u32[]{:S(2)}) %collective-permute-start.6) | collective-permute-done | bytes 262176 | tf_op jit(solution)/shard_map/ppermute | solution.py:207
  138.6 1.7 %collective-permute-done.7.refs_2_ = bf16[128,1024]{1,0:T(8,128)(2,1)S(1)} collective-permute-done((bf16[128,1024]{1,0:T(8,128)(2,1)S(1)}, bf16[128,1024]{1,0:T(8,128)(2,1)S(1)}, u32[]{:S(2)}, u32[]{:S(2)}) %collective-permute-start.7) | collective-permute-done | bytes 262176 | tf_op jit(solution)/shard_map/ppermute | solution.py:207
  140.3 0.9 shard_map.74
  (9 shorter events, 0.2 us)
Async XLA Ops:
  0.6 18.4 %copy-start.4 = (bf16[1,1,256,1024]{3,2,1,0:T(8,128)(2,1)S(1)}, bf16[1,1,256,1024]{3,2,1,0:T(8,128)(2,1)}, u32[]{:S(2)}) copy-start(bf16[1,1,256,1024]{3,2,1,0:T(8,128)(2,1)} %param.6) | copy-start | bytes 1572868
  3.2 107.6 %all-to-all-start = ((bf16[16,256,256]{2,1,0:T(8,128)(2,1)}), bf16[16,256,256]{2,1,0:T(8,128)(2,1)S(1)}, u32[]{:S(2)}, u32[]{:S(2)}) async-start(bf16[16,256,256]{2,1,0:T(8,128)(2,1)} %shard_map.68), calls=%async_computation | async-start | bytes 4194304 | tf_op jit(solution)/shard_map/all_to_all | solution.py:162
  19.0 15.7 %collective-permute-start = (bf16[256,1024]{1,0:T(8,128)(2,1)S(1)}, bf16[256,1024]{1,0:T(8,128)(2,1)S(1)}, u32[]{:S(2)}, u32[]{:S(2)}) collective-permute-start(bf16[256,1024]{1,0:T(8,128)(2,1)S(1)} %bitcast.16), channel_id=1, source_target_pairs={{0,32},{16,48},{32,64},{48,80},{64,96},{80,112},{96,0},{112,16},{1... | collective-permute-start | bytes 1572872 | tf_op jit(solution)/shard_map/ppermute | solution.py:141
  22.2 24.8 %collective-permute-start.1 = (bf16[256,1024]{1,0:T(8,128)(2,1)S(1)}, bf16[256,1024]{1,0:T(8,128)(2,1)S(1)}, u32[]{:S(2)}, u32[]{:S(2)}) collective-permute-start(bf16[256,1024]{1,0:T(8,128)(2,1)S(1)} %bitcast.17), channel_id=1, source_target_pairs={{0,64},{16,80},{32,96},{48,112},{64,0},{80,16},{96,32},{112,48},{1... | collective-permute-start | bytes 1572872 | tf_op jit(solution)/shard_map/ppermute | solution.py:141
  26.7 22.0 %collective-permute-start.2 = (bf16[256,1024]{1,0:T(8,128)(2,1)S(1)}, bf16[256,1024]{1,0:T(8,128)(2,1)S(1)}, u32[]{:S(2)}, u32[]{:S(2)}) collective-permute-start(bf16[256,1024]{1,0:T(8,128)(2,1)S(1)} %bitcast.18), channel_id=1, source_target_pairs={{0,96},{16,112},{32,0},{48,16},{64,32},{80,48},{96,64},{112,80},{1... | collective-permute-start | bytes 1572872 | tf_op jit(solution)/shard_map/ppermute | solution.py:141
  49.0 7.2 %collective-permute-start.3 = (bf16[4,256,1024]{2,1,0:T(8,128)(2,1)S(1)}, bf16[4,256,1024]{2,1,0:T(8,128)(2,1)S(1)}, u32[]{:S(2)}, u32[]{:S(2)}) collective-permute-start(bf16[4,256,1024]{2,1,0:T(8,128)(2,1)S(1)} %pad_maximum_fusion), channel_id=1, source_target_pairs={{0,16},{16,0},{32,48},{48,32},{64,80},{80,64},{96,112},{112,96},{1... | collective-permute-start | bytes 6291464 | tf_op jit(solution)/shard_map/ppermute | solution.py:144
  52.6 58.2 %copy-start.1 = (s32[16,8]{0,1:T(8,128)S(1)}, s32[16,8]{0,1:T(8,128)}, u32[]{:S(2)}) copy-start(s32[16,8]{0,1:T(8,128)} %param.8) | copy-start | bytes 1540
  52.6 58.2 %copy-start.2 = (s32[16]{0:T(128)S(1)}, s32[16]{0:T(128)}, u32[]{:S(2)}) copy-start(s32[16]{0:T(128)} %count_ref.1) | copy-start | bytes 196
  56.4 2.0 %copy-start.3 = (bf16[8,256,1024]{2,1,0:T(8,128)(2,1)}, bf16[8,256,1024]{2,1,0:T(8,128)(2,1)S(1)}, u32[]{:S(2)}) copy-start(bf16[8,256,1024]{2,1,0:T(8,128)(2,1)S(1)} %constant_dynamic-update-slice_fusion.f_ref) | copy-start | bytes 12582916
  59.8 80.5 %copy-start = (f32[1,128,1024]{2,1,0:T(8,128)S(1)}, f32[1,128,1024]{2,1,0:T(8,128)}, u32[]{:S(2)}) copy-start(f32[1,128,1024]{2,1,0:T(8,128)} %param.7) | copy-start | bytes 1572868
  114.1 8.2 %collective-permute-start.4 = (bf16[256,1024]{1,0:T(8,128)(2,1)S(1)}, bf16[256,1024]{1,0:T(8,128)(2,1)S(1)}, u32[]{:S(2)}, u32[]{:S(2)}) collective-permute-start(bf16[256,1024]{1,0:T(8,128)(2,1)S(1)} %shard_map.70.own_ref), channel_id=1, source_target_pairs={{0,16},{16,0},{32,48},{48,32},{64,80},{80,64},{96,112},{112,96},{1... | collective-permute-start | bytes 1572872 | tf_op jit(solution)/shard_map/ppermute | solution.py:144
  122.6 11.5 %collective-permute-start.5 = (bf16[128,1024]{1,0:T(8,128)(2,1)S(1)}, bf16[128,1024]{1,0:T(8,128)(2,1)S(1)}, u32[]{:S(2)}, u32[]{:S(2)}) collective-permute-start(bf16[128,1024]{1,0:T(8,128)(2,1)S(1)} %shard_map.73), channel_id=1, source_target_pairs={{0,64},{16,80},{32,96},{48,112},{64,0},{80,16},{96,32},{112,48},{1... | collective-permute-start | bytes 786440 | tf_op jit(solution)/shard_map/ppermute | solution.py:141
  128.0 10.6 %collective-permute-start.6 = (bf16[128,1024]{1,0:T(8,128)(2,1)S(1)}, bf16[128,1024]{1,0:T(8,128)(2,1)S(1)}, u32[]{:S(2)}, u32[]{:S(2)}) collective-permute-start(bf16[128,1024]{1,0:T(8,128)(2,1)S(1)} %get-tuple-element.10), channel_id=1, source_target_pairs={{0,32},{16,112},{32,64},{48,16},{64,96},{80,48},{96,0},{112,80},{1... | collective-permute-start | bytes 786440 | tf_op jit(solution)/shard_map/ppermute | solution.py:207
  130.7 9.6 %collective-permute-start.7 = (bf16[128,1024]{1,0:T(8,128)(2,1)S(1)}, bf16[128,1024]{1,0:T(8,128)(2,1)S(1)}, u32[]{:S(2)}, u32[]{:S(2)}) collective-permute-start(bf16[128,1024]{1,0:T(8,128)(2,1)S(1)} %get-tuple-element.11), channel_id=1, source_target_pairs={{0,96},{16,48},{32,0},{48,80},{64,32},{80,112},{96,64},{112,16},{1... | collective-permute-start | bytes 786440 | tf_op jit(solution)/shard_map/ppermute | solution.py:207

commit v7 on v6

--- a/solution.py
+++ b/solution.py
@@ -50,10 +50,16 @@
         pl.when(needed)(store.wait)
 
 
-def product_kernel(rows, cols, anc_ref, count_ref, a_ref, f_ref, own_ref, held, factors, total, sems):
+def product_kernel(rows, cols, anc_ref, count_ref, a_ref, f_ref, own_ref, held, factors, total, sems, names, counts, small_sems):
     half = rows // 2
     width = own_ref.shape[-1]
     step = 256
+    small = [
+        pltpu.make_async_copy(anc_ref, names, small_sems.at[0]),
+        pltpu.make_async_copy(count_ref, counts, small_sems.at[1]),
+    ]
+    for fetch in small:
+        fetch.start()
     loads = []
     for n in range(rows):
         load = pltpu.make_async_copy(f_ref.at[n], factors.at[n], sems.at[n])
@@ -61,12 +67,14 @@
         loads.append(load)
     me_row = lax.axis_index("prow")
     me_col = lax.axis_index("pcol")
-    count = count_ref[me_col]
+    for fetch in small:
+        fetch.wait()
+    count = counts[me_col]
     row_live = (me_row < count).astype(jnp.float32)
     for n in range(rows):
         t = slot_row(me_row, n, rows)
         live = (t < count).astype(jnp.bfloat16)
-        held[n] = a_ref[lax.rem(anc_ref[t, me_col], cols)] * live
+        held[n] = a_ref[lax.rem(names[t, me_col], cols)] * live
     for n in range(0, rows, 2):
         for load in loads[n : n + 2]:
             load.wait()
@@ -177,13 +185,16 @@
     own = pl.pallas_call(
         functools.partial(product_kernel, rows, cols),
         out_shape=jax.ShapeDtypeStruct((W, width), jnp.bfloat16),
-        in_specs=[SMEM, SMEM, VMEM, HBM],
+        in_specs=[HBM, HBM, VMEM, HBM],
         out_specs=VMEM,
         scratch_shapes=[
             pltpu.VMEM((rows, W, W), jnp.bfloat16),
             pltpu.VMEM((rows, W, width), jnp.bfloat16),
             pltpu.VMEM((W, width), jnp.float32),
             pltpu.SemaphoreType.DMA((rows,)),
+            pltpu.SMEM((rows, cols), jnp.int32),
+            pltpu.SMEM((cols,), jnp.int32),
+            pltpu.SemaphoreType.DMA((2,)),
         ],
         compiler_params=pltpu.CompilerParams(vmem_limit_bytes=50 * MIB),
         cost_estimate=pl.CostEstimate(flops=2 * rows * W * W * width, bytes_accessed=7 * MIB, transcendentals=0),

time: 142 us -> 141 us (level)
  no operation moved by 1% of the time
where the time goes in v7:
time: 141 us; the launch traced here: 140 us
  waiting for transfers between devices  81.2 us (58%)
  starting transfers between devices  46.4 us (33%)
  Pallas kernels  9.39 us (7%)
  local copies, waits for them, and re-layouts  2.29 us (2%)
    all_to_all x1, waiting for transfers between devices, local(): lax.all_to_all(sending, 'pcol', split_axis=0, concat_axis=0, tiled=True)  51 us
    ppermute x4, waiting for transfers between devices, shift(): lax.ppermute(x, 'prow', [(i, (i + 2 * h) % rows) for i in range(rows)])  19 us
    all_to_all x1, starting transfers between devices, local(): lax.all_to_all(sending, 'pcol', split_axis=0, concat_axis=0, tiled=True)  15.5 us
    ppermute x4, starting transfers between devices, shift(): lax.ppermute(x, 'prow', [(i, (i + 2 * h) % rows) for i in range(rows)])  15.5 us
    ppermute x2, starting transfers between devices, swap(): return lax.ppermute(x, 'prow', [(i, i ^ 1) for i in range(rows)])  10.1 us
    ppermute x2, waiting for transfers between devices, beside(): return lax.ppermute(x, 'prow', pairs)  6.13 us
    ppermute x2, starting transfers between devices, beside(): return lax.ppermute(x, 'prow', pairs)  5.28 us
    ppermute x2, waiting for transfers between devices, swap(): return lax.ppermute(x, 'prow', [(i, i ^ 1) for i in range(rows)])  5.08 us
  transfers between devices with their start and end apart: 9, of which 8 were waited for; matrix products, arithmetic and copies ran while one was open for 0% of the time, Pallas kernels for 2%

profile of v7, /device:TPU:1, one launch (start us, length us, event | category | flops | bytes accessed | tf_op | source)
XLA Modules:
  0.0 140.5 jit_solution(16106576823326560276)
XLA Ops:
  0.6 0.0 copy-start.4
  0.6 2.7 %shard_map.68 = bf16[16,256,256]{2,1,0:T(8,128)(2,1)} custom-call(s32[8,16]{1,0:T(8,128)} %bitcast.14, bf16[1024,512]{1,0:T(8,128)(2,1)} %a_ref.1), custom_call_target="tpu_custom_call" | custom-call | bytes 3145728 | tf_op jit(solution)/shard_map/pallas_call | solution.py:155
  3.3 15.5 %all-to-all-start = ((bf16[16,256,256]{2,1,0:T(8,128)(2,1)}), bf16[16,256,256]{2,1,0:T(8,128)(2,1)S(1)}, u32[]{:S(2)}, u32[]{:S(2)}) async-start(bf16[16,256,256]{2,1,0:T(8,128)(2,1)} %shard_map.68), calls=%async_computation | async-start | bytes 4194304 | tf_op jit(solution)/shard_map/all_to_all | solution.py:170
  18.9 3.2 %collective-permute-start = (bf16[256,1024]{1,0:T(8,128)(2,1)S(1)}, bf16[256,1024]{1,0:T(8,128)(2,1)S(1)}, u32[]{:S(2)}, u32[]{:S(2)}) collective-permute-start(bf16[256,1024]{1,0:T(8,128)(2,1)S(1)} %bitcast.16), channel_id=1, source_target_pairs={{0,32},{16,48},{32,64},{48,80},{64,96},{80,112},{96,0},{112,16},{1... | collective-permute-start | bytes 1572872 | tf_op jit(solution)/shard_map/ppermute | solution.py:149
  22.1 4.5 %collective-permute-start.1 = (bf16[256,1024]{1,0:T(8,128)(2,1)S(1)}, bf16[256,1024]{1,0:T(8,128)(2,1)S(1)}, u32[]{:S(2)}, u32[]{:S(2)}) collective-permute-start(bf16[256,1024]{1,0:T(8,128)(2,1)S(1)} %bitcast.17), channel_id=1, source_target_pairs={{0,64},{16,80},{32,96},{48,112},{64,0},{80,16},{96,32},{112,48},{1... | collective-permute-start | bytes 1572872 | tf_op jit(solution)/shard_map/ppermute | solution.py:149
  26.6 3.0 %collective-permute-start.2 = (bf16[256,1024]{1,0:T(8,128)(2,1)S(1)}, bf16[256,1024]{1,0:T(8,128)(2,1)S(1)}, u32[]{:S(2)}, u32[]{:S(2)}) collective-permute-start(bf16[256,1024]{1,0:T(8,128)(2,1)S(1)} %bitcast.18), channel_id=1, source_target_pairs={{0,96},{16,112},{32,0},{48,16},{64,32},{80,48},{96,64},{112,80},{1... | collective-permute-start | bytes 1572872 | tf_op jit(solution)/shard_map/ppermute | solution.py:149
  29.6 5.0 %collective-permute-done = bf16[256,1024]{1,0:T(8,128)(2,1)S(1)} collective-permute-done((bf16[256,1024]{1,0:T(8,128)(2,1)S(1)}, bf16[256,1024]{1,0:T(8,128)(2,1)S(1)}, u32[]{:S(2)}, u32[]{:S(2)}) %collective-permute-start) | collective-permute-done | bytes 524320 | tf_op jit(solution)/shard_map/ppermute | solution.py:149
  34.6 12.3 %collective-permute-done.1 = bf16[256,1024]{1,0:T(8,128)(2,1)S(1)} collective-permute-done((bf16[256,1024]{1,0:T(8,128)(2,1)S(1)}, bf16[256,1024]{1,0:T(8,128)(2,1)S(1)}, u32[]{:S(2)}, u32[]{:S(2)}) %collective-permute-start.1) | collective-permute-done | bytes 524320 | tf_op jit(solution)/shard_map/ppermute | solution.py:149
  46.9 1.7 %collective-permute-done.2 = bf16[256,1024]{1,0:T(8,128)(2,1)S(1)} collective-permute-done((bf16[256,1024]{1,0:T(8,128)(2,1)S(1)}, bf16[256,1024]{1,0:T(8,128)(2,1)S(1)}, u32[]{:S(2)}, u32[]{:S(2)}) %collective-permute-start.2) | collective-permute-done | bytes 524320 | tf_op jit(solution)/shard_map/ppermute | solution.py:149
  48.6 0.3 pad_maximum_fusion
  48.9 3.5 %collective-permute-start.3 = (bf16[4,256,1024]{2,1,0:T(8,128)(2,1)S(1)}, bf16[4,256,1024]{2,1,0:T(8,128)(2,1)S(1)}, u32[]{:S(2)}, u32[]{:S(2)}) collective-permute-start(bf16[4,256,1024]{2,1,0:T(8,128)(2,1)S(1)} %pad_maximum_fusion), channel_id=1, source_target_pairs={{0,16},{16,0},{32,48},{48,32},{64,80},{80,64},{96,112},{112,96},{1... | collective-permute-start | bytes 6291464 | tf_op jit(solution)/shard_map/ppermute | solution.py:152
  52.5 0.0 copy-start.1
  52.5 0.0 copy-start.2
  52.5 3.6 %collective-permute-done.3 = bf16[4,256,1024]{2,1,0:T(8,128)(2,1)S(1)} collective-permute-done((bf16[4,256,1024]{2,1,0:T(8,128)(2,1)S(1)}, bf16[4,256,1024]{2,1,0:T(8,128)(2,1)S(1)}, u32[]{:S(2)}, u32[]{:S(2)}) %collective-permute-start.3) | collective-permute-done | bytes 2097184 | tf_op jit(solution)/shard_map/ppermute | solution.py:152
  56.1 0.2 constant_dynamic-update-slice_fusion.f_ref
  56.3 1.9 %copy-done.3 = bf16[8,256,1024]{2,1,0:T(8,128)(2,1)} copy-done((bf16[8,256,1024]{2,1,0:T(8,128)(2,1)}, bf16[8,256,1024]{2,1,0:T(8,128)(2,1)S(1)}, u32[]{:S(2)}) %copy-start.3) | copy-done | bytes 4194328
  58.2 1.4 %shard_map.69.turned_ref = bf16[512,512]{1,0:T(8,128)(2,1)S(1)} custom-call(bf16[8,256,1024]{2,1,0:T(8,128)(2,1)} %copy-done.3), custom_call_target="tpu_custom_call" | custom-call | bytes 2097152 | tf_op jit(solution)/shard_map/pallas_call | solution.py:174
  59.6 0.0 copy-start
  59.7 51.0 %all-to-all-done.a_ref = bf16[16,256,256]{2,1,0:T(8,128)(2,1)S(1)} async-done(((bf16[16,256,256]{2,1,0:T(8,128)(2,1)}), bf16[16,256,256]{2,1,0:T(8,128)(2,1)S(1)}, u32[]{:S(2)}, u32[]{:S(2)}) %all-to-all-start) | async-done | bytes 2097184 | tf_op jit(solution)/shard_map/all_to_all | solution.py:170
  110.7 2.7 %shard_map.70.own_ref = bf16[256,1024]{1,0:T(8,128)(2,1)S(1)} custom-call(s32[8,16]{1,0:T(8,128)S(1)} %bitcast.15, s32[16]{0:T(128)S(1)} %copy-done.2, bf16[16,256,256]{2,1,0:T(8,128)(2,1)S(1)} %all-to-all-done.a_ref, bf16[8,256,1024]{2,1,0:T(8,128)(2,1)} %copy-done.3), custom_call_target="tpu_custom_call" | custom-call | flops 1073741824 | bytes 7340032 | tf_op jit(solution)/shard_map/pallas_call | solution.py:185
  113.4 6.6 %collective-permute-start.4 = (bf16[256,1024]{1,0:T(8,128)(2,1)S(1)}, bf16[256,1024]{1,0:T(8,128)(2,1)S(1)}, u32[]{:S(2)}, u32[]{:S(2)}) collective-permute-start(bf16[256,1024]{1,0:T(8,128)(2,1)S(1)} %shard_map.70.own_ref), channel_id=1, source_target_pairs={{0,16},{16,0},{32,48},{48,32},{64,80},{80,64},{96,112},{112,96},{1... | collective-permute-start | bytes 1572872 | tf_op jit(solution)/shard_map/ppermute | solution.py:152
  120.1 1.5 %collective-permute-done.4.other_ref = bf16[256,1024]{1,0:T(8,128)(2,1)S(1)} collective-permute-done((bf16[256,1024]{1,0:T(8,128)(2,1)S(1)}, bf16[256,1024]{1,0:T(8,128)(2,1)S(1)}, u32[]{:S(2)}, u32[]{:S(2)}) %collective-permute-start.4) | collective-permute-done | bytes 524320 | tf_op jit(solution)/shard_map/ppermute | solution.py:152
  121.6 0.3 shard_map.73
  121.9 4.8 %collective-permute-start.5 = (bf16[128,1024]{1,0:T(8,128)(2,1)S(1)}, bf16[128,1024]{1,0:T(8,128)(2,1)S(1)}, u32[]{:S(2)}, u32[]{:S(2)}) collective-permute-start(bf16[128,1024]{1,0:T(8,128)(2,1)S(1)} %shard_map.73), channel_id=1, source_target_pairs={{0,64},{16,80},{32,96},{48,112},{64,0},{80,16},{96,32},{112,48},{1... | collective-permute-start | bytes 786440 | tf_op jit(solution)/shard_map/ppermute | solution.py:149
  126.7 0.6 shard_map.72
  127.3 2.7 %collective-permute-start.6 = (bf16[128,1024]{1,0:T(8,128)(2,1)S(1)}, bf16[128,1024]{1,0:T(8,128)(2,1)S(1)}, u32[]{:S(2)}, u32[]{:S(2)}) collective-permute-start(bf16[128,1024]{1,0:T(8,128)(2,1)S(1)} %get-tuple-element.10), channel_id=1, source_target_pairs={{0,32},{16,112},{32,64},{48,16},{64,96},{80,48},{96,0},{112,80},{1... | collective-permute-start | bytes 786440 | tf_op jit(solution)/shard_map/ppermute | solution.py:218
  130.0 2.6 %collective-permute-start.7 = (bf16[128,1024]{1,0:T(8,128)(2,1)S(1)}, bf16[128,1024]{1,0:T(8,128)(2,1)S(1)}, u32[]{:S(2)}, u32[]{:S(2)}) collective-permute-start(bf16[128,1024]{1,0:T(8,128)(2,1)S(1)} %get-tuple-element.11), channel_id=1, source_target_pairs={{0,96},{16,48},{32,0},{48,80},{64,32},{80,112},{96,64},{112,16},{1... | collective-permute-start | bytes 786440 | tf_op jit(solution)/shard_map/ppermute | solution.py:218
  132.6 0.8 shard_map.71
  133.4 0.0 collective-permute-done.5.refs_0_
  133.4 4.4 %collective-permute-done.6.refs_1_ = bf16[128,1024]{1,0:T(8,128)(2,1)S(1)} collective-permute-done((bf16[128,1024]{1,0:T(8,128)(2,1)S(1)}, bf16[128,1024]{1,0:T(8,128)(2,1)S(1)}, u32[]{:S(2)}, u32[]{:S(2)}) %collective-permute-start.6) | collective-permute-done | bytes 262176 | tf_op jit(solution)/shard_map/ppermute | solution.py:218
  137.9 1.7 %collective-permute-done.7.refs_2_ = bf16[128,1024]{1,0:T(8,128)(2,1)S(1)} collective-permute-done((bf16[128,1024]{1,0:T(8,128)(2,1)S(1)}, bf16[128,1024]{1,0:T(8,128)(2,1)S(1)}, u32[]{:S(2)}, u32[]{:S(2)}) %collective-permute-start.7) | collective-permute-done | bytes 262176 | tf_op jit(solution)/shard_map/ppermute | solution.py:218
  139.6 0.9 shard_map.74
  (9 shorter events, 0.2 us)
Async XLA Ops:
  0.6 18.2 %copy-start.4 = (bf16[1,1,256,1024]{3,2,1,0:T(8,128)(2,1)S(1)}, bf16[1,1,256,1024]{3,2,1,0:T(8,128)(2,1)}, u32[]{:S(2)}) copy-start(bf16[1,1,256,1024]{3,2,1,0:T(8,128)(2,1)} %param.6) | copy-start | bytes 1572868
  3.3 107.4 %all-to-all-start = ((bf16[16,256,256]{2,1,0:T(8,128)(2,1)}), bf16[16,256,256]{2,1,0:T(8,128)(2,1)S(1)}, u32[]{:S(2)}, u32[]{:S(2)}) async-start(bf16[16,256,256]{2,1,0:T(8,128)(2,1)} %shard_map.68), calls=%async_computation | async-start | bytes 4194304 | tf_op jit(solution)/shard_map/all_to_all | solution.py:170
  18.9 15.7 %collective-permute-start = (bf16[256,1024]{1,0:T(8,128)(2,1)S(1)}, bf16[256,1024]{1,0:T(8,128)(2,1)S(1)}, u32[]{:S(2)}, u32[]{:S(2)}) collective-permute-start(bf16[256,1024]{1,0:T(8,128)(2,1)S(1)} %bitcast.16), channel_id=1, source_target_pairs={{0,32},{16,48},{32,64},{48,80},{64,96},{80,112},{96,0},{112,16},{1... | collective-permute-start | bytes 1572872 | tf_op jit(solution)/shard_map/ppermute | solution.py:149
  22.1 24.8 %collective-permute-start.1 = (bf16[256,1024]{1,0:T(8,128)(2,1)S(1)}, bf16[256,1024]{1,0:T(8,128)(2,1)S(1)}, u32[]{:S(2)}, u32[]{:S(2)}) collective-permute-start(bf16[256,1024]{1,0:T(8,128)(2,1)S(1)} %bitcast.17), channel_id=1, source_target_pairs={{0,64},{16,80},{32,96},{48,112},{64,0},{80,16},{96,32},{112,48},{1... | collective-permute-start | bytes 1572872 | tf_op jit(solution)/shard_map/ppermute | solution.py:149
  26.6 22.0 %collective-permute-start.2 = (bf16[256,1024]{1,0:T(8,128)(2,1)S(1)}, bf16[256,1024]{1,0:T(8,128)(2,1)S(1)}, u32[]{:S(2)}, u32[]{:S(2)}) collective-permute-start(bf16[256,1024]{1,0:T(8,128)(2,1)S(1)} %bitcast.18), channel_id=1, source_target_pairs={{0,96},{16,112},{32,0},{48,16},{64,32},{80,48},{96,64},{112,80},{1... | collective-permute-start | bytes 1572872 | tf_op jit(solution)/shard_map/ppermute | solution.py:149
  48.9 7.2 %collective-permute-start.3 = (bf16[4,256,1024]{2,1,0:T(8,128)(2,1)S(1)}, bf16[4,256,1024]{2,1,0:T(8,128)(2,1)S(1)}, u32[]{:S(2)}, u32[]{:S(2)}) collective-permute-start(bf16[4,256,1024]{2,1,0:T(8,128)(2,1)S(1)} %pad_maximum_fusion), channel_id=1, source_target_pairs={{0,16},{16,0},{32,48},{48,32},{64,80},{80,64},{96,112},{112,96},{1... | collective-permute-start | bytes 6291464 | tf_op jit(solution)/shard_map/ppermute | solution.py:152
  52.5 58.2 %copy-start.1 = (s32[16,8]{0,1:T(8,128)S(1)}, s32[16,8]{0,1:T(8,128)}, u32[]{:S(2)}) copy-start(s32[16,8]{0,1:T(8,128)} %param.8) | copy-start | bytes 1540
  52.5 58.2 %copy-start.2 = (s32[16]{0:T(128)S(1)}, s32[16]{0:T(128)}, u32[]{:S(2)}) copy-start(s32[16]{0:T(128)} %count_ref.1) | copy-start | bytes 196
  56.3 2.0 %copy-start.3 = (bf16[8,256,1024]{2,1,0:T(8,128)(2,1)}, bf16[8,256,1024]{2,1,0:T(8,128)(2,1)S(1)}, u32[]{:S(2)}) copy-start(bf16[8,256,1024]{2,1,0:T(8,128)(2,1)S(1)} %constant_dynamic-update-slice_fusion.f_ref) | copy-start | bytes 12582916
  59.6 79.9 %copy-start = (f32[1,128,1024]{2,1,0:T(8,128)S(1)}, f32[1,128,1024]{2,1,0:T(8,128)}, u32[]{:S(2)}) copy-start(f32[1,128,1024]{2,1,0:T(8,128)} %param.7) | copy-start | bytes 1572868
  113.4 8.2 %collective-permute-start.4 = (bf16[256,1024]{1,0:T(8,128)(2,1)S(1)}, bf16[256,1024]{1,0:T(8,128)(2,1)S(1)}, u32[]{:S(2)}, u32[]{:S(2)}) collective-permute-start(bf16[256,1024]{1,0:T(8,128)(2,1)S(1)} %shard_map.70.own_ref), channel_id=1, source_target_pairs={{0,16},{16,0},{32,48},{48,32},{64,80},{80,64},{96,112},{112,96},{1... | collective-permute-start | bytes 1572872 | tf_op jit(solution)/shard_map/ppermute | solution.py:152
  121.9 11.5 %collective-permute-start.5 = (bf16[128,1024]{1,0:T(8,128)(2,1)S(1)}, bf16[128,1024]{1,0:T(8,128)(2,1)S(1)}, u32[]{:S(2)}, u32[]{:S(2)}) collective-permute-start(bf16[128,1024]{1,0:T(8,128)(2,1)S(1)} %shard_map.73), channel_id=1, source_target_pairs={{0,64},{16,80},{32,96},{48,112},{64,0},{80,16},{96,32},{112,48},{1... | collective-permute-start | bytes 786440 | tf_op jit(solution)/shard_map/ppermute | solution.py:149
  127.3 10.6 %collective-permute-start.6 = (bf16[128,1024]{1,0:T(8,128)(2,1)S(1)}, bf16[128,1024]{1,0:T(8,128)(2,1)S(1)}, u32[]{:S(2)}, u32[]{:S(2)}) collective-permute-start(bf16[128,1024]{1,0:T(8,128)(2,1)S(1)} %get-tuple-element.10), channel_id=1, source_target_pairs={{0,32},{16,112},{32,64},{48,16},{64,96},{80,48},{96,0},{112,80},{1... | collective-permute-start | bytes 786440 | tf_op jit(solution)/shard_map/ppermute | solution.py:218
  130.0 9.6 %collective-permute-start.7 = (bf16[128,1024]{1,0:T(8,128)(2,1)S(1)}, bf16[128,1024]{1,0:T(8,128)(2,1)S(1)}, u32[]{:S(2)}, u32[]{:S(2)}) collective-permute-start(bf16[128,1024]{1,0:T(8,128)(2,1)S(1)} %get-tuple-element.11), channel_id=1, source_target_pairs={{0,96},{16,48},{32,0},{48,80},{64,32},{80,112},{96,64},{112,16},{1... | collective-permute-start | bytes 786440 | tf_op jit(solution)/shard_map/ppermute | solution.py:218

commit v8 on v7

--- a/solution.py
+++ b/solution.py
@@ -13,41 +13,31 @@
 
 
 def pick_kernel(rows, cols, anc_ref, a_ref, out_ref, names, held, names_sem, in_sems, out_sems):
-    high, wide = a_ref.shape[0] // W, a_ref.shape[1] // W
-    part = W // 2
     fetch = pltpu.make_async_copy(anc_ref, names, names_sem)
     fetch.start()
     loads = []
-    for p in range(2):
-        for n in range(high * wide):
-            i, j = n // wide, n % wide
-            load = pltpu.make_async_copy(
-                a_ref.at[pl.ds(i * W + p * part, part), pl.ds(j * W, W)],
-                held.at[n, pl.ds(p * part, part)],
-                in_sems.at[p, n],
-            )
-            load.start()
-            loads.append(load)
+    for i in range(a_ref.shape[0] // W):
+        at = pl.ds(i * W, W)
+        load = pltpu.make_async_copy(a_ref.at[at], held.at[at], in_sems.at[i])
+        load.start()
+        loads.append(load)
     me_row = lax.axis_index("prow")
     me_col = lax.axis_index("pcol")
     slot = lax.rem(me_col, rows)
     fetch.wait()
-    owed, picks = [], []
+    stores = []
     for k in range(cols):
         name = names[slot, k]
-        picks.append((names[me_row, k] // rows) * wide + name // cols)
-        owed.append(lax.rem(name, cols) == me_col)
-    stores = []
-    for p in range(2):
-        for load in loads[p * high * wide : (p + 1) * high * wide]:
-            load.wait()
-        at = pl.ds(p * part, part)
-        for k in range(cols):
-            store = pltpu.make_async_copy(held.at[picks[k], at], out_ref.at[k, at], out_sems.at[p, k])
-            pl.when(owed[k])(store.start)
-            stores.append((owed[k], store))
-    for needed, store in stores:
-        pl.when(needed)(store.wait)
+        i = names[me_row, k] // rows
+        j = name // cols
+        block = held.at[pl.ds(pl.multiple_of(i * W, W), W), pl.ds(pl.multiple_of(j * W, W), W)]
+        stores.append((lax.rem(name, cols) == me_col, pltpu.make_async_copy(block, out_ref.at[k], out_sems.at[k])))
+    for load in loads:
+        load.wait()
+    for owed, store in stores:
+        pl.when(owed)(store.start)
+    for owed, store in stores:
+        pl.when(owed)(store.wait)
 
 
 def product_kernel(rows, cols, anc_ref, count_ref, a_ref, f_ref, own_ref, held, factors, total, sems, names, counts, small_sems):
@@ -119,17 +109,28 @@
         ref[...] = total.astype(ref.dtype)
 
 
-def store_kernel(own_ref, out_ref, sem):
+def store_kernel(own_ref, diag_ref, kept_ref, out_ref, base_ref, sem):
     store = pltpu.make_async_copy(own_ref, out_ref, sem)
     store.start()
+    base_ref[...] = diag_ref[...] - kept_ref[...]
     store.wait()
 
 
-def sum_kernel(diag_ref, kept_ref, *refs):
-    total = kept_ref[...]
-    for ref in refs[:-1]:
-        total += ref[...].astype(jnp.float32)
-    refs[-1][...] = diag_ref[...] - total
+def sum_kernel(base_ref, *refs):
+    out_ref, held, sems = refs[-3:]
+    part = SLICE // 4
+    stores = []
+    for p in range(4):
+        at = pl.ds(p * part, part)
+        total = base_ref[at]
+        for ref in refs[:-3]:
+            total -= ref[at].astype(jnp.float32)
+        held[at] = total
+        store = pltpu.make_async_copy(held.at[at], out_ref.at[at], sems.at[p])
+        store.start()
+        stores.append(store)
+    for store in stores:
+        store.wait()
 
 
 SMEM = pl.BlockSpec(memory_space=pltpu.SMEM)
@@ -151,7 +152,6 @@
     def swap(x):
         return lax.ppermute(x, "prow", [(i, i ^ 1) for i in range(rows)])
 
-    blocks = (anc_inverse.shape[0] // W) * (anc_inverse.shape[1] // W)
     sending = pl.pallas_call(
         functools.partial(pick_kernel, rows, cols),
         out_shape=jax.ShapeDtypeStruct((cols, W, W), jnp.bfloat16),
@@ -159,10 +159,10 @@
         out_specs=HBM,
         scratch_shapes=[
             pltpu.SMEM((rows, cols), jnp.int32),
-            pltpu.VMEM((blocks, W, W), jnp.bfloat16),
+            pltpu.VMEM(anc_inverse.shape, jnp.bfloat16),
             pltpu.SemaphoreType.DMA,
-            pltpu.SemaphoreType.DMA((2, blocks)),
-            pltpu.SemaphoreType.DMA((2, cols)),
+            pltpu.SemaphoreType.DMA((anc_inverse.shape[0] // W,)),
+            pltpu.SemaphoreType.DMA((cols,)),
         ],
         compiler_params=pltpu.CompilerParams(vmem_limit_bytes=60 * MIB),
         cost_estimate=pl.CostEstimate(flops=0, bytes_accessed=3 * MIB, transcendentals=0),
@@ -221,23 +221,24 @@
     met = [shift(far, 2)]
     near, back, kept = terms(1, [jnp.bfloat16, jnp.bfloat16, jnp.float32])
     met += [beside(near, 1), beside(back, -1)]
-    product = pl.pallas_call(
+    product, base = pl.pallas_call(
         store_kernel,
-        out_shape=jax.ShapeDtypeStruct((W, width), jnp.bfloat16),
-        in_specs=[VMEM],
-        out_specs=HBM,
+        out_shape=(jax.ShapeDtypeStruct((W, width), jnp.bfloat16), jax.ShapeDtypeStruct((SLICE, width), jnp.float32)),
+        in_specs=[VMEM] * 3,
+        out_specs=(HBM, VMEM),
         scratch_shapes=[pltpu.SemaphoreType.DMA],
         compiler_params=pltpu.CompilerParams(vmem_limit_bytes=16 * MIB),
-        cost_estimate=pl.CostEstimate(flops=0, bytes_accessed=MIB, transcendentals=0),
-    )(own)
+        cost_estimate=pl.CostEstimate(flops=0, bytes_accessed=2 * MIB, transcendentals=0),
+    )(own, diag_in[0], kept)
     diagonal = pl.pallas_call(
         sum_kernel,
         out_shape=jax.ShapeDtypeStruct((SLICE, width), jnp.float32),
-        in_specs=[VMEM] * (chips + 1),
-        out_specs=VMEM,
+        in_specs=[VMEM] * chips,
+        out_specs=HBM,
+        scratch_shapes=[pltpu.VMEM((SLICE, width), jnp.float32), pltpu.SemaphoreType.DMA((4,))],
         compiler_params=pltpu.CompilerParams(vmem_limit_bytes=16 * MIB),
         cost_estimate=pl.CostEstimate(flops=0, bytes_accessed=2 * MIB, transcendentals=0),
-    )(diag_in[0], kept, *met)
+    )(base, *met)
     return (product[None, None], diagonal[None])
 
 

time: 141 us -> 141 us (level)
  no operation moved by 1% of the time
where the time goes in v8:
time: 141 us; the launch traced here: 140 us
  waiting for transfers between devices  81.2 us (58%)
  starting transfers between devices  46.5 us (33%)
  Pallas kernels  9.18 us (7%)
  local copies, waits for them, and re-layouts  2.3 us (2%)
    all_to_all x1, waiting for transfers between devices, local(): lax.all_to_all(sending, 'pcol', split_axis=0, concat_axis=0, tiled=True)  51 us
    ppermute x4, waiting for transfers between devices, shift(): lax.ppermute(x, 'prow', [(i, (i + 2 * h) % rows) for i in range(rows)])  19 us
    all_to_all x1, starting transfers between devices, local(): lax.all_to_all(sending, 'pcol', split_axis=0, concat_axis=0, tiled=True)  15.6 us
    ppermute x4, starting transfers between devices, shift(): lax.ppermute(x, 'prow', [(i, (i + 2 * h) % rows) for i in range(rows)])  15.5 us
    ppermute x2, starting transfers between devices, swap(): return lax.ppermute(x, 'prow', [(i, i ^ 1) for i in range(rows)])  10.1 us
    ppermute x2, waiting for transfers between devices, beside(): return lax.ppermute(x, 'prow', pairs)  6.12 us
    ppermute x2, starting transfers between devices, beside(): return lax.ppermute(x, 'prow', pairs)  5.28 us
    ppermute x2, waiting for transfers between devices, swap(): return lax.ppermute(x, 'prow', [(i, i ^ 1) for i in range(rows)])  5.08 us
  transfers between devices with their start and end apart: 9, of which 8 were waited for; matrix products, arithmetic and copies ran while one was open for 0% of the time, Pallas kernels for 2%

profile of v8, /device:TPU:1, one launch (start us, length us, event | category | flops | bytes accessed | tf_op | source)
XLA Modules:
  0.0 140.3 jit_solution(15497425845582941126)
XLA Ops:
  0.6 2.5 %shard_map.68 = bf16[16,256,256]{2,1,0:T(8,128)(2,1)} custom-call(s32[8,16]{1,0:T(8,128)} %bitcast.14, bf16[1024,512]{1,0:T(8,128)(2,1)} %a_ref.1), custom_call_target="tpu_custom_call" | custom-call | bytes 3145728 | tf_op jit(solution)/shard_map/pallas_call | solution.py:155
  3.2 15.6 %all-to-all-start = ((bf16[16,256,256]{2,1,0:T(8,128)(2,1)}), bf16[16,256,256]{2,1,0:T(8,128)(2,1)S(1)}, u32[]{:S(2)}, u32[]{:S(2)}) async-start(bf16[16,256,256]{2,1,0:T(8,128)(2,1)} %shard_map.68), calls=%async_computation | async-start | bytes 4194304 | tf_op jit(solution)/shard_map/all_to_all | solution.py:170
  18.7 3.2 %collective-permute-start = (bf16[256,1024]{1,0:T(8,128)(2,1)S(1)}, bf16[256,1024]{1,0:T(8,128)(2,1)S(1)}, u32[]{:S(2)}, u32[]{:S(2)}) collective-permute-start(bf16[256,1024]{1,0:T(8,128)(2,1)S(1)} %bitcast.16), channel_id=1, source_target_pairs={{0,32},{16,48},{32,64},{48,80},{64,96},{80,112},{96,0},{112,16},{1... | collective-permute-start | bytes 1572872 | tf_op jit(solution)/shard_map/ppermute | solution.py:150
  22.0 4.5 %collective-permute-start.1 = (bf16[256,1024]{1,0:T(8,128)(2,1)S(1)}, bf16[256,1024]{1,0:T(8,128)(2,1)S(1)}, u32[]{:S(2)}, u32[]{:S(2)}) collective-permute-start(bf16[256,1024]{1,0:T(8,128)(2,1)S(1)} %bitcast.17), channel_id=1, source_target_pairs={{0,64},{16,80},{32,96},{48,112},{64,0},{80,16},{96,32},{112,48},{1... | collective-permute-start | bytes 1572872 | tf_op jit(solution)/shard_map/ppermute | solution.py:150
  26.5 3.0 %collective-permute-start.2 = (bf16[256,1024]{1,0:T(8,128)(2,1)S(1)}, bf16[256,1024]{1,0:T(8,128)(2,1)S(1)}, u32[]{:S(2)}, u32[]{:S(2)}) collective-permute-start(bf16[256,1024]{1,0:T(8,128)(2,1)S(1)} %bitcast.18), channel_id=1, source_target_pairs={{0,96},{16,112},{32,0},{48,16},{64,32},{80,48},{96,64},{112,80},{1... | collective-permute-start | bytes 1572872 | tf_op jit(solution)/shard_map/ppermute | solution.py:150
  29.5 5.0 %collective-permute-done = bf16[256,1024]{1,0:T(8,128)(2,1)S(1)} collective-permute-done((bf16[256,1024]{1,0:T(8,128)(2,1)S(1)}, bf16[256,1024]{1,0:T(8,128)(2,1)S(1)}, u32[]{:S(2)}, u32[]{:S(2)}) %collective-permute-start) | collective-permute-done | bytes 524320 | tf_op jit(solution)/shard_map/ppermute | solution.py:150
  34.5 12.3 %collective-permute-done.1 = bf16[256,1024]{1,0:T(8,128)(2,1)S(1)} collective-permute-done((bf16[256,1024]{1,0:T(8,128)(2,1)S(1)}, bf16[256,1024]{1,0:T(8,128)(2,1)S(1)}, u32[]{:S(2)}, u32[]{:S(2)}) %collective-permute-start.1) | collective-permute-done | bytes 524320 | tf_op jit(solution)/shard_map/ppermute | solution.py:150
  46.8 1.7 %collective-permute-done.2 = bf16[256,1024]{1,0:T(8,128)(2,1)S(1)} collective-permute-done((bf16[256,1024]{1,0:T(8,128)(2,1)S(1)}, bf16[256,1024]{1,0:T(8,128)(2,1)S(1)}, u32[]{:S(2)}, u32[]{:S(2)}) %collective-permute-start.2) | collective-permute-done | bytes 524320 | tf_op jit(solution)/shard_map/ppermute | solution.py:150
  48.5 0.3 pad_maximum_fusion
  48.7 3.5 %collective-permute-start.3 = (bf16[4,256,1024]{2,1,0:T(8,128)(2,1)S(1)}, bf16[4,256,1024]{2,1,0:T(8,128)(2,1)S(1)}, u32[]{:S(2)}, u32[]{:S(2)}) collective-permute-start(bf16[4,256,1024]{2,1,0:T(8,128)(2,1)S(1)} %pad_maximum_fusion), channel_id=1, source_target_pairs={{0,16},{16,0},{32,48},{48,32},{64,80},{80,64},{96,112},{112,96},{1... | collective-permute-start | bytes 6291464 | tf_op jit(solution)/shard_map/ppermute | solution.py:153
  52.4 0.0 copy-start.1
  52.4 0.0 copy-start.2
  52.4 3.6 %collective-permute-done.3 = bf16[4,256,1024]{2,1,0:T(8,128)(2,1)S(1)} collective-permute-done((bf16[4,256,1024]{2,1,0:T(8,128)(2,1)S(1)}, bf16[4,256,1024]{2,1,0:T(8,128)(2,1)S(1)}, u32[]{:S(2)}, u32[]{:S(2)}) %collective-permute-start.3) | collective-permute-done | bytes 2097184 | tf_op jit(solution)/shard_map/ppermute | solution.py:153
  56.0 0.2 constant_dynamic-update-slice_fusion.f_ref
  56.2 2.0 %copy-done.3 = bf16[8,256,1024]{2,1,0:T(8,128)(2,1)} copy-done((bf16[8,256,1024]{2,1,0:T(8,128)(2,1)}, bf16[8,256,1024]{2,1,0:T(8,128)(2,1)S(1)}, u32[]{:S(2)}) %copy-start.3) | copy-done | bytes 4194328
  58.1 1.4 %shard_map.69.turned_ref = bf16[512,512]{1,0:T(8,128)(2,1)S(1)} custom-call(bf16[8,256,1024]{2,1,0:T(8,128)(2,1)} %copy-done.3), custom_call_target="tpu_custom_call" | custom-call | bytes 2097152 | tf_op jit(solution)/shard_map/pallas_call | solution.py:174
  59.5 0.0 copy-start
  59.5 51.0 %all-to-all-done.a_ref = bf16[16,256,256]{2,1,0:T(8,128)(2,1)S(1)} async-done(((bf16[16,256,256]{2,1,0:T(8,128)(2,1)}), bf16[16,256,256]{2,1,0:T(8,128)(2,1)S(1)}, u32[]{:S(2)}, u32[]{:S(2)}) %all-to-all-start) | async-done | bytes 2097184 | tf_op jit(solution)/shard_map/all_to_all | solution.py:170
  110.6 0.0 copy-done.1
  110.6 2.7 %shard_map.70.own_ref = bf16[256,1024]{1,0:T(8,128)(2,1)S(1)} custom-call(s32[8,16]{1,0:T(8,128)S(1)} %bitcast.15, s32[16]{0:T(128)S(1)} %copy-done.2, bf16[16,256,256]{2,1,0:T(8,128)(2,1)S(1)} %all-to-all-done.a_ref, bf16[8,256,1024]{2,1,0:T(8,128)(2,1)} %copy-done.3), custom_call_target="tpu_custom_call" | custom-call | flops 1073741824 | bytes 7340032 | tf_op jit(solution)/shard_map/pallas_call | solution.py:185
  113.3 6.6 %collective-permute-start.4 = (bf16[256,1024]{1,0:T(8,128)(2,1)S(1)}, bf16[256,1024]{1,0:T(8,128)(2,1)S(1)}, u32[]{:S(2)}, u32[]{:S(2)}) collective-permute-start(bf16[256,1024]{1,0:T(8,128)(2,1)S(1)} %shard_map.70.own_ref), channel_id=1, source_target_pairs={{0,16},{16,0},{32,48},{48,32},{64,80},{80,64},{96,112},{112,96},{1... | collective-permute-start | bytes 1572872 | tf_op jit(solution)/shard_map/ppermute | solution.py:153
  119.9 1.5 %collective-permute-done.4.other_ref = bf16[256,1024]{1,0:T(8,128)(2,1)S(1)} collective-permute-done((bf16[256,1024]{1,0:T(8,128)(2,1)S(1)}, bf16[256,1024]{1,0:T(8,128)(2,1)S(1)}, u32[]{:S(2)}, u32[]{:S(2)}) %collective-permute-start.4) | collective-permute-done | bytes 524320 | tf_op jit(solution)/shard_map/ppermute | solution.py:153
  121.5 0.3 shard_map.73
  121.8 4.8 %collective-permute-start.5 = (bf16[128,1024]{1,0:T(8,128)(2,1)S(1)}, bf16[128,1024]{1,0:T(8,128)(2,1)S(1)}, u32[]{:S(2)}, u32[]{:S(2)}) collective-permute-start(bf16[128,1024]{1,0:T(8,128)(2,1)S(1)} %shard_map.73), channel_id=1, source_target_pairs={{0,64},{16,80},{32,96},{48,112},{64,0},{80,16},{96,32},{112,48},{1... | collective-permute-start | bytes 786440 | tf_op jit(solution)/shard_map/ppermute | solution.py:150
  126.6 0.6 shard_map.71
  127.2 2.7 %collective-permute-start.6 = (bf16[128,1024]{1,0:T(8,128)(2,1)S(1)}, bf16[128,1024]{1,0:T(8,128)(2,1)S(1)}, u32[]{:S(2)}, u32[]{:S(2)}) collective-permute-start(bf16[128,1024]{1,0:T(8,128)(2,1)S(1)} %get-tuple-element.14), channel_id=1, source_target_pairs={{0,32},{16,112},{32,64},{48,16},{64,96},{80,48},{96,0},{112,80},{1... | collective-permute-start | bytes 786440 | tf_op jit(solution)/shard_map/ppermute | solution.py:218
  129.9 2.6 %collective-permute-start.7 = (bf16[128,1024]{1,0:T(8,128)(2,1)S(1)}, bf16[128,1024]{1,0:T(8,128)(2,1)S(1)}, u32[]{:S(2)}, u32[]{:S(2)}) collective-permute-start(bf16[128,1024]{1,0:T(8,128)(2,1)S(1)} %get-tuple-element.15), channel_id=1, source_target_pairs={{0,96},{16,48},{32,0},{48,80},{64,32},{80,112},{96,64},{112,16},{1... | collective-permute-start | bytes 786440 | tf_op jit(solution)/shard_map/ppermute | solution.py:218
  132.5 0.8 shard_map.72
  133.3 0.0 collective-permute-done.5.refs_0_
  133.3 4.4 %collective-permute-done.6.refs_1_ = bf16[128,1024]{1,0:T(8,128)(2,1)S(1)} collective-permute-done((bf16[128,1024]{1,0:T(8,128)(2,1)S(1)}, bf16[128,1024]{1,0:T(8,128)(2,1)S(1)}, u32[]{:S(2)}, u32[]{:S(2)}) %collective-permute-start.6) | collective-permute-done | bytes 262176 | tf_op jit(solution)/shard_map/ppermute | solution.py:218
  137.8 1.7 %collective-permute-done.7.refs_2_ = bf16[128,1024]{1,0:T(8,128)(2,1)S(1)} collective-permute-done((bf16[128,1024]{1,0:T(8,128)(2,1)S(1)}, bf16[128,1024]{1,0:T(8,128)(2,1)S(1)}, u32[]{:S(2)}, u32[]{:S(2)}) %collective-permute-start.7) | collective-permute-done | bytes 262176 | tf_op jit(solution)/shard_map/ppermute | solution.py:218
  139.4 0.8 shard_map.74
  (9 shorter events, 0.2 us)
Async XLA Ops:
  0.6 18.1 %copy-start.4 = (bf16[1,1,256,1024]{3,2,1,0:T(8,128)(2,1)S(1)}, bf16[1,1,256,1024]{3,2,1,0:T(8,128)(2,1)}, u32[]{:S(2)}) copy-start(bf16[1,1,256,1024]{3,2,1,0:T(8,128)(2,1)} %param.6) | copy-start | bytes 1572868
  3.2 107.4 %all-to-all-start = ((bf16[16,256,256]{2,1,0:T(8,128)(2,1)}), bf16[16,256,256]{2,1,0:T(8,128)(2,1)S(1)}, u32[]{:S(2)}, u32[]{:S(2)}) async-start(bf16[16,256,256]{2,1,0:T(8,128)(2,1)} %shard_map.68), calls=%async_computation | async-start | bytes 4194304 | tf_op jit(solution)/shard_map/all_to_all | solution.py:170
  18.7 15.7 %collective-permute-start = (bf16[256,1024]{1,0:T(8,128)(2,1)S(1)}, bf16[256,1024]{1,0:T(8,128)(2,1)S(1)}, u32[]{:S(2)}, u32[]{:S(2)}) collective-permute-start(bf16[256,1024]{1,0:T(8,128)(2,1)S(1)} %bitcast.16), channel_id=1, source_target_pairs={{0,32},{16,48},{32,64},{48,80},{64,96},{80,112},{96,0},{112,16},{1... | collective-permute-start | bytes 1572872 | tf_op jit(solution)/shard_map/ppermute | solution.py:150
  22.0 24.8 %collective-permute-start.1 = (bf16[256,1024]{1,0:T(8,128)(2,1)S(1)}, bf16[256,1024]{1,0:T(8,128)(2,1)S(1)}, u32[]{:S(2)}, u32[]{:S(2)}) collective-permute-start(bf16[256,1024]{1,0:T(8,128)(2,1)S(1)} %bitcast.17), channel_id=1, source_target_pairs={{0,64},{16,80},{32,96},{48,112},{64,0},{80,16},{96,32},{112,48},{1... | collective-permute-start | bytes 1572872 | tf_op jit(solution)/shard_map/ppermute | solution.py:150
  26.5 22.0 %collective-permute-start.2 = (bf16[256,1024]{1,0:T(8,128)(2,1)S(1)}, bf16[256,1024]{1,0:T(8,128)(2,1)S(1)}, u32[]{:S(2)}, u32[]{:S(2)}) collective-permute-start(bf16[256,1024]{1,0:T(8,128)(2,1)S(1)} %bitcast.18), channel_id=1, source_target_pairs={{0,96},{16,112},{32,0},{48,16},{64,32},{80,48},{96,64},{112,80},{1... | collective-permute-start | bytes 1572872 | tf_op jit(solution)/shard_map/ppermute | solution.py:150
  48.7 7.2 %collective-permute-start.3 = (bf16[4,256,1024]{2,1,0:T(8,128)(2,1)S(1)}, bf16[4,256,1024]{2,1,0:T(8,128)(2,1)S(1)}, u32[]{:S(2)}, u32[]{:S(2)}) collective-permute-start(bf16[4,256,1024]{2,1,0:T(8,128)(2,1)S(1)} %pad_maximum_fusion), channel_id=1, source_target_pairs={{0,16},{16,0},{32,48},{48,32},{64,80},{80,64},{96,112},{112,96},{1... | collective-permute-start | bytes 6291464 | tf_op jit(solution)/shard_map/ppermute | solution.py:153
  52.4 58.2 %copy-start.1 = (s32[16,8]{0,1:T(8,128)S(1)}, s32[16,8]{0,1:T(8,128)}, u32[]{:S(2)}) copy-start(s32[16,8]{0,1:T(8,128)} %param.8) | copy-start | bytes 1540
  52.4 58.2 %copy-start.2 = (s32[16]{0:T(128)S(1)}, s32[16]{0:T(128)}, u32[]{:S(2)}) copy-start(s32[16]{0:T(128)} %count_ref.1) | copy-start | bytes 196
  56.2 2.0 %copy-start.3 = (bf16[8,256,1024]{2,1,0:T(8,128)(2,1)}, bf16[8,256,1024]{2,1,0:T(8,128)(2,1)S(1)}, u32[]{:S(2)}) copy-start(bf16[8,256,1024]{2,1,0:T(8,128)(2,1)S(1)} %constant_dynamic-update-slice_fusion.f_ref) | copy-start | bytes 12582916
  59.5 73.0 %copy-start = (f32[1,128,1024]{2,1,0:T(8,128)S(1)}, f32[1,128,1024]{2,1,0:T(8,128)}, u32[]{:S(2)}) copy-start(f32[1,128,1024]{2,1,0:T(8,128)} %param.7) | copy-start | bytes 1572868
  113.3 8.2 %collective-permute-start.4 = (bf16[256,1024]{1,0:T(8,128)(2,1)S(1)}, bf16[256,1024]{1,0:T(8,128)(2,1)S(1)}, u32[]{:S(2)}, u32[]{:S(2)}) collective-permute-start(bf16[256,1024]{1,0:T(8,128)(2,1)S(1)} %shard_map.70.own_ref), channel_id=1, source_target_pairs={{0,16},{16,0},{32,48},{48,32},{64,80},{80,64},{96,112},{112,96},{1... | collective-permute-start | bytes 1572872 | tf_op jit(solution)/shard_map/ppermute | solution.py:153
  121.8 11.5 %collective-permute-start.5 = (bf16[128,1024]{1,0:T(8,128)(2,1)S(1)}, bf16[128,1024]{1,0:T(8,128)(2,1)S(1)}, u32[]{:S(2)}, u32[]{:S(2)}) collective-permute-start(bf16[128,1024]{1,0:T(8,128)(2,1)S(1)} %shard_map.73), channel_id=1, source_target_pairs={{0,64},{16,80},{32,96},{48,112},{64,0},{80,16},{96,32},{112,48},{1... | collective-permute-start | bytes 786440 | tf_op jit(solution)/shard_map/ppermute | solution.py:150
  127.2 10.6 %collective-permute-start.6 = (bf16[128,1024]{1,0:T(8,128)(2,1)S(1)}, bf16[128,1024]{1,0:T(8,128)(2,1)S(1)}, u32[]{:S(2)}, u32[]{:S(2)}) collective-permute-start(bf16[128,1024]{1,0:T(8,128)(2,1)S(1)} %get-tuple-element.14), channel_id=1, source_target_pairs={{0,32},{16,112},{32,64},{48,16},{64,96},{80,48},{96,0},{112,80},{1... | collective-permute-start | bytes 786440 | tf_op jit(solution)/shard_map/ppermute | solution.py:218
  129.9 9.6 %collective-permute-start.7 = (bf16[128,1024]{1,0:T(8,128)(2,1)S(1)}, bf16[128,1024]{1,0:T(8,128)(2,1)S(1)}, u32[]{:S(2)}, u32[]{:S(2)}) collective-permute-start(bf16[128,1024]{1,0:T(8,128)(2,1)S(1)} %get-tuple-element.15), channel_id=1, source_target_pairs={{0,96},{16,48},{32,0},{48,80},{64,32},{80,112},{96,64},{112,16},{1... | collective-permute-start | bytes 786440 | tf_op jit(solution)/shard_map/ppermute | solution.py:218

commit v9 on v8

--- a/solution.py
+++ b/solution.py
@@ -40,8 +40,7 @@
         pl.when(owed)(store.wait)
 
 
-def product_kernel(rows, cols, anc_ref, count_ref, a_ref, f_ref, own_ref, held, factors, total, sems, names, counts, small_sems):
-    half = rows // 2
+def product_kernel(rows, cols, anc_ref, count_ref, a_ref, mine_ref, f_ref, own_ref, held, factors, total, sems, names, counts, small_sems):
     width = own_ref.shape[-1]
     step = 256
     small = [
@@ -51,8 +50,8 @@
     for fetch in small:
         fetch.start()
     loads = []
-    for n in range(rows):
-        load = pltpu.make_async_copy(f_ref.at[n], factors.at[n], sems.at[n])
+    for n in range(1, rows):
+        load = pltpu.make_async_copy(f_ref.at[n], factors.at[pl.ds((n - 1) * W, W)], sems.at[n - 1])
         load.start()
         loads.append(load)
     me_row = lax.axis_index("prow")
@@ -61,20 +60,30 @@
         fetch.wait()
     count = counts[me_col]
     row_live = (me_row < count).astype(jnp.float32)
-    for n in range(rows):
+
+    def hold(n):
         t = slot_row(me_row, n, rows)
         live = (t < count).astype(jnp.bfloat16)
-        held[n] = a_ref[lax.rem(names[t, me_col], cols)] * live
-    for n in range(0, rows, 2):
-        for load in loads[n : n + 2]:
+        held[:, n * W : (n + 1) * W] = a_ref[lax.rem(names[t, me_col], cols)] * live
+
+    hold(0)
+    for q in range(width // step):
+        at = pl.ds(q * step, step)
+        total[:, at] = jnp.dot(held[:, 0:W], mine_ref[:, at], preferred_element_type=jnp.float32)
+    for n in range(1, rows):
+        hold(n)
+    for n in range(1, rows, 2):
+        size = min(2, rows - n)
+        for load in loads[n - 1 : n - 1 + size]:
             load.wait()
         for q in range(width // step):
             at = pl.ds(q * step, step)
-            part = jnp.dot(held[n], factors[n, :, at], preferred_element_type=jnp.float32)
-            part += jnp.dot(held[n + 1], factors[n + 1, :, at], preferred_element_type=jnp.float32)
-            if n > 0:
-                part += total[:, at]
-            if n < rows - 2:
+            part = total[:, at] + jnp.dot(
+                held[:, n * W : (n + size) * W],
+                factors[(n - 1) * W : (n - 1 + size) * W, at],
+                preferred_element_type=jnp.float32,
+            )
+            if n + size < rows:
                 total[:, at] = part
             else:
                 own_ref[:, at] = (part * -row_live).astype(jnp.bfloat16)
@@ -185,20 +194,20 @@
     own = pl.pallas_call(
         functools.partial(product_kernel, rows, cols),
         out_shape=jax.ShapeDtypeStruct((W, width), jnp.bfloat16),
-        in_specs=[HBM, HBM, VMEM, HBM],
+        in_specs=[HBM, HBM, VMEM, VMEM, HBM],
         out_specs=VMEM,
         scratch_shapes=[
-            pltpu.VMEM((rows, W, W), jnp.bfloat16),
-            pltpu.VMEM((rows, W, width), jnp.bfloat16),
+            pltpu.VMEM((W, rows * W), jnp.bfloat16),
+            pltpu.VMEM(((rows - 1) * W, width), jnp.bfloat16),
             pltpu.VMEM((W, width), jnp.float32),
-            pltpu.SemaphoreType.DMA((rows,)),
+            pltpu.SemaphoreType.DMA((rows - 1,)),
             pltpu.SMEM((rows, cols), jnp.int32),
             pltpu.SMEM((cols,), jnp.int32),
             pltpu.SemaphoreType.DMA((2,)),
         ],
         compiler_params=pltpu.CompilerParams(vmem_limit_bytes=50 * MIB),
         cost_estimate=pl.CostEstimate(flops=2 * rows * W * W * width, bytes_accessed=7 * MIB, transcendentals=0),
-    )(lists, active_count, arrived, factors)
+    )(lists, active_count, arrived, factor, factors)
     other = swap(own)
 
     def terms(base, dtypes):

time: 141 us -> 141 us (level)
  no operation moved by 1% of the time
where the time goes in v9:
time: 141 us; the launch traced here: 140 us
  waiting for transfers between devices  81.2 us (58%)
  starting transfers between devices  46.8 us (33%)
  Pallas kernels  8.94 us (6%)
  local copies, waits for them, and re-layouts  2.3 us (2%)
    all_to_all x1, waiting for transfers between devices, local(): lax.all_to_all(sending, 'pcol', split_axis=0, concat_axis=0, tiled=True)  51 us
    ppermute x4, waiting for transfers between devices, shift(): lax.ppermute(x, 'prow', [(i, (i + 2 * h) % rows) for i in range(rows)])  19 us
    all_to_all x1, starting transfers between devices, local(): lax.all_to_all(sending, 'pcol', split_axis=0, concat_axis=0, tiled=True)  15.9 us
    ppermute x4, starting transfers between devices, shift(): lax.ppermute(x, 'prow', [(i, (i + 2 * h) % rows) for i in range(rows)])  15.5 us
    ppermute x2, starting transfers between devices, swap(): return lax.ppermute(x, 'prow', [(i, i ^ 1) for i in range(rows)])  10.1 us
    ppermute x2, waiting for transfers between devices, beside(): return lax.ppermute(x, 'prow', pairs)  6.11 us
    ppermute x2, starting transfers between devices, beside(): return lax.ppermute(x, 'prow', pairs)  5.28 us
    ppermute x2, waiting for transfers between devices, swap(): return lax.ppermute(x, 'prow', [(i, i ^ 1) for i in range(rows)])  5.08 us
  transfers between devices with their start and end apart: 9, of which 8 were waited for; matrix products, arithmetic and copies ran while one was open for 0% of the time, Pallas kernels for 2%

profile of v9, /device:TPU:1, one launch (start us, length us, event | category | flops | bytes accessed | tf_op | source)
XLA Modules:
  0.0 140.4 jit_solution(13191781457473397700)
XLA Ops:
  0.6 0.0 copy-start
  0.6 2.4 %shard_map.68 = bf16[16,256,256]{2,1,0:T(8,128)(2,1)} custom-call(s32[8,16]{1,0:T(8,128)} %bitcast.19, bf16[1024,512]{1,0:T(8,128)(2,1)} %a_ref.1), custom_call_target="tpu_custom_call" | custom-call | bytes 3145728 | tf_op jit(solution)/shard_map/pallas_call | solution.py:164
  3.0 15.9 %all-to-all-start = ((bf16[16,256,256]{2,1,0:T(8,128)(2,1)}), bf16[16,256,256]{2,1,0:T(8,128)(2,1)S(1)}, u32[]{:S(2)}, u32[]{:S(2)}) async-start(bf16[16,256,256]{2,1,0:T(8,128)(2,1)} %shard_map.68), calls=%async_computation | async-start | bytes 4194304 | tf_op jit(solution)/shard_map/all_to_all | solution.py:179
  18.9 0.0 copy-done
  18.9 3.2 %collective-permute-start = (bf16[256,1024]{1,0:T(8,128)(2,1)S(1)}, bf16[256,1024]{1,0:T(8,128)(2,1)S(1)}, u32[]{:S(2)}, u32[]{:S(2)}) collective-permute-start(bf16[256,1024]{1,0:T(8,128)(2,1)S(1)} %bitcast.13), channel_id=1, source_target_pairs={{0,32},{16,48},{32,64},{48,80},{64,96},{80,112},{96,0},{112,16},{1... | collective-permute-start | bytes 1572872 | tf_op jit(solution)/shard_map/ppermute | solution.py:159
  22.1 4.5 %collective-permute-start.1 = (bf16[256,1024]{1,0:T(8,128)(2,1)S(1)}, bf16[256,1024]{1,0:T(8,128)(2,1)S(1)}, u32[]{:S(2)}, u32[]{:S(2)}) collective-permute-start(bf16[256,1024]{1,0:T(8,128)(2,1)S(1)} %bitcast.14), channel_id=1, source_target_pairs={{0,64},{16,80},{32,96},{48,112},{64,0},{80,16},{96,32},{112,48},{1... | collective-permute-start | bytes 1572872 | tf_op jit(solution)/shard_map/ppermute | solution.py:159
  26.7 3.0 %collective-permute-start.2 = (bf16[256,1024]{1,0:T(8,128)(2,1)S(1)}, bf16[256,1024]{1,0:T(8,128)(2,1)S(1)}, u32[]{:S(2)}, u32[]{:S(2)}) collective-permute-start(bf16[256,1024]{1,0:T(8,128)(2,1)S(1)} %bitcast.15), channel_id=1, source_target_pairs={{0,96},{16,112},{32,0},{48,16},{64,32},{80,48},{96,64},{112,80},{1... | collective-permute-start | bytes 1572872 | tf_op jit(solution)/shard_map/ppermute | solution.py:159
  29.7 5.0 %collective-permute-done = bf16[256,1024]{1,0:T(8,128)(2,1)S(1)} collective-permute-done((bf16[256,1024]{1,0:T(8,128)(2,1)S(1)}, bf16[256,1024]{1,0:T(8,128)(2,1)S(1)}, u32[]{:S(2)}, u32[]{:S(2)}) %collective-permute-start) | collective-permute-done | bytes 524320 | tf_op jit(solution)/shard_map/ppermute | solution.py:159
  34.7 12.3 %collective-permute-done.1 = bf16[256,1024]{1,0:T(8,128)(2,1)S(1)} collective-permute-done((bf16[256,1024]{1,0:T(8,128)(2,1)S(1)}, bf16[256,1024]{1,0:T(8,128)(2,1)S(1)}, u32[]{:S(2)}, u32[]{:S(2)}) %collective-permute-start.1) | collective-permute-done | bytes 524320 | tf_op jit(solution)/shard_map/ppermute | solution.py:159
  47.0 1.7 %collective-permute-done.2 = bf16[256,1024]{1,0:T(8,128)(2,1)S(1)} collective-permute-done((bf16[256,1024]{1,0:T(8,128)(2,1)S(1)}, bf16[256,1024]{1,0:T(8,128)(2,1)S(1)}, u32[]{:S(2)}, u32[]{:S(2)}) %collective-permute-start.2) | collective-permute-done | bytes 524320 | tf_op jit(solution)/shard_map/ppermute | solution.py:159
  48.7 0.3 pad_maximum_fusion
  48.9 3.5 %collective-permute-start.3 = (bf16[4,256,1024]{2,1,0:T(8,128)(2,1)S(1)}, bf16[4,256,1024]{2,1,0:T(8,128)(2,1)S(1)}, u32[]{:S(2)}, u32[]{:S(2)}) collective-permute-start(bf16[4,256,1024]{2,1,0:T(8,128)(2,1)S(1)} %pad_maximum_fusion), channel_id=1, source_target_pairs={{0,16},{16,0},{32,48},{48,32},{64,80},{80,64},{96,112},{112,96},{1... | collective-permute-start | bytes 6291464 | tf_op jit(solution)/shard_map/ppermute | solution.py:162
  52.6 0.0 copy-start.2
  52.6 0.0 copy-start.3
  52.6 3.6 %collective-permute-done.3 = bf16[4,256,1024]{2,1,0:T(8,128)(2,1)S(1)} collective-permute-done((bf16[4,256,1024]{2,1,0:T(8,128)(2,1)S(1)}, bf16[4,256,1024]{2,1,0:T(8,128)(2,1)S(1)}, u32[]{:S(2)}, u32[]{:S(2)}) %collective-permute-start.3) | collective-permute-done | bytes 2097184 | tf_op jit(solution)/shard_map/ppermute | solution.py:162
  56.2 0.2 constant_dynamic-update-slice_fusion.f_ref
  56.4 2.0 %copy-done.4 = bf16[8,256,1024]{2,1,0:T(8,128)(2,1)} copy-done((bf16[8,256,1024]{2,1,0:T(8,128)(2,1)}, bf16[8,256,1024]{2,1,0:T(8,128)(2,1)S(1)}, u32[]{:S(2)}) %copy-start.4) | copy-done | bytes 4194328
  58.3 1.4 %shard_map.69.turned_ref = bf16[512,512]{1,0:T(8,128)(2,1)S(1)} custom-call(bf16[8,256,1024]{2,1,0:T(8,128)(2,1)} %copy-done.4), custom_call_target="tpu_custom_call" | custom-call | bytes 2097152 | tf_op jit(solution)/shard_map/pallas_call | solution.py:183
  59.7 51.0 %all-to-all-done.a_ref = bf16[16,256,256]{2,1,0:T(8,128)(2,1)S(1)} async-done(((bf16[16,256,256]{2,1,0:T(8,128)(2,1)}), bf16[16,256,256]{2,1,0:T(8,128)(2,1)S(1)}, u32[]{:S(2)}, u32[]{:S(2)}) %all-to-all-start) | async-done | bytes 2097184 | tf_op jit(solution)/shard_map/all_to_all | solution.py:179
  110.8 2.6 %shard_map.70.own_ref = bf16[256,1024]{1,0:T(8,128)(2,1)S(1)} custom-call(s32[8,16]{1,0:T(8,128)S(1)} %bitcast.20, s32[16]{0:T(128)S(1)} %copy-done.3, bf16[16,256,256]{2,1,0:T(8,128)(2,1)S(1)} %all-to-all-done.a_ref, bf16[256,1024]{1,0:T(8,128)(2,1)S(1)} %bitcast.17, bf16[8,256,1024]{2,1,0:T(8,128)(2,1)} %copy-done.4), custom_call_target="tpu_custom_call" | custom-call | flops 1073741824 | bytes 7340032 | tf_op jit(solution)/shard_map/pallas_call | solution.py:194
  113.4 6.6 %collective-permute-start.4 = (bf16[256,1024]{1,0:T(8,128)(2,1)S(1)}, bf16[256,1024]{1,0:T(8,128)(2,1)S(1)}, u32[]{:S(2)}, u32[]{:S(2)}) collective-permute-start(bf16[256,1024]{1,0:T(8,128)(2,1)S(1)} %shard_map.70.own_ref), channel_id=1, source_target_pairs={{0,16},{16,0},{32,48},{48,32},{64,80},{80,64},{96,112},{112,96},{1... | collective-permute-start | bytes 1572872 | tf_op jit(solution)/shard_map/ppermute | solution.py:162
  120.0 1.5 %collective-permute-done.4.other_ref = bf16[256,1024]{1,0:T(8,128)(2,1)S(1)} collective-permute-done((bf16[256,1024]{1,0:T(8,128)(2,1)S(1)}, bf16[256,1024]{1,0:T(8,128)(2,1)S(1)}, u32[]{:S(2)}, u32[]{:S(2)}) %collective-permute-start.4) | collective-permute-done | bytes 524320 | tf_op jit(solution)/shard_map/ppermute | solution.py:162
  121.6 0.3 shard_map.73
  121.9 4.8 %collective-permute-start.5 = (bf16[128,1024]{1,0:T(8,128)(2,1)S(1)}, bf16[128,1024]{1,0:T(8,128)(2,1)S(1)}, u32[]{:S(2)}, u32[]{:S(2)}) collective-permute-start(bf16[128,1024]{1,0:T(8,128)(2,1)S(1)} %shard_map.73), channel_id=1, source_target_pairs={{0,64},{16,80},{32,96},{48,112},{64,0},{80,16},{96,32},{112,48},{1... | collective-permute-start | bytes 786440 | tf_op jit(solution)/shard_map/ppermute | solution.py:159
  126.7 0.6 shard_map.71
  127.3 2.7 %collective-permute-start.6 = (bf16[128,1024]{1,0:T(8,128)(2,1)S(1)}, bf16[128,1024]{1,0:T(8,128)(2,1)S(1)}, u32[]{:S(2)}, u32[]{:S(2)}) collective-permute-start(bf16[128,1024]{1,0:T(8,128)(2,1)S(1)} %get-tuple-element.14), channel_id=1, source_target_pairs={{0,32},{16,112},{32,64},{48,16},{64,96},{80,48},{96,0},{112,80},{1... | collective-permute-start | bytes 786440 | tf_op jit(solution)/shard_map/ppermute | solution.py:227
  130.0 2.6 %collective-permute-start.7 = (bf16[128,1024]{1,0:T(8,128)(2,1)S(1)}, bf16[128,1024]{1,0:T(8,128)(2,1)S(1)}, u32[]{:S(2)}, u32[]{:S(2)}) collective-permute-start(bf16[128,1024]{1,0:T(8,128)(2,1)S(1)} %get-tuple-element.15), channel_id=1, source_target_pairs={{0,96},{16,48},{32,0},{48,80},{64,32},{80,112},{96,64},{112,16},{1... | collective-permute-start | bytes 786440 | tf_op jit(solution)/shard_map/ppermute | solution.py:227
  132.6 0.8 shard_map.72
  133.4 0.0 collective-permute-done.5.refs_0_
  133.4 4.4 %collective-permute-done.6.refs_1_ = bf16[128,1024]{1,0:T(8,128)(2,1)S(1)} collective-permute-done((bf16[128,1024]{1,0:T(8,128)(2,1)S(1)}, bf16[128,1024]{1,0:T(8,128)(2,1)S(1)}, u32[]{:S(2)}, u32[]{:S(2)}) %collective-permute-start.6) | collective-permute-done | bytes 262176 | tf_op jit(solution)/shard_map/ppermute | solution.py:227
  137.9 1.7 %collective-permute-done.7.refs_2_ = bf16[128,1024]{1,0:T(8,128)(2,1)S(1)} collective-permute-done((bf16[128,1024]{1,0:T(8,128)(2,1)S(1)}, bf16[128,1024]{1,0:T(8,128)(2,1)S(1)}, u32[]{:S(2)}, u32[]{:S(2)}) %collective-permute-start.7) | collective-permute-done | bytes 262176 | tf_op jit(solution)/shard_map/ppermute | solution.py:227
  139.5 0.8 shard_map.74
  (9 shorter events, 0.2 us)
Async XLA Ops:
  0.6 18.3 %copy-start = (bf16[1,1,256,1024]{3,2,1,0:T(8,128)(2,1)S(1)}, bf16[1,1,256,1024]{3,2,1,0:T(8,128)(2,1)}, u32[]{:S(2)}) copy-start(bf16[1,1,256,1024]{3,2,1,0:T(8,128)(2,1)} %param.6) | copy-start | bytes 1572868
  3.0 107.8 %all-to-all-start = ((bf16[16,256,256]{2,1,0:T(8,128)(2,1)}), bf16[16,256,256]{2,1,0:T(8,128)(2,1)S(1)}, u32[]{:S(2)}, u32[]{:S(2)}) async-start(bf16[16,256,256]{2,1,0:T(8,128)(2,1)} %shard_map.68), calls=%async_computation | async-start | bytes 4194304 | tf_op jit(solution)/shard_map/all_to_all | solution.py:179
  18.9 15.7 %collective-permute-start = (bf16[256,1024]{1,0:T(8,128)(2,1)S(1)}, bf16[256,1024]{1,0:T(8,128)(2,1)S(1)}, u32[]{:S(2)}, u32[]{:S(2)}) collective-permute-start(bf16[256,1024]{1,0:T(8,128)(2,1)S(1)} %bitcast.13), channel_id=1, source_target_pairs={{0,32},{16,48},{32,64},{48,80},{64,96},{80,112},{96,0},{112,16},{1... | collective-permute-start | bytes 1572872 | tf_op jit(solution)/shard_map/ppermute | solution.py:159
  22.1 24.8 %collective-permute-start.1 = (bf16[256,1024]{1,0:T(8,128)(2,1)S(1)}, bf16[256,1024]{1,0:T(8,128)(2,1)S(1)}, u32[]{:S(2)}, u32[]{:S(2)}) collective-permute-start(bf16[256,1024]{1,0:T(8,128)(2,1)S(1)} %bitcast.14), channel_id=1, source_target_pairs={{0,64},{16,80},{32,96},{48,112},{64,0},{80,16},{96,32},{112,48},{1... | collective-permute-start | bytes 1572872 | tf_op jit(solution)/shard_map/ppermute | solution.py:159
  26.7 22.0 %collective-permute-start.2 = (bf16[256,1024]{1,0:T(8,128)(2,1)S(1)}, bf16[256,1024]{1,0:T(8,128)(2,1)S(1)}, u32[]{:S(2)}, u32[]{:S(2)}) collective-permute-start(bf16[256,1024]{1,0:T(8,128)(2,1)S(1)} %bitcast.15), channel_id=1, source_target_pairs={{0,96},{16,112},{32,0},{48,16},{64,32},{80,48},{96,64},{112,80},{1... | collective-permute-start | bytes 1572872 | tf_op jit(solution)/shard_map/ppermute | solution.py:159
  48.9 7.2 %collective-permute-start.3 = (bf16[4,256,1024]{2,1,0:T(8,128)(2,1)S(1)}, bf16[4,256,1024]{2,1,0:T(8,128)(2,1)S(1)}, u32[]{:S(2)}, u32[]{:S(2)}) collective-permute-start(bf16[4,256,1024]{2,1,0:T(8,128)(2,1)S(1)} %pad_maximum_fusion), channel_id=1, source_target_pairs={{0,16},{16,0},{32,48},{48,32},{64,80},{80,64},{96,112},{112,96},{1... | collective-permute-start | bytes 6291464 | tf_op jit(solution)/shard_map/ppermute | solution.py:162
  52.6 58.2 %copy-start.2 = (s32[16,8]{0,1:T(8,128)S(1)}, s32[16,8]{0,1:T(8,128)}, u32[]{:S(2)}) copy-start(s32[16,8]{0,1:T(8,128)} %param.8) | copy-start | bytes 1540
  52.6 58.2 %copy-start.3 = (s32[16]{0:T(128)S(1)}, s32[16]{0:T(128)}, u32[]{:S(2)}) copy-start(s32[16]{0:T(128)} %count_ref.1) | copy-start | bytes 196
  56.3 2.0 %copy-start.4 = (bf16[8,256,1024]{2,1,0:T(8,128)(2,1)}, bf16[8,256,1024]{2,1,0:T(8,128)(2,1)S(1)}, u32[]{:S(2)}) copy-start(bf16[8,256,1024]{2,1,0:T(8,128)(2,1)S(1)} %constant_dynamic-update-slice_fusion.f_ref) | copy-start | bytes 12582916
  110.8 21.8 %copy-start.1 = (f32[1,128,1024]{2,1,0:T(8,128)S(1)}, f32[1,128,1024]{2,1,0:T(8,128)}, u32[]{:S(2)}) copy-start(f32[1,128,1024]{2,1,0:T(8,128)} %param.7) | copy-start | bytes 1572868
  113.4 8.2 %collective-permute-start.4 = (bf16[256,1024]{1,0:T(8,128)(2,1)S(1)}, bf16[256,1024]{1,0:T(8,128)(2,1)S(1)}, u32[]{:S(2)}, u32[]{:S(2)}) collective-permute-start(bf16[256,1024]{1,0:T(8,128)(2,1)S(1)} %shard_map.70.own_ref), channel_id=1, source_target_pairs={{0,16},{16,0},{32,48},{48,32},{64,80},{80,64},{96,112},{112,96},{1... | collective-permute-start | bytes 1572872 | tf_op jit(solution)/shard_map/ppermute | solution.py:162
  121.9 11.6 %collective-permute-start.5 = (bf16[128,1024]{1,0:T(8,128)(2,1)S(1)}, bf16[128,1024]{1,0:T(8,128)(2,1)S(1)}, u32[]{:S(2)}, u32[]{:S(2)}) collective-permute-start(bf16[128,1024]{1,0:T(8,128)(2,1)S(1)} %shard_map.73), channel_id=1, source_target_pairs={{0,64},{16,80},{32,96},{48,112},{64,0},{80,16},{96,32},{112,48},{1... | collective-permute-start | bytes 786440 | tf_op jit(solution)/shard_map/ppermute | solution.py:159
  127.3 10.6 %collective-permute-start.6 = (bf16[128,1024]{1,0:T(8,128)(2,1)S(1)}, bf16[128,1024]{1,0:T(8,128)(2,1)S(1)}, u32[]{:S(2)}, u32[]{:S(2)}) collective-permute-start(bf16[128,1024]{1,0:T(8,128)(2,1)S(1)} %get-tuple-element.14), channel_id=1, source_target_pairs={{0,32},{16,112},{32,64},{48,16},{64,96},{80,48},{96,0},{112,80},{1... | collective-permute-start | bytes 786440 | tf_op jit(solution)/shard_map/ppermute | solution.py:227
  130.0 9.6 %collective-permute-start.7 = (bf16[128,1024]{1,0:T(8,128)(2,1)S(1)}, bf16[128,1024]{1,0:T(8,128)(2,1)S(1)}, u32[]{:S(2)}, u32[]{:S(2)}) collective-permute-start(bf16[128,1024]{1,0:T(8,128)(2,1)S(1)} %get-tuple-element.15), channel_id=1, source_target_pairs={{0,96},{16,48},{32,0},{48,80},{64,32},{80,112},{96,64},{112,16},{1... | collective-permute-start | bytes 786440 | tf_op jit(solution)/shard_map/ppermute | solution.py:227

commit v10 on v9

--- a/solution.py
+++ b/solution.py
@@ -226,10 +226,8 @@
             pairs.append((i, (i + way * (2 - 4 * (i % 2))) % rows))
         return lax.ppermute(x, "prow", pairs)
 
-    (far,) = terms(0, [jnp.bfloat16])
-    met = [shift(far, 2)]
-    near, back, kept = terms(1, [jnp.bfloat16, jnp.bfloat16, jnp.float32])
-    met += [beside(near, 1), beside(back, -1)]
+    far, near, back, kept = terms(0, [jnp.bfloat16, jnp.bfloat16, jnp.bfloat16, jnp.float32])
+    met = [shift(far, 2), beside(near, 1), beside(back, -1)]
     product, base = pl.pallas_call(
         store_kernel,
         out_shape=(jax.ShapeDtypeStruct((W, width), jnp.bfloat16), jax.ShapeDtypeStruct((SLICE, width), jnp.float32)),

time: 141 us -> 141 us (level)
    unnamed x14 -> x18, local copies, waits for them, and re-layouts: 2.13 us -> 2.91 us
where the time goes in v10:
time: 141 us; the launch traced here: 140 us
  waiting for transfers between devices  80.5 us (57%)
  starting transfers between devices  46.5 us (33%)
  Pallas kernels  8.88 us (6%)
  local copies, waits for them, and re-layouts  3.08 us (2%)
    all_to_all x1, waiting for transfers between devices, local(): lax.all_to_all(sending, 'pcol', split_axis=0, concat_axis=0, tiled=True)  50.3 us
    ppermute x4, waiting for transfers between devices, shift(): lax.ppermute(x, 'prow', [(i, (i + 2 * h) % rows) for i in range(rows)])  19 us
    all_to_all x1, starting transfers between devices, local(): lax.all_to_all(sending, 'pcol', split_axis=0, concat_axis=0, tiled=True)  15.6 us
    ppermute x4, starting transfers between devices, shift(): lax.ppermute(x, 'prow', [(i, (i + 2 * h) % rows) for i in range(rows)])  15.5 us
    ppermute x2, starting transfers between devices, swap(): return lax.ppermute(x, 'prow', [(i, i ^ 1) for i in range(rows)])  10.1 us
    ppermute x2, waiting for transfers between devices, beside(): return lax.ppermute(x, 'prow', pairs)  6.12 us
    ppermute x2, starting transfers between devices, beside(): return lax.ppermute(x, 'prow', pairs)  5.28 us
    ppermute x2, waiting for transfers between devices, swap(): return lax.ppermute(x, 'prow', [(i, i ^ 1) for i in range(rows)])  5.08 us
  transfers between devices with their start and end apart: 9, of which 8 were waited for; matrix products, arithmetic and copies ran while one was open for 0% of the time, Pallas kernels for 2%

profile of v10, /device:TPU:1, one launch (start us, length us, event | category | flops | bytes accessed | tf_op | source)
XLA Modules:
  0.0 140.0 jit_solution(1492168396005490492)
XLA Ops:
  0.6 2.5 %shard_map.68 = bf16[16,256,256]{2,1,0:T(8,128)(2,1)} custom-call(s32[8,16]{1,0:T(8,128)} %bitcast.19, bf16[1024,512]{1,0:T(8,128)(2,1)} %a_ref.1), custom_call_target="tpu_custom_call" | custom-call | bytes 3145728 | tf_op jit(solution)/shard_map/pallas_call | solution.py:164
  3.1 15.6 %all-to-all-start = ((bf16[16,256,256]{2,1,0:T(8,128)(2,1)}), bf16[16,256,256]{2,1,0:T(8,128)(2,1)S(1)}, u32[]{:S(2)}, u32[]{:S(2)}) async-start(bf16[16,256,256]{2,1,0:T(8,128)(2,1)} %shard_map.68), calls=%async_computation | async-start | bytes 4194304 | tf_op jit(solution)/shard_map/all_to_all | solution.py:179
  18.8 3.2 %collective-permute-start = (bf16[256,1024]{1,0:T(8,128)(2,1)S(1)}, bf16[256,1024]{1,0:T(8,128)(2,1)S(1)}, u32[]{:S(2)}, u32[]{:S(2)}) collective-permute-start(bf16[256,1024]{1,0:T(8,128)(2,1)S(1)} %bitcast.13), channel_id=1, source_target_pairs={{0,32},{16,48},{32,64},{48,80},{64,96},{80,112},{96,0},{112,16},{1... | collective-permute-start | bytes 1572872 | tf_op jit(solution)/shard_map/ppermute | solution.py:159
  22.0 4.5 %collective-permute-start.1 = (bf16[256,1024]{1,0:T(8,128)(2,1)S(1)}, bf16[256,1024]{1,0:T(8,128)(2,1)S(1)}, u32[]{:S(2)}, u32[]{:S(2)}) collective-permute-start(bf16[256,1024]{1,0:T(8,128)(2,1)S(1)} %bitcast.14), channel_id=1, source_target_pairs={{0,64},{16,80},{32,96},{48,112},{64,0},{80,16},{96,32},{112,48},{1... | collective-permute-start | bytes 1572872 | tf_op jit(solution)/shard_map/ppermute | solution.py:159
  26.5 3.0 %collective-permute-start.2 = (bf16[256,1024]{1,0:T(8,128)(2,1)S(1)}, bf16[256,1024]{1,0:T(8,128)(2,1)S(1)}, u32[]{:S(2)}, u32[]{:S(2)}) collective-permute-start(bf16[256,1024]{1,0:T(8,128)(2,1)S(1)} %bitcast.15), channel_id=1, source_target_pairs={{0,96},{16,112},{32,0},{48,16},{64,32},{80,48},{96,64},{112,80},{1... | collective-permute-start | bytes 1572872 | tf_op jit(solution)/shard_map/ppermute | solution.py:159
  29.5 5.0 %collective-permute-done = bf16[256,1024]{1,0:T(8,128)(2,1)S(1)} collective-permute-done((bf16[256,1024]{1,0:T(8,128)(2,1)S(1)}, bf16[256,1024]{1,0:T(8,128)(2,1)S(1)}, u32[]{:S(2)}, u32[]{:S(2)}) %collective-permute-start) | collective-permute-done | bytes 524320 | tf_op jit(solution)/shard_map/ppermute | solution.py:159
  34.5 12.3 %collective-permute-done.1 = bf16[256,1024]{1,0:T(8,128)(2,1)S(1)} collective-permute-done((bf16[256,1024]{1,0:T(8,128)(2,1)S(1)}, bf16[256,1024]{1,0:T(8,128)(2,1)S(1)}, u32[]{:S(2)}, u32[]{:S(2)}) %collective-permute-start.1) | collective-permute-done | bytes 524320 | tf_op jit(solution)/shard_map/ppermute | solution.py:159
  46.8 1.7 %collective-permute-done.2 = bf16[256,1024]{1,0:T(8,128)(2,1)S(1)} collective-permute-done((bf16[256,1024]{1,0:T(8,128)(2,1)S(1)}, bf16[256,1024]{1,0:T(8,128)(2,1)S(1)}, u32[]{:S(2)}, u32[]{:S(2)}) %collective-permute-start.2) | collective-permute-done | bytes 524320 | tf_op jit(solution)/shard_map/ppermute | solution.py:159
  48.5 0.3 pad_maximum_fusion
  48.8 3.5 %collective-permute-start.3 = (bf16[4,256,1024]{2,1,0:T(8,128)(2,1)S(1)}, bf16[4,256,1024]{2,1,0:T(8,128)(2,1)S(1)}, u32[]{:S(2)}, u32[]{:S(2)}) collective-permute-start(bf16[4,256,1024]{2,1,0:T(8,128)(2,1)S(1)} %pad_maximum_fusion), channel_id=1, source_target_pairs={{0,16},{16,0},{32,48},{48,32},{64,80},{80,64},{96,112},{112,96},{1... | collective-permute-start | bytes 6291464 | tf_op jit(solution)/shard_map/ppermute | solution.py:162
  52.4 0.0 copy-start.4
  52.4 0.0 copy-start.5
  52.4 3.6 %collective-permute-done.3 = bf16[4,256,1024]{2,1,0:T(8,128)(2,1)S(1)} collective-permute-done((bf16[4,256,1024]{2,1,0:T(8,128)(2,1)S(1)}, bf16[4,256,1024]{2,1,0:T(8,128)(2,1)S(1)}, u32[]{:S(2)}, u32[]{:S(2)}) %collective-permute-start.3) | collective-permute-done | bytes 2097184 | tf_op jit(solution)/shard_map/ppermute | solution.py:162
  56.0 0.2 constant_dynamic-update-slice_fusion.f_ref
  56.2 0.0 copy-start.6
  56.2 1.9 %copy-done.6 = bf16[8,256,1024]{2,1,0:T(8,128)(2,1)} copy-done((bf16[8,256,1024]{2,1,0:T(8,128)(2,1)}, bf16[8,256,1024]{2,1,0:T(8,128)(2,1)S(1)}, u32[]{:S(2)}) %copy-start.6) | copy-done | bytes 4194328
  58.1 1.4 %shard_map.69.turned_ref = bf16[512,512]{1,0:T(8,128)(2,1)S(1)} custom-call(bf16[8,256,1024]{2,1,0:T(8,128)(2,1)} %copy-done.6), custom_call_target="tpu_custom_call" | custom-call | bytes 2097152 | tf_op jit(solution)/shard_map/pallas_call | solution.py:183
  59.5 0.0 copy-start.2
  59.6 0.8 copy-done.2
  60.3 50.3 %all-to-all-done.a_ref = bf16[16,256,256]{2,1,0:T(8,128)(2,1)S(1)} async-done(((bf16[16,256,256]{2,1,0:T(8,128)(2,1)}), bf16[16,256,256]{2,1,0:T(8,128)(2,1)S(1)}, u32[]{:S(2)}, u32[]{:S(2)}) %all-to-all-start) | async-done | bytes 2097184 | tf_op jit(solution)/shard_map/all_to_all | solution.py:179
  110.6 2.6 %shard_map.70.own_ref = bf16[256,1024]{1,0:T(8,128)(2,1)S(1)} custom-call(s32[8,16]{1,0:T(8,128)S(1)} %bitcast.20, s32[16]{0:T(128)S(1)} %copy-done.5, bf16[16,256,256]{2,1,0:T(8,128)(2,1)S(1)} %all-to-all-done.a_ref, bf16[256,1024]{1,0:T(8,128)(2,1)S(1)} %bitcast.17, bf16[8,256,1024]{2,1,0:T(8,128)(2,1)} %copy-done.6), custom_call_target="tpu_custom_call" | custom-call | flops 1073741824 | bytes 7340032 | tf_op jit(solution)/shard_map/pallas_call | solution.py:194
  113.2 6.6 %collective-permute-start.4 = (bf16[256,1024]{1,0:T(8,128)(2,1)S(1)}, bf16[256,1024]{1,0:T(8,128)(2,1)S(1)}, u32[]{:S(2)}, u32[]{:S(2)}) collective-permute-start(bf16[256,1024]{1,0:T(8,128)(2,1)S(1)} %shard_map.70.own_ref), channel_id=1, source_target_pairs={{0,16},{16,0},{32,48},{48,32},{64,80},{80,64},{96,112},{112,96},{1... | collective-permute-start | bytes 1572872 | tf_op jit(solution)/shard_map/ppermute | solution.py:162
  119.9 1.5 %collective-permute-done.4.other_ref = bf16[256,1024]{1,0:T(8,128)(2,1)S(1)} collective-permute-done((bf16[256,1024]{1,0:T(8,128)(2,1)S(1)}, bf16[256,1024]{1,0:T(8,128)(2,1)S(1)}, u32[]{:S(2)}, u32[]{:S(2)}) %collective-permute-start.4) | collective-permute-done | bytes 524320 | tf_op jit(solution)/shard_map/ppermute | solution.py:162
  121.4 0.7 shard_map.71
  122.1 4.8 %collective-permute-start.5 = (bf16[128,1024]{1,0:T(8,128)(2,1)S(1)}, bf16[128,1024]{1,0:T(8,128)(2,1)S(1)}, u32[]{:S(2)}, u32[]{:S(2)}) collective-permute-start(bf16[128,1024]{1,0:T(8,128)(2,1)S(1)} %get-tuple-element.15), channel_id=1, source_target_pairs={{0,64},{16,80},{32,96},{48,112},{64,0},{80,16},{96,32},{112,48},{1... | collective-permute-start | bytes 786440 | tf_op jit(solution)/shard_map/ppermute | solution.py:159
  126.9 2.7 %collective-permute-start.6 = (bf16[128,1024]{1,0:T(8,128)(2,1)S(1)}, bf16[128,1024]{1,0:T(8,128)(2,1)S(1)}, u32[]{:S(2)}, u32[]{:S(2)}) collective-permute-start(bf16[128,1024]{1,0:T(8,128)(2,1)S(1)} %get-tuple-element.16), channel_id=1, source_target_pairs={{0,32},{16,112},{32,64},{48,16},{64,96},{80,48},{96,0},{112,80},{1... | collective-permute-start | bytes 786440 | tf_op jit(solution)/shard_map/ppermute | solution.py:227
  129.6 2.6 %collective-permute-start.7 = (bf16[128,1024]{1,0:T(8,128)(2,1)S(1)}, bf16[128,1024]{1,0:T(8,128)(2,1)S(1)}, u32[]{:S(2)}, u32[]{:S(2)}) collective-permute-start(bf16[128,1024]{1,0:T(8,128)(2,1)S(1)} %get-tuple-element.17), channel_id=1, source_target_pairs={{0,96},{16,48},{32,0},{48,80},{64,32},{80,112},{96,64},{112,16},{1... | collective-permute-start | bytes 786440 | tf_op jit(solution)/shard_map/ppermute | solution.py:227
  132.3 0.8 shard_map.72
  133.1 0.0 collective-permute-done.5.refs_0_
  133.1 5.7 %collective-permute-done.6.refs_1_ = bf16[128,1024]{1,0:T(8,128)(2,1)S(1)} collective-permute-done((bf16[128,1024]{1,0:T(8,128)(2,1)S(1)}, bf16[128,1024]{1,0:T(8,128)(2,1)S(1)}, u32[]{:S(2)}, u32[]{:S(2)}) %collective-permute-start.6) | collective-permute-done | bytes 262176 | tf_op jit(solution)/shard_map/ppermute | solution.py:227
  138.7 0.5 collective-permute-done.7.refs_2_
  139.2 0.8 shard_map.73
  (12 shorter events, 0.2 us)
Async XLA Ops:
  0.6 18.1 %copy-start = (bf16[1,1,256,1024]{3,2,1,0:T(8,128)(2,1)S(1)}, bf16[1,1,256,1024]{3,2,1,0:T(8,128)(2,1)}, u32[]{:S(2)}) copy-start(bf16[1,1,256,1024]{3,2,1,0:T(8,128)(2,1)} %param.6) | copy-start | bytes 1572868
  3.1 107.5 %all-to-all-start = ((bf16[16,256,256]{2,1,0:T(8,128)(2,1)}), bf16[16,256,256]{2,1,0:T(8,128)(2,1)S(1)}, u32[]{:S(2)}, u32[]{:S(2)}) async-start(bf16[16,256,256]{2,1,0:T(8,128)(2,1)} %shard_map.68), calls=%async_computation | async-start | bytes 4194304 | tf_op jit(solution)/shard_map/all_to_all | solution.py:179
  18.8 15.7 %collective-permute-start = (bf16[256,1024]{1,0:T(8,128)(2,1)S(1)}, bf16[256,1024]{1,0:T(8,128)(2,1)S(1)}, u32[]{:S(2)}, u32[]{:S(2)}) collective-permute-start(bf16[256,1024]{1,0:T(8,128)(2,1)S(1)} %bitcast.13), channel_id=1, source_target_pairs={{0,32},{16,48},{32,64},{48,80},{64,96},{80,112},{96,0},{112,16},{1... | collective-permute-start | bytes 1572872 | tf_op jit(solution)/shard_map/ppermute | solution.py:159
  22.0 24.8 %collective-permute-start.1 = (bf16[256,1024]{1,0:T(8,128)(2,1)S(1)}, bf16[256,1024]{1,0:T(8,128)(2,1)S(1)}, u32[]{:S(2)}, u32[]{:S(2)}) collective-permute-start(bf16[256,1024]{1,0:T(8,128)(2,1)S(1)} %bitcast.14), channel_id=1, source_target_pairs={{0,64},{16,80},{32,96},{48,112},{64,0},{80,16},{96,32},{112,48},{1... | collective-permute-start | bytes 1572872 | tf_op jit(solution)/shard_map/ppermute | solution.py:159
  26.5 22.0 %collective-permute-start.2 = (bf16[256,1024]{1,0:T(8,128)(2,1)S(1)}, bf16[256,1024]{1,0:T(8,128)(2,1)S(1)}, u32[]{:S(2)}, u32[]{:S(2)}) collective-permute-start(bf16[256,1024]{1,0:T(8,128)(2,1)S(1)} %bitcast.15), channel_id=1, source_target_pairs={{0,96},{16,112},{32,0},{48,16},{64,32},{80,48},{96,64},{112,80},{1... | collective-permute-start | bytes 1572872 | tf_op jit(solution)/shard_map/ppermute | solution.py:159
  48.8 7.2 %collective-permute-start.3 = (bf16[4,256,1024]{2,1,0:T(8,128)(2,1)S(1)}, bf16[4,256,1024]{2,1,0:T(8,128)(2,1)S(1)}, u32[]{:S(2)}, u32[]{:S(2)}) collective-permute-start(bf16[4,256,1024]{2,1,0:T(8,128)(2,1)S(1)} %pad_maximum_fusion), channel_id=1, source_target_pairs={{0,16},{16,0},{32,48},{48,32},{64,80},{80,64},{96,112},{112,96},{1... | collective-permute-start | bytes 6291464 | tf_op jit(solution)/shard_map/ppermute | solution.py:162
  52.4 58.2 %copy-start.4 = (s32[16,8]{0,1:T(8,128)S(1)}, s32[16,8]{0,1:T(8,128)}, u32[]{:S(2)}) copy-start(s32[16,8]{0,1:T(8,128)} %param.8) | copy-start | bytes 1540
  52.4 58.2 %copy-start.5 = (s32[16]{0:T(128)S(1)}, s32[16]{0:T(128)}, u32[]{:S(2)}) copy-start(s32[16]{0:T(128)} %count_ref.1) | copy-start | bytes 196
  56.2 2.0 %copy-start.6 = (bf16[8,256,1024]{2,1,0:T(8,128)(2,1)}, bf16[8,256,1024]{2,1,0:T(8,128)(2,1)S(1)}, u32[]{:S(2)}) copy-start(bf16[8,256,1024]{2,1,0:T(8,128)(2,1)S(1)} %constant_dynamic-update-slice_fusion.f_ref) | copy-start | bytes 12582916
  59.5 0.8 copy-start.2
  60.3 71.9 %copy-start.1 = (f32[1,128,1024]{2,1,0:T(8,128)S(1)}, f32[1,128,1024]{2,1,0:T(8,128)}, u32[]{:S(2)}) copy-start(f32[1,128,1024]{2,1,0:T(8,128)} %param.7) | copy-start | bytes 1572868
  110.6 10.8 %copy-start.3 = (bf16[512,512]{1,0:T(8,128)(2,1)S(1)}, bf16[512,512]{1,0:T(8,128)(2,1)}, u32[]{:S(2)}) copy-start(bf16[512,512]{1,0:T(8,128)(2,1)} %copy-done.2) | copy-start | bytes 1572868
  113.2 8.2 %collective-permute-start.4 = (bf16[256,1024]{1,0:T(8,128)(2,1)S(1)}, bf16[256,1024]{1,0:T(8,128)(2,1)S(1)}, u32[]{:S(2)}, u32[]{:S(2)}) collective-permute-start(bf16[256,1024]{1,0:T(8,128)(2,1)S(1)} %shard_map.70.own_ref), channel_id=1, source_target_pairs={{0,16},{16,0},{32,48},{48,32},{64,80},{80,64},{96,112},{112,96},{1... | collective-permute-start | bytes 1572872 | tf_op jit(solution)/shard_map/ppermute | solution.py:162
  122.1 11.0 %collective-permute-start.5 = (bf16[128,1024]{1,0:T(8,128)(2,1)S(1)}, bf16[128,1024]{1,0:T(8,128)(2,1)S(1)}, u32[]{:S(2)}, u32[]{:S(2)}) collective-permute-start(bf16[128,1024]{1,0:T(8,128)(2,1)S(1)} %get-tuple-element.15), channel_id=1, source_target_pairs={{0,64},{16,80},{32,96},{48,112},{64,0},{80,16},{96,32},{112,48},{1... | collective-permute-start | bytes 786440 | tf_op jit(solution)/shard_map/ppermute | solution.py:159
  126.9 11.8 %collective-permute-start.6 = (bf16[128,1024]{1,0:T(8,128)(2,1)S(1)}, bf16[128,1024]{1,0:T(8,128)(2,1)S(1)}, u32[]{:S(2)}, u32[]{:S(2)}) collective-permute-start(bf16[128,1024]{1,0:T(8,128)(2,1)S(1)} %get-tuple-element.16), channel_id=1, source_target_pairs={{0,32},{16,112},{32,64},{48,16},{64,96},{80,48},{96,0},{112,80},{1... | collective-permute-start | bytes 786440 | tf_op jit(solution)/shard_map/ppermute | solution.py:227
  129.6 9.6 %collective-permute-start.7 = (bf16[128,1024]{1,0:T(8,128)(2,1)S(1)}, bf16[128,1024]{1,0:T(8,128)(2,1)S(1)}, u32[]{:S(2)}, u32[]{:S(2)}) collective-permute-start(bf16[128,1024]{1,0:T(8,128)(2,1)S(1)} %get-tuple-element.17), channel_id=1, source_target_pairs={{0,96},{16,48},{32,0},{48,80},{64,32},{80,112},{96,64},{112,16},{1... | collective-permute-start | bytes 786440 | tf_op jit(solution)/shard_map/ppermute | solution.py:227
